TPU v7x, 256 devices: a whole 4x4x8 slice. The times are simulated.
256 devices in a mesh: dp: 64 (over z, x, core), mp: 4 (over y).
Axes of the slice: x: 4, y: 4, z: 8, core: 2. Of those that a mesh axis runs over, the one named last changes fastest.
Arguments:
- feature_ids: int32 [65536, 8], P('dp'), may hold values from 0 to 4095
- context_ids: int32 [65536], P('dp'), may hold values from 0 to 511
- shown_positions: int32 [65536], P('dp'), may hold values from 0 to 63
- clicked_positions: int32 [65536], P('dp'), may hold values from 0 to 63
- clicks: int32 [65536], P('dp'), may hold values 0 or 1
- embed_table: bfloat16 [4096, 1024], P(None, 'mp'), may hold values from -2 to 2
- cross_weight: bfloat16 [1024, 1024], P('dp', 'mp'), may hold values from -0.1875 to 0.1875
- deep_weight: bfloat16 [1024, 1024], P('dp', 'mp'), may hold values from -0.1875 to 0.1875
- cross_bias: float32 [1024], P('mp'), may hold values from -3 to 3
- deep_bias: float32 [1024], P('mp'), may hold values from -3 to 3
- out_weight: float32 [1024], P('mp'), may hold values from -0.1875 to 0.1875
- shown_embed: float32 [64, 64], replicated, may hold values from -4 to 4
- click_embed: float32 [64, 64], replicated, may hold values from -4 to 4
- theta_relevant: float32 [512, 64], P('mp'), may hold values from -2 to 2
- theta_irrelevant: float32 [512, 64], P('mp'), may hold values from -2 to 2
Outputs:
- bias_hessians: float32 [2, 512, 64, 64], P(None, 'mp', 'dp')
- bias_gradients: float32 [2, 512, 64], P(None, 'mp', 'dp')
- cross_update: float32 [1024, 1024], P('dp', 'mp')
- deep_update: float32 [1024, 1024], P('dp', 'mp')
- cross_bias_update: float32 [1024], P('mp')
- deep_bias_update: float32 [1024], P('mp')
- out_weight_update: float32 [1024], P('mp')
All inputs are finite; a program needn't handle non-finite values. No bound on the sum of `clicks` on one device may be relied on, other than what follows from the above.
Results may differ from a plain program's by a relative error of at most 0.0085.
Values may be sent and summed in bfloat16 or wider, within the bound.
No kernel may reach another device: no remote copies, remote signals or barrier semaphores. Data moves between devices by JAX's collectives and lax.ppermute only.
A program may use at most 64 MiB of HBM per device.

v0:
```python
import jax
import jax.numpy as jnp
from jax import lax
from jax.sharding import PartitionSpec as P


def silu_parts(pre_act):
    gating = jax.nn.sigmoid(pre_act)
    return (pre_act * gating, gating * (1.0 + pre_act * (1.0 - gating)))


def posterior_of(relevance, mu_rel, mu_irr, click_float):
    on_click = mu_rel * relevance / (mu_rel * relevance + mu_irr * (1.0 - relevance))
    no_click = (
        (1.0 - mu_rel)
        * relevance
        / ((1.0 - mu_rel) * relevance + (1.0 - mu_irr) * (1.0 - relevance))
    )
    return jnp.where(click_float > 0.5, on_click, no_click)


def table_lookup(indices, table):
    onehot_rows = (indices[:, None] == jnp.arange(table.shape[0])[None, :]).astype(jnp.float32)
    return jnp.dot(onehot_rows, table, precision=lax.Precision.HIGHEST)


def accumulate(selector, weights, features):
    row_count = selector.shape[0]
    ctx_count = selector.shape[1]
    width_bias = features.shape[1]
    block_rows = 512
    block_count = row_count // block_rows

    def add_block(running, row_block):
        sel_block, weight_block, feat_block = row_block
        outer_prod = (feat_block[:, :, None] * feat_block[:, None, :]).reshape(block_rows, -1)
        hess_weights = jnp.concatenate(
            [sel_block * weight_block[:, 0:1], sel_block * weight_block[:, 1:2]], axis=1
        )
        grad_weights = jnp.concatenate(
            [sel_block * weight_block[:, 2:3], sel_block * weight_block[:, 3:4]], axis=1
        )
        contract = (((0,), (0,)), ((), ()))
        hess_new = lax.dot_general(
            hess_weights, outer_prod, contract, precision=lax.Precision.HIGHEST
        )
        grad_new = lax.dot_general(
            grad_weights, feat_block, contract, precision=lax.Precision.HIGHEST
        )
        return ((running[0] + hess_new, running[1] + grad_new), None)

    start_stats = (
        jnp.zeros((2 * ctx_count, width_bias * width_bias), jnp.float32),
        jnp.zeros((2 * ctx_count, width_bias), jnp.float32),
    )
    blocks = (
        selector.reshape(block_count, block_rows, ctx_count),
        weights.reshape(block_count, block_rows, 4),
        features.reshape(block_count, block_rows, width_bias),
    )
    (hess_all, grad_all), unused = lax.scan(add_block, start_stats, blocks)
    return (
        hess_all.reshape(2, ctx_count, width_bias, width_bias),
        grad_all.reshape(2, ctx_count, width_bias),
    )


def shards(
    feature_ids,
    context_ids,
    shown_positions,
    clicked_positions,
    clicks,
    embed_table,
    cross_weight,
    deep_weight,
    cross_bias,
    deep_bias,
    out_weight,
    shown_embed,
    click_embed,
    theta_relevant,
    theta_irrelevant,
):
    row_count = context_ids.shape[0]
    local_width = embed_table.shape[1]
    summed = jnp.zeros((row_count, local_width), jnp.float32)
    for slot_index in range(feature_ids.shape[1]):
        summed = summed + jnp.take(embed_table, feature_ids[:, slot_index], axis=0).astype(
            jnp.float32
        )
    base_rows = summed.astype(jnp.bfloat16)
    base_float = base_rows.astype(jnp.float32)
    base_full = lax.all_gather(base_rows, "mp", axis=1, tiled=True)
    full_width = base_full.shape[1]
    columns = base_full
    cross_pre = jnp.dot(
        columns,
        lax.all_gather(cross_weight, "dp", axis=0, tiled=True),
        preferred_element_type=jnp.float32,
    )
    crossed = (base_float * (cross_pre + cross_bias) + base_float).astype(jnp.bfloat16)
    crossed_full = lax.all_gather(crossed, "mp", axis=1, tiled=True)
    columns = crossed_full
    deep_pre = jnp.dot(
        columns,
        lax.all_gather(deep_weight, "dp", axis=0, tiled=True),
        preferred_element_type=jnp.float32,
    )
    deep_pre = deep_pre + deep_bias
    activated, slope = silu_parts(deep_pre)
    hidden = activated.astype(jnp.bfloat16)
    partial_score = jnp.sum(hidden * out_weight, axis=1)
    score_sum = lax.psum(partial_score, "mp")
    relevance = jax.nn.sigmoid(score_sum)
    ctx_count = theta_relevant.shape[0]
    ctx_first = lax.axis_index("mp") * ctx_count
    local_ctx = context_ids - ctx_first
    selector = (local_ctx[:, None] == jnp.arange(ctx_count)[None, :]).astype(jnp.float32)
    owned = (local_ctx >= 0) & (local_ctx < ctx_count)
    features = jnp.tanh(
        table_lookup(shown_positions, shown_embed) + table_lookup(clicked_positions, click_embed)
    )
    rel_rows = jnp.dot(selector, theta_relevant, precision=lax.Precision.HIGHEST)
    irr_rows = jnp.dot(selector, theta_irrelevant, precision=lax.Precision.HIGHEST)
    mu_rel = jax.nn.sigmoid(jnp.sum(rel_rows * features, axis=1))
    mu_irr = jax.nn.sigmoid(jnp.sum(irr_rows * features, axis=1))
    click_float = clicks.astype(jnp.float32)
    posterior = posterior_of(relevance, mu_rel, mu_irr, click_float)
    weights = jnp.stack(
        [
            posterior * mu_rel * (1.0 - mu_rel),
            (1.0 - posterior) * mu_irr * (1.0 - mu_irr),
            posterior * (click_float - mu_rel),
            (1.0 - posterior) * (click_float - mu_irr),
        ],
        axis=1,
    )
    posterior_full = lax.psum(jnp.where(owned, posterior, 0.0), "mp")
    hess_part, grad_part = accumulate(selector, weights, features)
    hess_out, stat_grad_out = (
        lax.psum_scatter(hess_part, "dp", scatter_dimension=2, tiled=True),
        lax.psum_scatter(grad_part, "dp", scatter_dimension=2, tiled=True),
    )
    score_grad = relevance - posterior_full
    pre_grad = score_grad[:, None] * out_weight[None, :] * slope
    pre_grad_b = pre_grad.astype(jnp.bfloat16)
    deep_part = jnp.einsum(
        "rd,re->de", crossed_full, pre_grad_b, preferred_element_type=jnp.float32
    )
    deep_bias_grad = jnp.sum(pre_grad, axis=0)
    out_grad = jnp.sum(score_grad[:, None] * hidden, axis=0)
    crossed_part = jnp.einsum(
        "re,ne->rn",
        pre_grad_b,
        lax.all_gather(deep_weight, "dp", axis=0, tiled=True),
        preferred_element_type=jnp.float32,
    )
    crossed_grad = lax.psum_scatter(crossed_part, "mp", scatter_dimension=1, tiled=True)
    cross_pre_grad = crossed_grad * base_float
    cross_pre_b = cross_pre_grad.astype(jnp.bfloat16)
    cross_part = jnp.einsum("rd,re->de", base_full, cross_pre_b, preferred_element_type=jnp.float32)
    cross_bias_grad = jnp.sum(cross_pre_grad, axis=0)
    cross_shard, deep_shard = (
        lax.psum_scatter(cross_part, "dp", scatter_dimension=0, tiled=True),
        lax.psum_scatter(deep_part, "dp", scatter_dimension=0, tiled=True),
    )
    cross_bias_sum, deep_bias_sum, out_sum = lax.psum(
        (cross_bias_grad, deep_bias_grad, out_grad), "dp"
    )
    vector_squares = (
        jnp.sum(cross_bias_sum * cross_bias_sum)
        + jnp.sum(deep_bias_sum * deep_bias_sum)
        + jnp.sum(out_sum * out_sum)
    )
    local_squares = (
        jnp.sum(cross_shard * cross_shard)
        + jnp.sum(deep_shard * deep_shard)
        + jnp.where(lax.axis_index("dp") == 0, vector_squares, 0.0)
    )
    squares_total = lax.psum(local_squares, ("dp", "mp"))
    param_count = 2 * full_width * full_width + 3 * full_width
    norm_scale = 1.0 / jnp.sqrt(squares_total / param_count + 1e-06)
    return (
        hess_out,
        stat_grad_out,
        cross_shard * norm_scale,
        deep_shard * norm_scale,
        cross_bias_sum * norm_scale,
        deep_bias_sum * norm_scale,
        out_sum * norm_scale,
    )


def solution(mesh):
    return jax.shard_map(
        shards,
        mesh=mesh,
        in_specs=(
            P("dp", None),
            P("dp"),
            P("dp"),
            P("dp"),
            P("dp"),
            P(None, "mp"),
            P("dp", "mp"),
            P("dp", "mp"),
            P("mp"),
            P("mp"),
            P("mp"),
            P(),
            P(),
            P("mp", None),
            P("mp", None),
        ),
        out_specs=(
            P(None, "mp", "dp", None),
            P(None, "mp", "dp"),
            P("dp", "mp"),
            P("dp", "mp"),
            P("mp"),
            P("mp"),
            P("mp"),
        ),
        check_vma=False,
    )
```

profile of v0, /device:TPU:1, one launch (start us, length us, event | category | flops | bytes accessed | tf_op | source)
XLA Modules:
  0.0 835.8 jit_solution(7851789412682946161)
XLA Ops:
  7.2 1.1 fusion.41
  8.9 3.9 gather_fusion.7
  12.8 3.9 gather_fusion.6
  16.8 4.9 gather_fusion.3
  21.7 4.9 gather_fusion.2
  26.7 4.9 gather_fusion.1
  31.6 4.9 gather_fusion
  36.5 4.9 gather_fusion.5
  41.5 4.9 gather_fusion.4
  46.4 4.5 add_convert_fusion
  51.0 54.7 %all_gather.14 = bf16[1024,256]{1,0:T(8,128)(2,1)S(1)} all-gather(bf16[16,256]{1,0:T(8,128)(2,1)S(1)} %copy-done.11), channel_id=1, replica_groups=mesh['dp'=64,'mp'=4] {'dp'}, dimensions={0}, use_global_device_ids=true | all-gather | bytes 532480 | tf_op jit(solution)/shard_map/all_gather | solution.py:99
  105.7 3.2 fusion.8
  111.4 49.2 %all_gather.16 = bf16[1024,256]{1,0:T(8,128)(2,1)S(1)} all-gather(bf16[16,256]{1,0:T(8,128)(2,1)S(1)} %copy-done.12), channel_id=1, replica_groups=mesh['dp'=64,'mp'=4] {'dp'}, dimensions={0}, use_global_device_ids=true | all-gather | bytes 532480 | tf_op jit(solution)/shard_map/all_gather | solution.py:107
  160.6 3.5 fusion.12
  164.1 8.7 %psum.42 = f32[1024]{0:T(1024)S(1)} all-reduce(f32[1024]{0:T(1024)S(1)} %get-tuple-element.115), channel_id=1, replica_groups=mesh['dp'=64,'mp'=4] {'mp'}, use_global_device_ids=true, to_apply=%region_2.4 | all-reduce | flops 1024 | bytes 8192 | tf_op jit(solution)/shard_map/psum | solution.py:114
  172.8 6.0 psum.43
  178.8 4.0 fusion.22
  182.9 3.8 fusion.20
  187.3 44.7 %reduce-scatter.7.cloned.1.call-done = f32[1024,256]{1,0:T(8,128)} async-done(((f32[1024,1024]{1,0:T(8,128)}), f32[1024,256]{1,0:T(8,128)}) %reduce-scatter.7.cloned.1.call-update) | async-done | bytes 1048592 | tf_op jit(solution)/shard_map/reduce_scatter | solution.py:159
  232.1 3.6 fusion.16
  235.8 42.1 %while.13 = (s32[]{:T(128)}, f32[256,4096]{1,0:T(8,128)}, f32[256,64]{0,1:T(8,128)S(1)}, f32[2,512,128]{2,1,0:T(8,128)S(1)}, f32[2,512,4]{1,2,0:T(4,128)S(1)}, /...) while((s32[]{:T(128)}, f32[256,4096]{1,0:T(8,128)}, f32[256,64]{0,1:T(8,128)S(1)}, ...), condition=%wide.region_5.7_spmd.clone, body=%wide.region_4.6_spmd.clone.sunk | while | flops 6547865600 | bytes 62038184 | solution.py:61
  236.8 1.1 broadcast_multiply_fusion.7
  237.9 1.1 copy-done.1
  238.9 15.9 %convolution_add_fusion.7 = f32[256,4096]{1,0:T(8,128)S(1)} fusion(f32[512,4096]{0,1:T(8,128)S(1)} %bitcast.67, f32[256,4096]{1,0:T(8,128)S(1)} %copy-done.1, pred[]{:T(512)S(6)} %compare.3, f32[512,128]{1,0:T(8,128)S(1)} %get-tuple-element.195, f32[512,128]{1,0:T(8,128)S(1)} %get-tuple-element.196), kind=kOutput, calls=%fused_computation.8.clone.1 | convolution fusion | flops 6444679168 | bytes 17301504 | tf_op jit(solution)/shard_map/while/body/eval_jaxpr/dot_general | solution.py:44
  254.8 2.0 copy-done.2
  257.7 1.1 broadcast_multiply_fusion.7
  258.8 1.1 copy-done.1
  260.0 15.9 %convolution_add_fusion.7 = f32[256,4096]{1,0:T(8,128)S(1)} fusion(f32[512,4096]{0,1:T(8,128)S(1)} %bitcast.67, f32[256,4096]{1,0:T(8,128)S(1)} %copy-done.1, pred[]{:T(512)S(6)} %compare.3, f32[512,128]{1,0:T(8,128)S(1)} %get-tuple-element.195, f32[512,128]{1,0:T(8,128)S(1)} %get-tuple-element.196), kind=kOutput, calls=%fused_computation.8.clone.1 | convolution fusion | flops 6444679168 | bytes 17301504 | tf_op jit(solution)/shard_map/while/body/eval_jaxpr/dot_general | solution.py:44
  275.8 2.0 copy-done.2
  277.8 0.6 reshape.63
  278.5 7.9 reshape.152
  286.4 7.8 copy.29
  294.3 0.6 copy-done.18
  295.5 1.8 fusion.13
  297.2 73.1 %reduce-scatter.11.cloned.1.call-done = f32[16,256]{1,0:T(8,128)} async-done(((f32[1024,256]{1,0:T(8,128)}), f32[16,256]{1,0:T(8,128)}) %reduce-scatter.11.cloned.1.call-update) | async-done | bytes 16400 | tf_op jit(solution)/shard_map/reduce_scatter | solution.py:166
  370.4 1.3 multiply_reduce_fusion
  371.7 1.4 fusion.14
  373.1 129.2 %all-reduce.2 = (f32[256]{0:T(256)S(1)}, f32[256]{0:T(256)S(1)}, f32[256]{0:T(256)S(1)}) all-reduce(f32[256]{0:T(256)S(1)} %fusion.14, f32[256]{0:T(256)S(1)} %get-tuple-element.97, f32[256]{0:T(256)S(1)} %get-tuple-element.96), channel_id=1, replica_groups=mesh['dp'=64,'mp'=4] {'dp'}, use_global_device_ids=true, to_apply=%region_15.17 | all-reduce | flops 768 | bytes 6144 | tf_op jit(solution)/shard_map/psum | solution.py:168
  502.3 0.6 multiply_reduce_fusion.3
  504.8 0.6 multiply_reduce_fusion.2
  506.0 6.6 reduce-scatter.9.cloned.1.call-done
  512.6 1.3 multiply_reduce_fusion.1
  515.2 172.8 %all-reduce.5.cloned.1.call-done = f32[2,128,64]{1,0,2:T(2,128)} async-done(((f32[2,128,64]{1,0,2:T(2,128)}), f32[2,128,64]{1,0,2:T(2,128)}) %all-reduce.5.cloned.1.call-update) | async-done | bytes 65552
  688.0 1.9 constant_dynamic-slice_fusion.1
  689.9 75.0 %psum.47 = f32[]{:T(128)} all-reduce(f32[]{:T(128)S(6)} %add.139), channel_id=1, replica_groups=mesh['dp'=64,'mp'=4] {'dp','mp'}, use_global_device_ids=true, to_apply=%region_23.25 | all-reduce | flops 1 | bytes 8 | tf_op jit(solution)/shard_map/psum | solution.py:181
  767.2 1.3 broadcast_multiply_fusion.1
  768.6 1.3 broadcast_multiply_fusion.2
  769.9 59.1 %reduce-scatter.13.cloned.1.call-done = f32[2,128,1,64]{1,3,0,2:T(8,128)} async-done(((f32[2,128,64,64]{1,3,0,2:T(8,128)}), f32[2,128,1,64]{1,3,0,2:T(8,128)}) %reduce-scatter.13.cloned.1.call-update) | async-done | bytes 65552
  (96 shorter events, 8.5 us)
Async XLA Ops:
  7.2 1.7 copy-start
  7.2 98.5 %all-gather.3.cloned.1.call-start = ((), (), s32[]{:S(2)}) async-start(), calls=%async_computation.4 | async-start | bytes 2621440 | tf_op jit(solution)/shard_map/all_gather | solution.py:94
  46.4 4.6 copy-start.11
  46.4 59.3 %copy-start.16 = (f32[256]{0:T(256)S(1)}, f32[256]{0:T(256)}, u32[]{:S(2)}) copy-start(f32[256]{0:T(256)} %param.27) | copy-start | bytes 3076
  50.9 109.7 %all-gather.5.cloned.1.call-start = ((), (), s32[]{:S(2)}) async-start(), calls=%async_computation.5 | async-start | bytes 2621440 | tf_op jit(solution)/shard_map/all_gather | solution.py:103
  105.6 3.4 copy-start.9
  105.6 3.4 copy-start.5
  105.6 3.4 copy-start.13
  105.6 4.0 copy-start.6
  105.7 4.0 copy-start.14
  105.7 4.6 copy-start.7
  105.7 5.1 copy-start.8
  105.7 5.7 copy-start.12
  108.9 51.6 %copy-start.15 = (f32[256]{0:T(256)S(1)}, f32[256]{0:T(256)}, u32[]{:S(2)}) copy-start(f32[256]{0:T(256)} %param.29) | copy-start | bytes 3076
  108.9 51.6 %copy-start.17 = (f32[256]{0:T(256)S(1)}, f32[256]{0:T(256)}, u32[]{:S(2)}) copy-start(f32[256]{0:T(256)} %param.28) | copy-start | bytes 3076
  109.0 123.1 %reduce-scatter.7.cloned.1.call-start = ((), (), s32[]{:S(2)}) async-start(), calls=%async_computation.6 | async-start | bytes 5242880 | tf_op jit(solution)/shard_map/reduce_scatter | solution.py:159
  160.5 12.3 %copy-start.10 = (s32[1024]{0:T(1024)S(1)}, s32[1024]{0:T(1024)}, u32[]{:S(2)}) copy-start(s32[1024]{0:T(1024)} %param.23) | copy-start | bytes 12292
  182.9 187.5 %reduce-scatter.11.cloned.1.call-start = ((), (), s32[]{:S(2)}) async-start(), calls=%async_computation.8 | async-start | bytes 1064960 | tf_op jit(solution)/shard_map/reduce_scatter | solution.py:166
  186.8 45.3 %copy-start.3 = (bf16[1024,256]{1,0:T(8,128)(2,1)S(1)}, bf16[1024,256]{1,0:T(8,128)(2,1)}, u32[]{:S(2)}) copy-start(bf16[1024,256]{1,0:T(8,128)(2,1)} %add_convert_fusion) | copy-start | bytes 1572868
  186.8 325.8 %reduce-scatter.9.cloned.1.call-start = ((), (), s32[]{:S(2)}) async-start(), calls=%async_computation.7 | async-start | bytes 1064960 | tf_op jit(solution)/shard_map/reduce_scatter | solution.py:165
  235.7 452.3 %all-reduce.5.cloned.1.call-start = ((), (), s32[]{:S(2)}) async-start(), calls=%async_computation.9 | async-start | bytes 131072
  236.7 2.2 copy-start.1
  254.8 2.0 copy-start.2
  257.7 2.2 copy-start.1
  275.8 2.0 copy-start.2
  278.5 550.5 %reduce-scatter.13.cloned.1.call-start = ((), (), s32[]{:S(2)}) async-start(), calls=%async_computation.10 | async-start | bytes 4259840
  294.2 0.7 copy-start.18
  294.2 1.3 copy-start.4
Sparse Core Ops, SparseCore 0:
  51.0 39.9 all-gather.2
  109.1 33.4 all-gather.4
  183.0 49.0 reduce-scatter.6
  236.4 133.8 reduce-scatter.10
  374.7 137.8 reduce-scatter.8
  516.3 171.6 all-reduce.4
  693.3 135.6 reduce-scatter.12
where the time goes:
time: 841 us; the launch traced here: 836 us
  waiting for transfers between devices  356 us (42%)
  blocking collectives  323 us (38%)
  local copies, waits for them, and re-layouts  65.1 us (8%)
  matrix products  53 us (6%)
  other arithmetic  19.6 us (2%)
  between operations  18.5 us (2%)
    unnamed x9, waiting for transfers between devices  232 us
    psum x1, blocking collectives, shards(): lax.psum((cross_bias_grad, deep_bias_grad, out_grad), 'dp')  129 us
    psum x1, blocking collectives, shards(): squares_total = lax.psum(local_squares, ('dp', 'mp'))  75 us
    reduce_scatter x1, waiting for transfers between devices, shards(): lax.psum_scatter(deep_part, 'dp', scatter_dimension=0, tiled=True)  73.1 us
    all_gather x1, blocking collectives, shards(): lax.all_gather(cross_weight, 'dp', axis=0, tiled=True)  54.7 us
    all_gather x1, blocking collectives, shards(): lax.all_gather(deep_weight, 'dp', axis=0, tiled=True)  49.2 us
    reduce_scatter x1, waiting for transfers between devices, shards(): lax.psum_scatter(crossed_part, 'mp', scatter_dimension=1, tiled=True)  44.7 us
    gather x8, local copies, waits for them, and re-layouts, shards(): jnp.take(embed_table, feature_ids[:, slot_index], axis=0)  37.5 us
  transfers between devices with their start and end apart: 7, of which 5 were waited for; matrix products, arithmetic and copies ran while one was open for 9% of the time, Pallas kernels for 0%

commit v1 on v0

v1 whole, which is shorter than its diff:
```python
import jax
import jax.numpy as jnp
import numpy as np
from jax import lax
from jax.experimental import pallas as pl
from jax.experimental.pallas import tpu as pltpu
from jax.sharding import Mesh, PartitionSpec as P

DP = ("z", "x", "c")
BF16 = jnp.bfloat16
F32 = jnp.float32


def posterior_of(relevance, mu_rel, mu_irr, click_float):
    on_click = mu_rel * relevance / (mu_rel * relevance + mu_irr * (1.0 - relevance))
    no_click = (
        (1.0 - mu_rel)
        * relevance
        / ((1.0 - mu_rel) * relevance + (1.0 - mu_irr) * (1.0 - relevance))
    )
    return jnp.where(click_float > 0.5, on_click, no_click)


def table_lookup(indices, table):
    onehot_rows = (indices[:, None] == jnp.arange(table.shape[0])[None, :]).astype(F32)
    return jnp.dot(onehot_rows, table, precision=lax.Precision.HIGHEST)


def embed_kernel(ids_ref, table_ref, out_ref, wide_ref):
    rows, slots = ids_ref.shape
    vocab, width = table_ref.shape
    lanes = 256
    tile = 256
    ids = ids_ref[...]
    for s in range(slots):
        wide_ref[s] = jnp.broadcast_to(ids[:, s : s + 1], (rows, lanes)).astype(jnp.int16)
    lane = lax.broadcasted_iota(jnp.int32, (tile, lanes), 1)

    def body(r, carry):
        first = pl.multiple_of(r * tile, tile)
        total = jnp.zeros((tile, width), F32)
        for k in range(vocab // lanes):
            names = (lane + k * lanes).astype(jnp.int16)
            counts = jnp.zeros((tile, lanes), BF16)
            for s in range(slots):
                hit = wide_ref[s, pl.ds(first, tile), :] == names
                counts = counts + jnp.where(hit, jnp.ones((), BF16), jnp.zeros((), BF16))
            total = total + jnp.dot(
                counts, table_ref[k * lanes : (k + 1) * lanes, :], preferred_element_type=F32
            )
        out_ref[pl.ds(first, tile), :] = total.astype(BF16)
        return carry

    lax.fori_loop(0, rows // tile, body, 0)


def embed(ids, table):
    rows = ids.shape[0]
    return pl.pallas_call(
        embed_kernel,
        out_shape=jax.ShapeDtypeStruct((rows, table.shape[1]), BF16),
        in_specs=[pl.BlockSpec(memory_space=pltpu.VMEM)] * 2,
        out_specs=pl.BlockSpec(memory_space=pltpu.VMEM),
        scratch_shapes=[pltpu.VMEM((ids.shape[1], rows, 256), jnp.int16)],
        compiler_params=pltpu.CompilerParams(vmem_limit_bytes=40 * 2**20),
    )(ids, table)


def swap(value):
    return lax.ppermute(value, "c", [(0, 1), (1, 0)])


def gather(value, axes, count):
    wide = jnp.broadcast_to(value[None], (count,) + value.shape)
    return lax.all_to_all(wide, axes, 0, 0, tiled=True)


def shards(
    feature_ids,
    context_ids,
    shown_positions,
    clicked_positions,
    clicks,
    embed_table,
    cross_weight,
    deep_weight,
    cross_bias,
    deep_bias,
    out_weight,
    shown_embed,
    click_embed,
    theta_relevant,
    theta_irrelevant,
):
    n_z, n_x, n_mp = lax.axis_size("z"), lax.axis_size("x"), lax.axis_size("mp")
    n_zx = n_z * n_x
    n_dp = 2 * n_zx
    row_count = context_ids.shape[0]
    part = row_count // n_mp
    depth, width = cross_weight.shape
    full = n_mp * width
    core = lax.axis_index("c")
    mine = lax.axis_index("mp")

    with jax.named_scope("weights_dp"):
        both = jnp.stack([cross_weight, deep_weight])
        held = gather(both, ("z", "x"), n_zx)
        other = swap(held)
        cores = jnp.where(core == 0, jnp.stack([held, other], 1), jnp.stack([other, held], 1))
        cross_col = cores[:, :, 0].reshape(full, width)
    with jax.named_scope("deep_weight_mp"):
        deep_all = gather(held[:, 1], "mp", n_mp)
        deep_other = swap(deep_all)
        deep_cores = jnp.where(
            core == 0, jnp.stack([deep_all, deep_other], 2), jnp.stack([deep_other, deep_all], 2)
        )
        deep_full = deep_cores.transpose(1, 2, 3, 0, 4).reshape(full, full)
    with jax.named_scope("vectors_mp"):
        vectors = gather(jnp.stack([deep_bias, out_weight]), "mp", n_mp)
        deep_bias_full = vectors[:, 0].reshape(full)
        out_full = vectors[:, 1].reshape(full)

    with jax.named_scope("embed"):
        base_rows = embed(feature_ids, embed_table)
        base_float = base_rows.astype(F32)
    with jax.named_scope("base_mp"):
        base_full = gather(base_rows, "mp", n_mp).transpose(1, 0, 2).reshape(row_count, full)

    with jax.named_scope("click_models"):
        ctx_count = theta_relevant.shape[0]
        local_ctx = context_ids - mine * ctx_count
        select = local_ctx[:, None] == jnp.arange(ctx_count)[None, :]
        selector = select.astype(F32)
        owned = (local_ctx >= 0) & (local_ctx < ctx_count)
        features = jnp.tanh(
            table_lookup(shown_positions, shown_embed)
            + table_lookup(clicked_positions, click_embed)
        )
        rel_rows = jnp.dot(selector, theta_relevant, precision=lax.Precision.HIGHEST)
        irr_rows = jnp.dot(selector, theta_irrelevant, precision=lax.Precision.HIGHEST)
        mu_rel = jax.nn.sigmoid(jnp.sum(rel_rows * features, axis=1))
        mu_irr = jax.nn.sigmoid(jnp.sum(irr_rows * features, axis=1))
        click_float = clicks.astype(F32)
        features_t = features.T
        sent = jnp.where(owned[None, :], jnp.stack([mu_rel, mu_irr]), 0.0)
        sent = sent.reshape(2, n_mp, part).transpose(1, 0, 2)
        mu_mine = jnp.sum(lax.all_to_all(sent, "mp", 0, 0, tiled=True), axis=0)
        click_mine = lax.dynamic_slice(click_float, (mine * part,), (part,))

    with jax.named_scope("cross"):
        cross_pre = jnp.dot(base_full, cross_col, preferred_element_type=F32)
        crossed = (base_float * (cross_pre + cross_bias) + base_float).astype(BF16)
    with jax.named_scope("crossed_mp"):
        crossed_mine = lax.all_to_all(crossed.reshape(n_mp, part, width), "mp", 0, 0, tiled=True)
        crossed_mine = crossed_mine.transpose(1, 0, 2).reshape(part, full)
    with jax.named_scope("deep"):
        deep_pre = jnp.dot(crossed_mine, deep_full, preferred_element_type=F32) + deep_bias_full
        gating = jax.nn.sigmoid(deep_pre)
        hidden = (deep_pre * gating).astype(BF16).astype(F32)
        slope = gating * (1.0 + deep_pre * (1.0 - gating))
        score = jnp.sum(hidden * out_full, axis=1)
        rel_mine = jax.nn.sigmoid(score)
        post_mine = posterior_of(rel_mine, mu_mine[0], mu_mine[1], click_mine)
        score_grad = rel_mine - post_mine
        pre_grad = score_grad[:, None] * out_full[None, :] * slope
        pre_grad_b = pre_grad.astype(BF16)
        deep_bias_part = jnp.sum(pre_grad, axis=0)
        out_part = jnp.sum(score_grad[:, None] * hidden, axis=0)
    with jax.named_scope("crossed_grad"):
        crossed_grad = lax.dot_general(
            pre_grad_b, deep_full, (((1,), (1,)), ((), ())), preferred_element_type=F32
        ).astype(BF16)
        back = crossed_grad.reshape(part, n_mp, width).transpose(1, 0, 2)
        extra = jnp.stack([deep_bias_part, out_part]).reshape(2, n_mp, width).transpose(1, 0, 2)
        extra_hi = extra.astype(BF16)
        extra_lo = (extra - extra_hi.astype(F32)).astype(BF16)
        pad = jnp.zeros((n_mp, 4, width), BF16)
        back = lax.all_to_all(
            jnp.concatenate([back, extra_hi, extra_lo, pad], axis=1), "mp", 0, 0, tiled=True
        )
        crossed_back = back[:, :part].reshape(row_count, width).astype(F32)
        extra_sum = jnp.sum(
            back[:, part : part + 2].astype(F32) + back[:, part + 2 : part + 4].astype(F32), axis=0
        )
    with jax.named_scope("deep_grad"):
        deep_part = lax.dot_general(
            crossed_mine, pre_grad_b, (((0,), (0,)), ((), ())), preferred_element_type=F32
        )
        deep_part = deep_part.reshape(n_zx, 2, depth, full)
        deep_keep = jnp.where(core == 0, deep_part[:, 0], deep_part[:, 1])
        deep_send = jnp.where(core == 0, deep_part[:, 1], deep_part[:, 0]).astype(BF16)
        deep_pair = (deep_keep + swap(deep_send).astype(F32)).astype(BF16)
        deep_pair = deep_pair.reshape(n_z, n_x, depth, n_mp, width).transpose(1, 3, 0, 2, 4)
        deep_pair = deep_pair.reshape(n_x * n_mp, n_z, depth, width)
        deep_xm = lax.all_to_all(deep_pair, ("x", "mp"), 0, 0, tiled=True)
        deep_xm = jnp.sum(deep_xm.astype(F32), axis=0).astype(BF16)
        deep_z = lax.all_to_all(deep_xm, "z", 0, 0, tiled=True)
        deep_shard = jnp.sum(deep_z.astype(F32), axis=0)

    with jax.named_scope("cross_grad"):
        cross_pre_grad = crossed_back * base_float
        cross_pre_b = cross_pre_grad.astype(BF16)
        cross_part = lax.dot_general(
            base_full, cross_pre_b, (((0,), (0,)), ((), ())), preferred_element_type=F32
        )
        vec_part = jnp.concatenate([jnp.sum(cross_pre_grad, axis=0)[None], extra_sum])
        message = jnp.concatenate(
            [
                cross_part.astype(BF16).reshape(n_dp, depth, width),
                jnp.broadcast_to(vec_part.astype(BF16)[None], (n_dp, 3, width)),
                jnp.zeros((n_dp, 5, width), BF16),
            ],
            axis=1,
        )
        got = lax.all_to_all(message, DP, 0, 0, tiled=True)
        got_sum = jnp.sum(got.astype(F32), axis=0)
        cross_shard = got_sum[:depth]
        vec_sum = got_sum[depth : depth + 3]

    with jax.named_scope("norm"):
        local_squares = (
            jnp.sum(cross_shard * cross_shard)
            + jnp.sum(deep_shard * deep_shard)
            + jnp.where(lax.axis_index(DP) == 0, jnp.sum(vec_sum * vec_sum), 0.0)
        )
        squares = jnp.broadcast_to(local_squares, (n_dp, 128))
        squares = jnp.sum(lax.all_to_all(squares, DP, 0, 0, tiled=True), axis=0)
        squares = jnp.broadcast_to(squares[None], (n_mp, 128))
        squares = jnp.sum(lax.all_to_all(squares, "mp", 0, 0, tiled=True), axis=0)[0]
        norm_scale = 1.0 / jnp.sqrt(squares / (2 * full * full + 3 * full) + 1e-06)

    with jax.named_scope("relevance_mp"):
        relevance = gather(rel_mine, "mp", n_mp).reshape(row_count)
    with jax.named_scope("stats"):
        posterior = posterior_of(relevance, mu_rel, mu_irr, click_float)
        hess_w = jnp.concatenate(
            [
                selector * (posterior * mu_rel * (1.0 - mu_rel))[:, None],
                selector * ((1.0 - posterior) * mu_irr * (1.0 - mu_irr))[:, None],
            ],
            axis=1,
        ).astype(BF16)
        grad_w = jnp.concatenate(
            [
                selector * (posterior * (click_float - mu_rel))[:, None],
                selector * ((1.0 - posterior) * (click_float - mu_irr))[:, None],
            ],
            axis=1,
        )
        feats = features.shape[1]
        outer = (features_t[:, None, :] * features_t[None, :, :]).astype(BF16)
        hess_part = jnp.dot(
            outer.reshape(feats * feats, row_count), hess_w, preferred_element_type=F32
        ).reshape(feats, feats, 2 * ctx_count)
        grad_part = jnp.dot(features_t, grad_w, precision=lax.Precision.HIGHEST)
        stats = jnp.concatenate(
            [hess_part, grad_part[:, None, :], jnp.zeros((feats, 7, 2 * ctx_count), F32)], axis=1
        )
        stats = stats.reshape(n_zx, 2, feats + 8, 2 * ctx_count)
        stats_keep = jnp.where(core == 0, stats[:, 0], stats[:, 1])
        stats_send = jnp.where(core == 0, stats[:, 1], stats[:, 0]).astype(BF16)
        stats_pair = (stats_keep + swap(stats_send).astype(F32)).astype(BF16)
        stats_zx = lax.all_to_all(stats_pair, ("z", "x"), 0, 0, tiled=True)
        stats_sum = jnp.sum(stats_zx.astype(F32), axis=0)
        hess_out = stats_sum[:feats].T.reshape(2, ctx_count, 1, feats)
        stat_grad_out = stats_sum[feats].reshape(2, ctx_count, 1)

    return (
        hess_out,
        stat_grad_out,
        cross_shard * norm_scale,
        deep_shard * norm_scale,
        vec_sum[0] * norm_scale,
        vec_sum[1] * norm_scale,
        vec_sum[2] * norm_scale,
    )


def solution(mesh):
    devices = np.asarray(mesh.devices).reshape(8, 4, 2, 4)
    fine = Mesh(devices, ("z", "x", "c", "mp"))
    return jax.shard_map(
        shards,
        mesh=fine,
        in_specs=(
            P(DP, None),
            P(DP),
            P(DP),
            P(DP),
            P(DP),
            P(None, "mp"),
            P(DP, "mp"),
            P(DP, "mp"),
            P("mp"),
            P("mp"),
            P("mp"),
            P(),
            P(),
            P("mp", None),
            P("mp", None),
        ),
        out_specs=(
            P(None, "mp", DP, None),
            P(None, "mp", DP),
            P(DP, "mp"),
            P(DP, "mp"),
            P("mp"),
            P("mp"),
            P("mp"),
        ),
        check_vma=False,
    )
```

time: 841 us -> 269 us (0.32)
  blocking collectives: 323 us -> 15.5 us
  waiting for transfers between devices: 356 us -> 90.8 us
  starting transfers between devices: 0.29 us -> 83.5 us
  local copies, waits for them, and re-layouts: 65.1 us -> 20 us
  matrix products: 53 us -> 17.4 us
  between operations: 18.5 us -> 3.2 us
  Pallas kernels: 0 us -> 8.49 us
    unnamed x9 -> x0, waiting for transfers between devices: 232 us -> none
    psum x4 -> x0, blocking collectives: 219 us -> none  [the longest x1 129 us: shards(): lax.psum((cross_bias_grad, deep_bias_grad, out_grad), 'dp')]
    reduce_scatter x3 -> x0, waiting for transfers between devices: 124 us -> none  [the longest x1 73.1 us: shards(): lax.psum_scatter(deep_part, 'dp', scatter_dimension=0, tiled=True)]
    all_gather x2 -> x0, blocking collectives: 104 us -> none  [the longest x1 54.7 us: shards(): lax.all_gather(cross_weight, 'dp', axis=0, tiled=True)]
    all_to_all x0 -> x13, waiting for transfers between devices: none -> 88.6 us  [the longest x1 26.8 us: shards(): stats_zx = lax.all_to_all(stats_pair, ('z', 'x'), 0, 0, tiled=True)]
    all_to_all x0 -> x13, starting transfers between devices: none -> 67.7 us  [the longest x5 28 us: gather(): return lax.all_to_all(wide, axes, 0, 0, tiled=True)]
    gather x8 -> x0, local copies, waits for them, and re-layouts: 37.5 us -> none  [shards(): jnp.take(embed_table, feature_ids[:, slot_index], axis=0)]
    dot_general x9 -> x7, matrix products: 50.8 us -> 13.7 us  [the longest x1 4.34 us: shards(): jnp.dot(outer.reshape(feats * feats, row_count), hess_w, preferred_elemen...]
  transfers between devices with their start and end apart: 7 -> 17, of which waited for: 5 -> 12; matrix products, arithmetic and copies ran while one was open for 9% -> 18% of each run, Pallas kernels for 0% -> 3%
where the time goes in v1:
time: 269 us; the launch traced here: 265 us
  waiting for transfers between devices  90.8 us (34%)
  starting transfers between devices  83.5 us (31%)
  other arithmetic  25.8 us (10%)
  local copies, waits for them, and re-layouts  20 us (7%)
  matrix products  17.4 us (6%)
  blocking collectives  15.5 us (6%)
  Pallas kernels  8.49 us (3%)
  between operations  3.2 us (1%)
    all_to_all x5, starting transfers between devices, gather(): return lax.all_to_all(wide, axes, 0, 0, tiled=True)  28 us
    all_to_all x1, waiting for transfers between devices, shards(): stats_zx = lax.all_to_all(stats_pair, ('z', 'x'), 0, 0, tiled=True)  26.8 us
    all_to_all x5, waiting for transfers between devices, gather(): return lax.all_to_all(wide, axes, 0, 0, tiled=True)  23.4 us
    ppermute x4, starting transfers between devices, swap(): return lax.ppermute(value, 'c', [(0, 1), (1, 0)])  15.8 us
    all_to_all x1, blocking collectives, shards(): squares = jnp.sum(lax.all_to_all(squares, DP, 0, 0, tiled=True), axis=0)  15.5 us
    all_to_all x1, waiting for transfers between devices, shards(): got = lax.all_to_all(message, DP, 0, 0, tiled=True)  12.8 us
    all_to_all x1, starting transfers between devices, shards(): got = lax.all_to_all(message, DP, 0, 0, tiled=True)  10 us
    all_to_all x1, waiting for transfers between devices, shards(): lax.all_to_all(jnp.concatenate([back, extra_hi, extra_lo, pad], axis=1),...  9.46 us
  transfers between devices with their start and end apart: 17, of which 12 were waited for; matrix products, arithmetic and copies ran while one was open for 18% of the time, Pallas kernels for 3%

profile of v1, /device:TPU:1, one launch (start us, length us, event | category | flops | bytes accessed | tf_op | source)
XLA Modules:
  0.0 264.6 jit_solution(9142484555095288491)
XLA Ops:
  2.0 5.0 %all-to-all-start.4 = ((f32[4,2,256]{2,1,0:T(2,128)}), f32[4,2,256]{2,1,0:T(2,128)S(1)}, u32[]{:S(2)}, u32[]{:S(2)}) async-start(f32[4,2,256]{2,1,0:T(2,128)} %broadcast_in_dim.42), calls=%async_computation.4 | async-start | bytes 16384 | tf_op jit(solution)/shard_map/vectors_mp/all_to_all | solution.py:75
  7.0 1.3 fusion.32
  8.3 1.4 fusion.12
  12.0 11.0 %all-to-all-start.1 = ((bf16[32,2,16,256]{3,2,1,0:T(8,128)(2,1)}), bf16[32,2,16,256]{3,2,1,0:T(8,128)(2,1)S(1)}, u32[]{:S(2)}, u32[]{:S(2)}) async-start(bf16[32,2,16,256]{3,2,1,0:T(8,128)(2,1)} %broadcast_in_dim.39), calls=%async_computation.1 | async-start | bytes 1048576 | tf_op jit(solution)/shard_map/weights_dp/all_to_all | solution.py:75
  24.9 12.7 %all-to-all-done.1 = bf16[32,2,16,256]{3,2,1,0:T(8,128)(2,1)S(1)} async-done(((bf16[32,2,16,256]{3,2,1,0:T(8,128)(2,1)}), bf16[32,2,16,256]{3,2,1,0:T(8,128)(2,1)S(1)}, u32[]{:S(2)}, u32[]{:S(2)}) %all-to-all-start.1) | async-done | bytes 524320 | tf_op jit(solution)/shard_map/weights_dp/all_to_all | solution.py:75
  37.6 4.3 %all-to-all-start.7 = ((f32[4,2,256]{2,1,0:T(2,128)}), f32[4,2,256]{2,1,0:T(2,128)S(1)}, u32[]{:S(2)}, u32[]{:S(2)}) async-start(f32[4,2,256]{2,1,0:T(2,128)} %fusion.39), calls=%async_computation.7 | async-start | bytes 16384 | tf_op jit(solution)/shard_map/click_models/all_to_all | solution.py:147
  41.9 4.1 %all-to-all-done.7 = f32[4,2,256]{2,1,0:T(2,128)S(1)} async-done(((f32[4,2,256]{2,1,0:T(2,128)}), f32[4,2,256]{2,1,0:T(2,128)S(1)}, u32[]{:S(2)}, u32[]{:S(2)}) %all-to-all-start.7) | async-done | bytes 8224 | tf_op jit(solution)/shard_map/click_models/all_to_all | solution.py:147
  47.1 4.2 %all-to-all-start.3 = ((bf16[4,32,16,256]{3,2,1,0:T(8,128)(2,1)}), bf16[4,32,16,256]{3,2,1,0:T(8,128)(2,1)}, u32[]{:S(2)}, u32[]{:S(2)}) async-start(bf16[4,32,16,256]{3,2,1,0:T(8,128)(2,1)} %broadcast_in_dim.41), calls=%async_computation.3 | async-start | bytes 2097152 | tf_op jit(solution)/shard_map/deep_weight_mp/all_to_all | solution.py:75
  51.6 8.5 %embed.1 = bf16[1024,256]{1,0:T(8,128)(2,1)S(1)} custom-call(s32[1024,8]{1,0:T(8,128)S(1)} %copy.99.ids_ref, bf16[4096,256]{1,0:T(8,128)(2,1)S(1)} %copy-done.1), custom_call_target="tpu_custom_call" | custom-call | tf_op jit(solution)/shard_map/embed/pallas_call | solution.py:59
  60.3 1.1 all-to-all-done.3
  61.4 1.6 broadcast_in_dim.38
  63.0 3.7 %all-to-all-start = ((bf16[4,1024,256]{1,2,0:T(8,128)(2,1)}), bf16[4,1024,256]{1,2,0:T(8,128)(2,1)S(1)}, u32[]{:S(2)}, u32[]{:S(2)}) async-start(bf16[4,1024,256]{1,2,0:T(8,128)(2,1)} %broadcast_in_dim.38), calls=%async_computation | async-start | bytes 4194304 | tf_op jit(solution)/shard_map/base_mp/all_to_all | solution.py:75
  67.6 6.0 %collective-permute-start = (bf16[32,2,16,256]{3,2,0,1:T(8,128)(2,1)}, bf16[32,2,16,256]{3,2,0,1:T(8,128)(2,1)S(1)}, u32[]{:S(2)}, u32[]{:S(2)}) collective-permute-start(bf16[32,2,16,256]{3,2,0,1:T(8,128)(2,1)} %copy.128), channel_id=1, source_target_pairs={{0,4},{4,0},{1,5},{5,1},{2,6},{6,2},{3,7},{7,3},{8,12},{12,8},{9,1... | collective-permute-start | bytes 1572872 | tf_op jit(solution)/shard_map/weights_dp/ppermute | solution.py:70
  74.0 2.2 collective-permute-done
  76.1 1.9 fusion.25
  78.0 8.7 %all-to-all-done = bf16[4,1024,256]{1,2,0:T(8,128)(2,1)S(1)} async-done(((bf16[4,1024,256]{1,2,0:T(8,128)(2,1)}), bf16[4,1024,256]{1,2,0:T(8,128)(2,1)S(1)}, u32[]{:S(2)}, u32[]{:S(2)}) %all-to-all-start) | async-done | bytes 2097184 | tf_op jit(solution)/shard_map/base_mp/all_to_all | solution.py:75
  86.8 1.8 fusion.10
  89.6 3.6 %all-to-all-start.2 = ((bf16[4,256,256]{1,2,0:T(8,128)(2,1)}), bf16[4,256,256]{1,2,0:T(8,128)(2,1)S(1)}, u32[]{:S(2)}, u32[]{:S(2)}) async-start(bf16[4,256,256]{1,2,0:T(8,128)(2,1)} %copy.103), calls=%async_computation.2 | async-start | bytes 1048576 | tf_op jit(solution)/shard_map/crossed_mp/all_to_all | solution.py:154
  93.3 2.6 fusion.6
  95.9 2.7 %copy.104 = bf16[32,2,16,4,256]{4,3,2,1,0:T(4,128)(2,1)S(1)} copy(bf16[32,2,16,4,256]{4,2,0,3,1:T(8,128)(2,1)S(1)} %fusion.6) | data formatting | bytes 4194304 | tf_op jit(solution)/shard_map/deep_weight_mp/transpose | solution.py:117
  98.6 1.8 copy.123
  100.4 2.8 %fusion.15 = (f32[256]{0:T(256)S(1)}, bf16[256,1024]{1,0:T(8,128)(2,1)S(1)}, f32[256,1024]{1,0:T(8,128)S(1)}) fusion(f32[1024]{0:T(1024)S(1)} %bitcast.166, f32[1024]{0:T(1024)S(1)} %bitcast.176, bf16[256,1024]{0,1:T(8,128)(2,1)S(1)} %bitcast.154, bf16[1024,1024]{1,0:T(8,128)(2,1)} %bitcast.151), kind=kOutput, calls=%fused_computation.35 | convolution fusion | flops 539229952 | bytes 4203520 | tf_op jit(solution)/shard_map/deep/dot_general | solution.py:157
  105.5 4.0 %all-to-all-start.5 = ((f32[4,1,256]{2,1,0:T(1,128)}), f32[4,1,256]{2,1,0:T(1,128)S(1)}, u32[]{:S(2)}, u32[]{:S(2)}) async-start(f32[4,1,256]{2,1,0:T(1,128)} %broadcast_in_dim.43), calls=%async_computation.5 | async-start | bytes 8192 | tf_op jit(solution)/shard_map/relevance_mp/all_to_all | solution.py:75
  109.5 2.4 fusion.28
  111.9 1.9 copy-done.3
  113.8 1.1 fusion.17
  115.0 7.8 %collective-permute-start.3 = (bf16[32,16,1024]{2,1,0:T(8,128)(2,1)}, bf16[32,16,1024]{2,1,0:T(8,128)(2,1)}, u32[]{:S(2)}, u32[]{:S(2)}) collective-permute-start(bf16[32,16,1024]{2,1,0:T(8,128)(2,1)} %fusion.17), channel_id=1, source_target_pairs={{0,4},{4,0},{1,5},{5,1},{2,6},{6,2},{3,7},{7,3},{8,12},{12,8},{9,1... | collective-permute-start | bytes 3145736 | tf_op jit(solution)/shard_map/deep_grad/ppermute | solution.py:70
  123.8 4.5 %all-to-all-start.8 = ((bf16[4,264,256]{2,1,0:T(8,128)(2,1)}), bf16[4,264,256]{2,1,0:T(8,128)(2,1)S(1)}, u32[]{:S(2)}, u32[]{:S(2)}) async-start(bf16[4,264,256]{2,1,0:T(8,128)(2,1)} %maximum_maximum_fusion.2), calls=%async_computation.8 | async-start | bytes 1081344 | tf_op jit(solution)/shard_map/crossed_grad/all_to_all | solution.py:178
  128.3 9.5 %all-to-all-done.8 = bf16[4,264,256]{2,1,0:T(8,128)(2,1)S(1)} async-done(((bf16[4,264,256]{2,1,0:T(8,128)(2,1)}), bf16[4,264,256]{2,1,0:T(8,128)(2,1)S(1)}, u32[]{:S(2)}, u32[]{:S(2)}) %all-to-all-start.8) | async-done | bytes 540704 | tf_op jit(solution)/shard_map/crossed_grad/all_to_all | solution.py:178
  138.9 1.2 maximum_maximum_fusion.1
  140.1 10.0 %all-to-all-start.9 = ((bf16[64,24,256]{2,1,0:T(8,128)(2,1)}), bf16[64,24,256]{2,1,0:T(8,128)(2,1)S(1)}, u32[]{:S(2)}, u32[]{:S(2)}) async-start(bf16[64,24,256]{2,1,0:T(8,128)(2,1)} %maximum_maximum_fusion.1), calls=%async_computation.9 | async-start | bytes 1572864 | tf_op jit(solution)/shard_map/cross_grad/all_to_all | solution.py:215
  151.8 4.3 %fusion = f32[64,64,256]{2,1,0:T(8,128)} fusion(f32[64,1024]{1,0:T(8,128)S(1)} %bitcast.147, bf16[1024,128]{1,0:T(8,128)(2,1)S(1)} %get-tuple-element.62, bf16[1024,128]{1,0:T(8,128)(2,1)S(1)} %get-tuple-element.61), kind=kOutput, calls=%fused_computation.1 | convolution fusion | flops 2156920832 | bytes 4980736 | tf_op jit(solution)/shard_map/stats/dot_general | solution.py:252
  156.2 1.8 fusion.9
  158.8 1.2 copy.115
  160.0 12.8 %all-to-all-done.9 = bf16[64,24,256]{2,1,0:T(8,128)(2,1)S(1)} async-done(((bf16[64,24,256]{2,1,0:T(8,128)(2,1)}), bf16[64,24,256]{2,1,0:T(8,128)(2,1)S(1)}, u32[]{:S(2)}, u32[]{:S(2)}) %all-to-all-start.9) | async-done | bytes 786464 | tf_op jit(solution)/shard_map/cross_grad/all_to_all | solution.py:215
  172.9 4.0 %all-to-all-start.10 = ((bf16[16,8,16,256]{3,2,1,0:T(8,128)(2,1)}), bf16[16,8,16,256]{3,2,1,0:T(8,128)(2,1)S(1)}, u32[]{:S(2)}, u32[]{:S(2)}) async-start(bf16[16,8,16,256]{3,2,1,0:T(8,128)(2,1)} %bitcast.52), calls=%async_computation.10 | async-start | bytes 2097152 | tf_op jit(solution)/shard_map/deep_grad/all_to_all | solution.py:195
  176.9 2.9 %maximum_maximum_fusion = f32[32,2,72,256]{3,2,1,0:T(8,128)S(1)} fusion(f32[32,2,1,256]{3,2,1,0:T(1,128)S(1)} %concatenate.42, f32[32,2,64,256]{3,2,1,0:T(8,128)} %bitcast.146, f32[72]{0:T(128)S(1)} %pad.15.clone), kind=kLoop, calls=%fused_computation.4 | loop fusion | flops 2359296 | bytes 8978720 | tf_op jit(solution)/shard_map/stats/concatenate | solution.py:256
  179.8 2.1 copy-done.2
  182.0 1.3 fusion.11
  183.3 1.9 collective-permute-start.2
  185.3 6.5 %all-to-all-done.10 = bf16[16,8,16,256]{3,2,1,0:T(8,128)(2,1)S(1)} async-done(((bf16[16,8,16,256]{3,2,1,0:T(8,128)(2,1)}), bf16[16,8,16,256]{3,2,1,0:T(8,128)(2,1)S(1)}, u32[]{:S(2)}, u32[]{:S(2)}) %all-to-all-start.10) | async-done | bytes 1048608 | tf_op jit(solution)/shard_map/deep_grad/all_to_all | solution.py:195
  192.6 6.1 %all-to-all-start.11 = ((bf16[8,16,256]{2,1,0:T(8,128)(2,1)}), bf16[8,16,256]{2,1,0:T(8,128)(2,1)S(1)}, u32[]{:S(2)}, u32[]{:S(2)}) async-start(bf16[8,16,256]{2,1,0:T(8,128)(2,1)} %reduce_sum.167), calls=%async_computation.11 | async-start | bytes 131072 | tf_op jit(solution)/shard_map/deep_grad/all_to_all | solution.py:197
  200.5 5.4 %all-to-all-done.11 = bf16[8,16,256]{2,1,0:T(8,128)(2,1)S(1)} async-done(((bf16[8,16,256]{2,1,0:T(8,128)(2,1)}), bf16[8,16,256]{2,1,0:T(8,128)(2,1)S(1)}, u32[]{:S(2)}, u32[]{:S(2)}) %all-to-all-start.11) | async-done | bytes 65568 | tf_op jit(solution)/shard_map/deep_grad/all_to_all | solution.py:197
  207.9 15.5 %all_to_all.73 = f32[64,1,128]{2,1,0:T(1,128)S(1)} all-to-all(f32[64,1,128]{2,1,0:T(1,128)S(1)} %broadcast_in_dim.51), channel_id=1, replica_groups=mesh['z'=8,'x'=4,'c'=2,'mp'=4] {'z','x','c'}, dimensions={0} | all-to-all | bytes 65536 | tf_op jit(solution)/shard_map/norm/all_to_all | solution.py:227
  224.0 3.2 %all-to-all-start.13 = ((f32[4,1,128]{2,1,0:T(1,128)}), f32[4,1,128]{2,1,0:T(1,128)S(1)}, u32[]{:S(2)}, u32[]{:S(2)}) async-start(f32[4,1,128]{2,1,0:T(1,128)} %broadcast_in_dim.52), calls=%async_computation.13 | async-start | bytes 4096 | tf_op jit(solution)/shard_map/norm/all_to_all | solution.py:229
  227.2 3.9 %fusion.5 = bf16[32,72,256]{2,1,0:T(8,128)(2,1)} fusion(bf16[32,72,256]{2,1,0:T(8,128)(2,1)S(1)} %collective-permute-done.2, f32[32,2,72,256]{3,2,1,0:T(8,128)} %copy-done.2, pred[]{:T(512)S(6)} %eq.22), kind=kLoop, calls=%fused_computation.8 | loop fusion | flops 2359296 | bytes 7077889 | tf_op jit(solution)/shard_map/stats/convert_element_type | solution.py:262
  231.2 3.9 %all-to-all-start.6 = ((bf16[32,72,256]{2,1,0:T(8,128)(2,1)}), bf16[32,72,256]{2,1,0:T(8,128)(2,1)S(1)}, u32[]{:S(2)}, u32[]{:S(2)}) async-start(bf16[32,72,256]{2,1,0:T(8,128)(2,1)} %fusion.5), calls=%async_computation.6 | async-start | bytes 2359296 | tf_op jit(solution)/shard_map/stats/all_to_all | solution.py:263
  236.4 26.8 %all-to-all-done.6 = bf16[32,72,256]{2,1,0:T(8,128)(2,1)S(1)} async-done(((bf16[32,72,256]{2,1,0:T(8,128)(2,1)}), bf16[32,72,256]{2,1,0:T(8,128)(2,1)S(1)}, u32[]{:S(2)}, u32[]{:S(2)}) %all-to-all-start.6) | async-done | bytes 1179680 | tf_op jit(solution)/shard_map/stats/all_to_all | solution.py:263
  (105 shorter events, 22.0 us)
Async XLA Ops:
  0.6 6.4 %copy-start = (f32[64,64]{1,0:T(8,128)S(1)}, f32[64,64]{1,0:T(8,128)}, u32[]{:S(2)}) copy-start(f32[64,64]{1,0:T(8,128)} %param.26) | copy-start | bytes 49156
  0.6 22.4 %copy-start.14 = (s32[1024]{0:T(1024)S(1)}, s32[1024]{0:T(1024)}, u32[]{:S(2)}) copy-start(s32[1024]{0:T(1024)} %param.16) | copy-start | bytes 12292
  0.7 22.5 %copy-start.11 = (f32[128,64]{0,1:T(8,128)S(1)}, f32[128,64]{0,1:T(8,128)}, u32[]{:S(2)}) copy-start(f32[128,64]{0,1:T(8,128)} %param.29) | copy-start | bytes 98308
  0.7 23.0 %copy-start.12 = (f32[128,64]{0,1:T(8,128)S(1)}, f32[128,64]{0,1:T(8,128)}, u32[]{:S(2)}) copy-start(f32[128,64]{0,1:T(8,128)} %param.28) | copy-start | bytes 98308
  2.0 9.2 %all-to-all-start.4 = ((f32[4,2,256]{2,1,0:T(2,128)}), f32[4,2,256]{2,1,0:T(2,128)S(1)}, u32[]{:S(2)}, u32[]{:S(2)}) async-start(f32[4,2,256]{2,1,0:T(2,128)} %broadcast_in_dim.42), calls=%async_computation.4 | async-start | bytes 16384 | tf_op jit(solution)/shard_map/vectors_mp/all_to_all | solution.py:75
  12.0 25.6 %all-to-all-start.1 = ((bf16[32,2,16,256]{3,2,1,0:T(8,128)(2,1)}), bf16[32,2,16,256]{3,2,1,0:T(8,128)(2,1)S(1)}, u32[]{:S(2)}, u32[]{:S(2)}) async-start(bf16[32,2,16,256]{3,2,1,0:T(8,128)(2,1)} %broadcast_in_dim.39), calls=%async_computation.1 | async-start | bytes 1048576 | tf_op jit(solution)/shard_map/weights_dp/all_to_all | solution.py:75
  23.7 27.7 %copy-start.13 = (s32[1024,8]{0,1:T(8,128)S(1)}, s32[1024,8]{0,1:T(8,128)}, u32[]{:S(2)}) copy-start(s32[1024,8]{0,1:T(8,128)} %param.15) | copy-start | bytes 98308
  37.6 13.7 %copy-start.5 = (bf16[32,2,16,256]{3,2,1,0:T(8,128)(2,1)}, bf16[32,2,16,256]{3,2,1,0:T(8,128)(2,1)S(1)}, u32[]{:S(2)}) copy-start(bf16[32,2,16,256]{3,2,1,0:T(8,128)(2,1)S(1)} %all-to-all-done.1) | copy-start | bytes 1572868
  37.6 8.4 %all-to-all-start.7 = ((f32[4,2,256]{2,1,0:T(2,128)}), f32[4,2,256]{2,1,0:T(2,128)S(1)}, u32[]{:S(2)}, u32[]{:S(2)}) async-start(f32[4,2,256]{2,1,0:T(2,128)} %fusion.39), calls=%async_computation.7 | async-start | bytes 16384 | tf_op jit(solution)/shard_map/click_models/all_to_all | solution.py:147
  41.9 9.7 %copy-start.1 = (bf16[4096,256]{1,0:T(8,128)(2,1)S(1)}, bf16[4096,256]{1,0:T(8,128)(2,1)}, u32[]{:S(2)}) copy-start(bf16[4096,256]{1,0:T(8,128)(2,1)} %table_ref.1) | copy-start | bytes 6291460
  47.1 14.3 %all-to-all-start.3 = ((bf16[4,32,16,256]{3,2,1,0:T(8,128)(2,1)}), bf16[4,32,16,256]{3,2,1,0:T(8,128)(2,1)}, u32[]{:S(2)}, u32[]{:S(2)}) async-start(bf16[4,32,16,256]{3,2,1,0:T(8,128)(2,1)} %broadcast_in_dim.41), calls=%async_computation.3 | async-start | bytes 2097152 | tf_op jit(solution)/shard_map/deep_weight_mp/all_to_all | solution.py:75
  63.0 3.8 %copy-start.6 = (bf16[32,2,16,256]{3,2,1,0:T(8,128)(2,1)S(1)}, bf16[32,2,16,256]{3,2,1,0:T(8,128)(2,1)}, u32[]{:S(2)}) copy-start(bf16[32,2,16,256]{3,2,1,0:T(8,128)(2,1)} %copy-done.5) | copy-start | bytes 1572868
  63.0 10.8 %copy-start.10 = (s32[1024]{0:T(1024)S(1)}, s32[1024]{0:T(1024)}, u32[]{:S(2)}) copy-start(s32[1024]{0:T(1024)} %param.19) | copy-start | bytes 12292
  63.0 23.7 %all-to-all-start = ((bf16[4,1024,256]{1,2,0:T(8,128)(2,1)}), bf16[4,1024,256]{1,2,0:T(8,128)(2,1)S(1)}, u32[]{:S(2)}, u32[]{:S(2)}) async-start(bf16[4,1024,256]{1,2,0:T(8,128)(2,1)} %broadcast_in_dim.38), calls=%async_computation | async-start | bytes 4194304 | tf_op jit(solution)/shard_map/base_mp/all_to_all | solution.py:75
  66.8 20.0 %copy-start.15 = (f32[256]{0:T(256)S(1)}, f32[256]{0:T(256)}, u32[]{:S(2)}) copy-start(f32[256]{0:T(256)} %param.23) | copy-start | bytes 3076
  67.6 8.5 %collective-permute-start = (bf16[32,2,16,256]{3,2,0,1:T(8,128)(2,1)}, bf16[32,2,16,256]{3,2,0,1:T(8,128)(2,1)S(1)}, u32[]{:S(2)}, u32[]{:S(2)}) collective-permute-start(bf16[32,2,16,256]{3,2,0,1:T(8,128)(2,1)} %copy.128), channel_id=1, source_target_pairs={{0,4},{4,0},{1,5},{5,1},{2,6},{6,2},{3,7},{7,3},{8,12},{12,8},{9,1... | collective-permute-start | bytes 1572872 | tf_op jit(solution)/shard_map/weights_dp/ppermute | solution.py:70
  73.7 19.6 %collective-permute-start.1 = (bf16[4,32,16,256]{3,2,1,0:T(8,128)(2,1)}, bf16[4,32,16,256]{3,2,1,0:T(8,128)(2,1)}, u32[]{:S(2)}, u32[]{:S(2)}) collective-permute-start(bf16[4,32,16,256]{3,2,1,0:T(8,128)(2,1)} %all-to-all-done.3), channel_id=1, source_target_pairs={{0,4},{4,0},{1,5},{5,1},{2,6},{6,2},{3,7},{7,3},{8,12},{12,8},{9,1... | collective-permute-start | bytes 3145736 | tf_op jit(solution)/shard_map/deep_weight_mp/ppermute | solution.py:70
  89.6 10.8 %all-to-all-start.2 = ((bf16[4,256,256]{1,2,0:T(8,128)(2,1)}), bf16[4,256,256]{1,2,0:T(8,128)(2,1)S(1)}, u32[]{:S(2)}, u32[]{:S(2)}) async-start(bf16[4,256,256]{1,2,0:T(8,128)(2,1)} %copy.103), calls=%async_computation.2 | async-start | bytes 1048576 | tf_op jit(solution)/shard_map/crossed_mp/all_to_all | solution.py:154
  100.4 2.9 %copy-start.9 = (bf16[4,256,256]{1,2,0:T(8,128)(2,1)}, bf16[4,256,256]{1,2,0:T(8,128)(2,1)S(1)}, u32[]{:S(2)}) copy-start(bf16[4,256,256]{1,2,0:T(8,128)(2,1)S(1)} %all-to-all-done.2) | copy-start | bytes 1572868
  100.4 2.9 %copy-start.7 = (bf16[128,8,4,256]{3,1,2,0:T(8,128)(2,1)S(1)}, bf16[128,8,4,256]{3,1,2,0:T(8,128)(2,1)}, u32[]{:S(2)}) copy-start(bf16[128,8,4,256]{3,1,2,0:T(8,128)(2,1)} %copy.123) | copy-start | bytes 6291460
  103.3 1.0 copy-start.8
  105.5 18.3 %all-to-all-start.5 = ((f32[4,1,256]{2,1,0:T(1,128)}), f32[4,1,256]{2,1,0:T(1,128)S(1)}, u32[]{:S(2)}, u32[]{:S(2)}) async-start(f32[4,1,256]{2,1,0:T(1,128)} %broadcast_in_dim.43), calls=%async_computation.5 | async-start | bytes 8192 | tf_op jit(solution)/shard_map/relevance_mp/all_to_all | solution.py:75
  111.9 1.9 copy-start.3
  115.0 41.2 %collective-permute-start.3 = (bf16[32,16,1024]{2,1,0:T(8,128)(2,1)}, bf16[32,16,1024]{2,1,0:T(8,128)(2,1)}, u32[]{:S(2)}, u32[]{:S(2)}) collective-permute-start(bf16[32,16,1024]{2,1,0:T(8,128)(2,1)} %fusion.17), channel_id=1, source_target_pairs={{0,4},{4,0},{1,5},{5,1},{2,6},{6,2},{3,7},{7,3},{8,12},{12,8},{9,1... | collective-permute-start | bytes 3145736 | tf_op jit(solution)/shard_map/deep_grad/ppermute | solution.py:70
  123.8 14.0 %all-to-all-start.8 = ((bf16[4,264,256]{2,1,0:T(8,128)(2,1)}), bf16[4,264,256]{2,1,0:T(8,128)(2,1)S(1)}, u32[]{:S(2)}, u32[]{:S(2)}) async-start(bf16[4,264,256]{2,1,0:T(8,128)(2,1)} %maximum_maximum_fusion.2), calls=%async_computation.8 | async-start | bytes 1081344 | tf_op jit(solution)/shard_map/crossed_grad/all_to_all | solution.py:178
  140.1 32.8 %all-to-all-start.9 = ((bf16[64,24,256]{2,1,0:T(8,128)(2,1)}), bf16[64,24,256]{2,1,0:T(8,128)(2,1)S(1)}, u32[]{:S(2)}, u32[]{:S(2)}) async-start(bf16[64,24,256]{2,1,0:T(8,128)(2,1)} %maximum_maximum_fusion.1), calls=%async_computation.9 | async-start | bytes 1572864 | tf_op jit(solution)/shard_map/cross_grad/all_to_all | solution.py:215
  151.8 4.4 %copy-start.4 = (f32[32,2,16,1024]{3,2,1,0:T(8,128)S(1)}, f32[32,2,16,1024]{3,2,1,0:T(8,128)}, u32[]{:S(2)}) copy-start(f32[32,2,16,1024]{3,2,1,0:T(8,128)} %copy-done.3) | copy-start | bytes 12582916
  172.9 18.9 %all-to-all-start.10 = ((bf16[16,8,16,256]{3,2,1,0:T(8,128)(2,1)}), bf16[16,8,16,256]{3,2,1,0:T(8,128)(2,1)S(1)}, u32[]{:S(2)}, u32[]{:S(2)}) async-start(bf16[16,8,16,256]{3,2,1,0:T(8,128)(2,1)} %bitcast.52), calls=%async_computation.10 | async-start | bytes 2097152 | tf_op jit(solution)/shard_map/deep_grad/all_to_all | solution.py:195
  179.8 2.1 copy-start.2
  183.3 43.9 %collective-permute-start.2 = (bf16[32,72,256]{2,1,0:T(8,128)(2,1)}, bf16[32,72,256]{2,1,0:T(8,128)(2,1)S(1)}, u32[]{:S(2)}, u32[]{:S(2)}) collective-permute-start(bf16[32,72,256]{2,1,0:T(8,128)(2,1)} %fusion.11), channel_id=1, source_target_pairs={{0,4},{4,0},{1,5},{5,1},{2,6},{6,2},{3,7},{7,3},{8,12},{12,8},{9,1... | collective-permute-start | bytes 3538952 | tf_op jit(solution)/shard_map/stats/ppermute | solution.py:70
  192.6 13.3 %all-to-all-start.11 = ((bf16[8,16,256]{2,1,0:T(8,128)(2,1)}), bf16[8,16,256]{2,1,0:T(8,128)(2,1)S(1)}, u32[]{:S(2)}, u32[]{:S(2)}) async-start(bf16[8,16,256]{2,1,0:T(8,128)(2,1)} %reduce_sum.167), calls=%async_computation.11 | async-start | bytes 131072 | tf_op jit(solution)/shard_map/deep_grad/all_to_all | solution.py:197
  224.0 7.2 %all-to-all-start.13 = ((f32[4,1,128]{2,1,0:T(1,128)}), f32[4,1,128]{2,1,0:T(1,128)S(1)}, u32[]{:S(2)}, u32[]{:S(2)}) async-start(f32[4,1,128]{2,1,0:T(1,128)} %broadcast_in_dim.52), calls=%async_computation.13 | async-start | bytes 4096 | tf_op jit(solution)/shard_map/norm/all_to_all | solution.py:229
  231.2 32.0 %all-to-all-start.6 = ((bf16[32,72,256]{2,1,0:T(8,128)(2,1)}), bf16[32,72,256]{2,1,0:T(8,128)(2,1)S(1)}, u32[]{:S(2)}, u32[]{:S(2)}) async-start(bf16[32,72,256]{2,1,0:T(8,128)(2,1)} %fusion.5), calls=%async_computation.6 | async-start | bytes 2359296 | tf_op jit(solution)/shard_map/stats/all_to_all | solution.py:263

commit v2 on v1

v2 whole, which is shorter than its diff:
```python
import jax
import jax.numpy as jnp
import numpy as np
from jax import lax
from jax.experimental import pallas as pl
from jax.experimental.pallas import tpu as pltpu
from jax.sharding import Mesh, PartitionSpec as P

DP = ("z", "x", "c")
BF16 = jnp.bfloat16
F32 = jnp.float32


def posterior_of(relevance, mu_rel, mu_irr, click_float):
    on_click = mu_rel * relevance / (mu_rel * relevance + mu_irr * (1.0 - relevance))
    no_click = (
        (1.0 - mu_rel)
        * relevance
        / ((1.0 - mu_rel) * relevance + (1.0 - mu_irr) * (1.0 - relevance))
    )
    return jnp.where(click_float > 0.5, on_click, no_click)


def table_lookup(indices, table):
    onehot_rows = (indices[:, None] == jnp.arange(table.shape[0])[None, :]).astype(F32)
    return jnp.dot(onehot_rows, table, precision=lax.Precision.HIGHEST)


def embed_kernel(ids_ref, table_ref, out_ref, wide_ref):
    rows, slots = ids_ref.shape
    vocab, width = table_ref.shape
    lanes = 256
    tile = 256
    ids = ids_ref[...]
    for s in range(slots):
        wide_ref[s] = jnp.broadcast_to(ids[:, s : s + 1], (rows, lanes)).astype(jnp.int16)
    lane = lax.broadcasted_iota(jnp.int32, (tile, lanes), 1)

    def body(r, carry):
        first = pl.multiple_of(r * tile, tile)
        total = jnp.zeros((tile, width), F32)
        for k in range(vocab // lanes):
            names = (lane + k * lanes).astype(jnp.int16)
            counts = jnp.zeros((tile, lanes), BF16)
            for s in range(slots):
                hit = wide_ref[s, pl.ds(first, tile), :] == names
                counts = counts + jnp.where(hit, jnp.ones((), BF16), jnp.zeros((), BF16))
            total = total + jnp.dot(
                counts, table_ref[k * lanes : (k + 1) * lanes, :], preferred_element_type=F32
            )
        out_ref[pl.ds(first, tile), :] = total.astype(BF16)
        return carry

    lax.fori_loop(0, rows // tile, body, 0)


def embed(ids, table):
    rows = ids.shape[0]
    return pl.pallas_call(
        embed_kernel,
        out_shape=jax.ShapeDtypeStruct((rows, table.shape[1]), BF16),
        in_specs=[pl.BlockSpec(memory_space=pltpu.VMEM)] * 2,
        out_specs=pl.BlockSpec(memory_space=pltpu.VMEM),
        scratch_shapes=[pltpu.VMEM((ids.shape[1], rows, 256), jnp.int16)],
        compiler_params=pltpu.CompilerParams(vmem_limit_bytes=40 * 2**20),
    )(ids, table)


def stats_kernel(core_ref, feats_ref, weights_ref, grads_ref, keep_ref, send_ref):
    feats = feats_ref.shape[0]
    group = 4
    core = core_ref[0]
    head = lax.broadcasted_iota(jnp.int32, (16, grads_ref.shape[1]), 0) == 0
    for out_ref, side in ((keep_ref, core), (send_ref, 1 - core)):

        def body(g, carry, out_ref=out_ref, side=side):
            features = feats_ref[...]
            places = [2 * (group * g + q) + side for q in range(group)]
            outer = jnp.concatenate(
                [(features * feats_ref[pl.ds(i, 1), :]).astype(BF16) for i in places]
            )
            sums = jnp.dot(outer, weights_ref[...], preferred_element_type=F32)
            for q in range(group):
                out_ref[group * g + q, 0:feats, :] = sums[q * feats : (q + 1) * feats].astype(BF16)
                row = jnp.where(head, grads_ref[pl.ds(places[q], 1), :], 0.0)
                out_ref[group * g + q, feats : feats + 16, :] = row.astype(BF16)
            return carry

        lax.fori_loop(0, feats // (2 * group), body, 0)


def stats_blocks(core, features_t, hess_w, grad_part):
    feats, columns = grad_part.shape
    shape = jax.ShapeDtypeStruct((feats // 2, feats + 16, columns), BF16)
    vmem = pl.BlockSpec(memory_space=pltpu.VMEM)
    return pl.pallas_call(
        stats_kernel,
        out_shape=(shape, shape),
        in_specs=[pl.BlockSpec(memory_space=pltpu.SMEM), vmem, vmem, vmem],
        out_specs=(vmem, vmem),
        compiler_params=pltpu.CompilerParams(vmem_limit_bytes=32 * 2**20),
        cost_estimate=pl.CostEstimate(flops=1000, transcendentals=0, bytes_accessed=1000),
    )(core.reshape(1).astype(jnp.int32), features_t, hess_w, grad_part)


def swap(value):
    return lax.ppermute(value, "c", [(0, 1), (1, 0)])


def gather(value, axes, count):
    wide = jnp.broadcast_to(value[None], (count,) + value.shape)
    return lax.all_to_all(wide, axes, 0, 0, tiled=True)


def shift(value, axis, count, ahead):
    return lax.ppermute(value, axis, [(i, (i + ahead) % count) for i in range(count)])


def gather_ahead(value, axis, count):
    return [value] + [shift(value, axis, count, count - t) for t in range(1, count)]


def scatter_ahead(parts, axis):
    count = len(parts)
    total = parts[0].astype(F32)
    for arrived in [shift(parts[t], axis, count, t) for t in range(1, count)]:
        total = total + arrived.astype(F32)
    return total


def to_absolute(blocks, mine):
    count = blocks.shape[0]
    return lax.dynamic_slice_in_dim(
        jnp.concatenate([blocks, blocks]), (count - mine) % count, count, 0
    )


def to_ahead(blocks, mine):
    return lax.dynamic_slice_in_dim(jnp.concatenate([blocks, blocks]), mine, blocks.shape[0], 0)


def block_ahead(blocks, mine, t, dim=0):
    count = blocks.shape[dim]
    return lax.dynamic_index_in_dim(blocks, (mine + t) % count, dim, keepdims=False)


def after(value, *earlier):
    return lax.optimization_barrier((value,) + earlier)[0]


def split3(value):
    high = lax.reduce_precision(value, 8, 7)
    rest = value - high
    middle = lax.reduce_precision(rest, 8, 7)
    return jnp.concatenate([high, middle, rest - middle], axis=-2).astype(BF16)


def join3(value):
    high, middle, low = jnp.split(value.astype(F32), 3, axis=-2)
    return high + (middle + low)


def by_core(core, even, odd):
    return jnp.where(core == 0, even, odd)


def shards(
    feature_ids,
    context_ids,
    shown_positions,
    clicked_positions,
    clicks,
    embed_table,
    cross_weight,
    deep_weight,
    cross_bias,
    deep_bias,
    out_weight,
    shown_embed,
    click_embed,
    theta_relevant,
    theta_irrelevant,
):
    n_z, n_x, n_mp = lax.axis_size("z"), lax.axis_size("x"), lax.axis_size("mp")
    n_zx = n_z * n_x
    n_dp = 2 * n_zx
    row_count = context_ids.shape[0]
    part = row_count // n_mp
    depth, width = cross_weight.shape
    full = n_mp * width
    half = full // 2
    core = lax.axis_index("c")
    mine = lax.axis_index("mp")

    my_x = lax.axis_index("x")

    with jax.named_scope("weights_dp"):
        held = gather(jnp.concatenate([cross_weight, deep_weight]), DP, n_dp)
        cross_col = held[:, :depth].reshape(full, width)
        deep_col = held[:, depth:].reshape(full, width)
    with jax.named_scope("embed"):
        base_rows = embed(feature_ids, embed_table)
        base_float = base_rows.astype(F32)
    with jax.named_scope("base_mp"):
        base = gather_ahead(base_rows, "mp", n_mp)

    with jax.named_scope("click_models"):
        context_ids = after(context_ids, held)
        shown_positions = after(shown_positions, held)
        clicked_positions = after(clicked_positions, held)
        ctx_count = theta_relevant.shape[0]
        local_ctx = context_ids - mine * ctx_count
        select = local_ctx[:, None] == jnp.arange(ctx_count)[None, :]
        selector = select.astype(F32)
        owned = (local_ctx >= 0) & (local_ctx < ctx_count)
        features = jnp.tanh(
            table_lookup(shown_positions, shown_embed)
            + table_lookup(clicked_positions, click_embed)
        )
        rel_rows = jnp.dot(selector, theta_relevant, precision=lax.Precision.HIGHEST)
        irr_rows = jnp.dot(selector, theta_irrelevant, precision=lax.Precision.HIGHEST)
        mu_rel = jax.nn.sigmoid(jnp.sum(rel_rows * features, axis=1))
        mu_irr = jax.nn.sigmoid(jnp.sum(irr_rows * features, axis=1))
        click_float = clicks.astype(F32)
        features_t = features.T
        click_mine = lax.dynamic_slice(click_float, (mine * part,), (part,))
    with jax.named_scope("vectors"):
        sent = jnp.where(owned[None, :], jnp.stack([mu_rel, mu_irr]), 0.0)
        sent = sent.reshape(2, n_mp, part).transpose(1, 0, 2)
        vectors = jnp.broadcast_to(jnp.stack([deep_bias, out_weight])[None], (n_mp, 2, width))
        vectors = split3(jnp.concatenate([sent, vectors], axis=1))
        vectors = jnp.concatenate([vectors, jnp.zeros((n_mp, 4, width), BF16)], axis=1)
        vectors = lax.optimization_barrier(vectors)

    with jax.named_scope("deep_weight_mp"):
        deep_half = lax.dynamic_slice(deep_col, (core * half, 0), (half, width))
        deep_half = gather_ahead(deep_half, "mp", n_mp)

    with jax.named_scope("cross"):
        cross_pre = cross_bias
        for t in range(n_mp):
            rows_t = lax.dynamic_slice(
                cross_col, (((mine + t) % n_mp) * width, 0), (width, width)
            )
            cross_pre = cross_pre + jnp.dot(base[t], rows_t, preferred_element_type=F32)
        crossed = (base_float * cross_pre + base_float).astype(BF16)
    with jax.named_scope("crossed_mp"):
        arrived = jnp.concatenate([crossed.reshape(n_mp, part, width), vectors], axis=1)
        arrived = lax.all_to_all(arrived, "mp", 0, 0, tiled=True)
        crossed_mine = arrived[:, :part].transpose(1, 0, 2).reshape(part, full)
        vectors = join3(arrived[:, part : part + 12])
        mu_mine = jnp.sum(vectors[:, :2], axis=0)
        vectors = to_ahead(vectors, mine)
        deep_bias_full = vectors[:, 2].reshape(full)
        out_full = vectors[:, 3].reshape(full)
    with jax.named_scope("deep_weight_core"):
        deep_half = lax.optimization_barrier((crossed, *deep_half))[1:]
        deep_half = jnp.concatenate(deep_half, axis=1)
        deep_other = swap(deep_half)
        deep_top = by_core(core, deep_half, deep_other)
        deep_low = by_core(core, deep_other, deep_half)
    with jax.named_scope("deep"):
        deep_pre = (
            jnp.dot(crossed_mine[:, :half], deep_top, preferred_element_type=F32)
            + jnp.dot(crossed_mine[:, half:], deep_low, preferred_element_type=F32)
            + deep_bias_full
        )
        gating = jax.nn.sigmoid(deep_pre)
        hidden = (deep_pre * gating).astype(BF16).astype(F32)
        slope = gating * (1.0 + deep_pre * (1.0 - gating))
        score = jnp.sum(hidden * out_full, axis=1)
        rel_mine = jax.nn.sigmoid(score)
        post_mine = posterior_of(rel_mine, mu_mine[0], mu_mine[1], click_mine)
        score_grad = rel_mine - post_mine
        pre_grad = score_grad[:, None] * out_full[None, :] * slope
        pre_grad_b = pre_grad.astype(BF16)
        deep_bias_part = jnp.sum(pre_grad, axis=0)
        out_part = jnp.sum(score_grad[:, None] * hidden, axis=0)
    with jax.named_scope("crossed_grad"):
        back = []
        for k in range(n_mp):
            rows = deep_top if k * width < half else deep_low
            first = (k * width) % half
            back.append(
                lax.dot_general(
                    pre_grad_b,
                    rows[first : first + width],
                    (((1,), (1,)), ((), ())),
                    preferred_element_type=F32,
                ).astype(BF16)
            )
        back = jnp.stack(back)
        extra = jnp.stack([deep_bias_part, out_part]).reshape(2, n_mp, width).transpose(1, 0, 2)
        extra = to_absolute(extra, mine)
        tail = jnp.concatenate([split3(extra), jnp.zeros((n_mp, 2, width), BF16)], axis=1)
        tail = lax.optimization_barrier(tail)
        back = jnp.concatenate([back, tail], axis=1)
        rel_sent = after(rel_mine, back)
        back = lax.all_to_all(back, "mp", 0, 0, tiled=True)
        crossed_back = back[:, :part].reshape(row_count, width).astype(F32)
        extra_sum = jnp.sum(join3(back[:, part : part + 6]), axis=0)
    with jax.named_scope("stats"):
        relevance = jnp.stack(gather_ahead(rel_sent, "mp", n_mp))
        relevance = to_absolute(relevance, mine).reshape(row_count)
        posterior = posterior_of(relevance, mu_rel, mu_irr, click_float)
        hess_w = jnp.concatenate(
            [
                selector * (posterior * mu_rel * (1.0 - mu_rel))[:, None],
                selector * ((1.0 - posterior) * mu_irr * (1.0 - mu_irr))[:, None],
            ],
            axis=1,
        ).astype(BF16)
        grad_w = jnp.concatenate(
            [
                selector * (posterior * (click_float - mu_rel))[:, None],
                selector * ((1.0 - posterior) * (click_float - mu_irr))[:, None],
            ],
            axis=1,
        )
        feats = features.shape[1]
        grad_part = jnp.dot(features_t, grad_w, precision=lax.Precision.HIGHEST)
        stats_keep, stats_send = stats_blocks(core, features_t, hess_w, grad_part)

    with jax.named_scope("deep_grad"):
        slopes = pre_grad_b.reshape(part, n_mp, width).transpose(1, 0, 2)
        deep_part = jnp.stack(
            [
                lax.dot_general(
                    crossed_mine,
                    block_ahead(slopes, n_mp - mine, k),
                    (((0,), (0,)), ((), ())),
                    preferred_element_type=F32,
                ).astype(BF16)
                for k in range(n_mp)
            ]
        ).reshape(n_mp, n_zx, 2, depth, width)
        deep_keep = by_core(core, deep_part[:, :, 0], deep_part[:, :, 1])
        deep_send = by_core(core, deep_part[:, :, 1], deep_part[:, :, 0])
        deep_pair = (deep_keep.astype(F32) + swap(deep_send).astype(F32)).astype(BF16)
        deep_pair, stats_send, crossed_back = lax.optimization_barrier(
            (deep_pair, stats_send, crossed_back)
        )
        deep_sum = lax.all_to_all(deep_pair, "mp", 0, 0, tiled=True)
    with jax.named_scope("stats_sum"):
        stats_pair = (stats_keep.astype(F32) + swap(stats_send).astype(F32)).astype(BF16)
        stats_pair = stats_pair.reshape(n_z, n_x, feats + 16, 2 * ctx_count)
        stats_x = scatter_ahead(
            [block_ahead(stats_pair, my_x, t, 1) for t in range(n_x)], "x"
        ).astype(BF16)
        deep_sum, stats_x = lax.optimization_barrier((deep_sum, stats_x))
        deep_sum = jnp.sum(deep_sum.astype(F32), axis=0).astype(BF16)

    with jax.named_scope("cross_grad"):
        cross_pre_grad = crossed_back * base_float
        cross_pre_b = cross_pre_grad.astype(BF16)
        cross_part = jnp.stack(
            [
                lax.dot_general(
                    base[t], cross_pre_b, (((0,), (0,)), ((), ())), preferred_element_type=F32
                ).astype(BF16)
                for t in range(n_mp)
            ]
        )
        cross_part = to_absolute(cross_part, mine).reshape(n_zx, 2, depth, width)
        vec_part = jnp.concatenate([jnp.sum(cross_pre_grad, axis=0)[None], extra_sum])
        cross_keep = by_core(core, cross_part[:, 0], cross_part[:, 1])
        cross_send = by_core(core, cross_part[:, 1], cross_part[:, 0])
        cross_pair = (cross_keep.astype(F32) + swap(cross_send).astype(F32)).astype(BF16)
        vec_pair = (vec_part + swap(vec_part)).astype(BF16)
    with jax.named_scope("grads_x"):
        message = jnp.concatenate(
            [
                cross_pair,
                deep_sum,
                jnp.broadcast_to(vec_pair[None], (n_zx, 3, width)),
                jnp.zeros((n_zx, 5, width), BF16),
            ],
            axis=1,
        ).reshape(n_z, n_x, 2 * depth + 8, width)
        grads_x = scatter_ahead(
            [block_ahead(message, my_x, t, 1) for t in range(n_x)], "x"
        ).astype(BF16)
    with jax.named_scope("sums_z"):
        got = lax.all_to_all(jnp.concatenate([grads_x, stats_x], axis=1), "z", 0, 0, tiled=True)
        got_sum = jnp.sum(got.astype(F32), axis=0)
        matrix_shards = got_sum[: 2 * depth]
        vec_sum = got_sum[2 * depth : 2 * depth + 3]
        stats_sum = got_sum[2 * depth + 8 :]

    with jax.named_scope("norm"):
        squares = jnp.sum(matrix_shards * matrix_shards) + jnp.where(
            lax.axis_index(DP) == 0, jnp.sum(vec_sum * vec_sum), 0.0
        )
        squares = jnp.broadcast_to(squares, (2 * n_x * n_mp, 128))
        squares = lax.all_to_all(squares, ("x", "c", "mp"), 0, 0, tiled=True)
        squares = jnp.broadcast_to(jnp.sum(squares, axis=0)[None], (n_z, 128))
        squares = jnp.sum(lax.all_to_all(squares, "z", 0, 0, tiled=True), axis=0)[0]
        norm_scale = 1.0 / jnp.sqrt(squares / (2 * full * full + 3 * full) + 1e-06)

    with jax.named_scope("outputs"):
        hess_out = stats_sum[:feats].T.reshape(2, ctx_count, 1, feats)
        stat_grad_out = stats_sum[feats].reshape(2, ctx_count, 1)

    return (
        hess_out,
        stat_grad_out,
        matrix_shards[:depth] * norm_scale,
        matrix_shards[depth:] * norm_scale,
        vec_sum[0] * norm_scale,
        vec_sum[1] * norm_scale,
        vec_sum[2] * norm_scale,
    )


def solution(mesh):
    devices = np.asarray(mesh.devices).reshape(8, 4, 2, 4)
    fine = Mesh(devices, ("z", "x", "c", "mp"))
    return jax.shard_map(
        shards,
        mesh=fine,
        in_specs=(
            P(DP, None),
            P(DP),
            P(DP),
            P(DP),
            P(DP),
            P(None, "mp"),
            P(DP, "mp"),
            P(DP, "mp"),
            P("mp"),
            P("mp"),
            P("mp"),
            P(),
            P(),
            P("mp", None),
            P("mp", None),
        ),
        out_specs=(
            P(None, "mp", DP, None),
            P(None, "mp", DP),
            P(DP, "mp"),
            P(DP, "mp"),
            P("mp"),
            P("mp"),
            P("mp"),
        ),
        check_vma=False,
    )
```

time: 269 us -> 196 us (0.73); the launches traced: 265 us -> 195 us
  waiting for transfers between devices: 90.8 us -> 60.4 us
  starting transfers between devices: 83.5 us -> 62 us
  local copies, waits for them, and re-layouts: 20 us -> 10.3 us
  other arithmetic: 25.8 us -> 17.3 us
  matrix products: 17.4 us -> 12.4 us
  Pallas kernels: 8.49 us -> 13.4 us
    all_to_all x8 -> x5, waiting for transfers between devices: 65.2 us -> 20.8 us  [the longest x1 14.4 us: shards(): lax.all_to_all(jnp.concatenate([grads_x, stats_x], axis=1), 'z', 0, 0, ti...]
    ppermute x0 -> x15, waiting for transfers between devices: none -> 24.1 us  [shift(): lax.ppermute(value, axis, [(i, (i + ahead) % count) for i in range(count)])]
    ppermute x0 -> x15, starting transfers between devices: none -> 21.9 us  [shift(): lax.ppermute(value, axis, [(i, (i + ahead) % count) for i in range(count)])]
    all_to_all x8 -> x5, starting transfers between devices: 39.7 us -> 21 us  [the longest x1 5.75 us: shards(): lax.all_to_all(jnp.concatenate([grads_x, stats_x], axis=1), 'z', 0, 0, ti...]
    all_to_all x5 -> x1, starting transfers between devices: 28 us -> 13.3 us  [gather(): return lax.all_to_all(wide, axes, 0, 0, tiled=True)]
    ppermute x4 -> x5, starting transfers between devices: 15.8 us -> 5.75 us  [swap(): return lax.ppermute(value, 'c', [(0, 1), (1, 0)])]
    all_to_all x5 -> x1, waiting for transfers between devices: 23.4 us -> 13.9 us  [gather(): return lax.all_to_all(wide, axes, 0, 0, tiled=True)]
    pallas_call x0 -> x1, Pallas kernels: none -> 4.94 us  [stats_blocks(): pl.pallas_call(stats_kernel, out_shape=(shape, shape), in_specs=[pl.Block...]
  transfers between devices with their start and end apart: 17 -> 26, of which waited for: 12 -> 12; matrix products, arithmetic and copies ran while one was open for 18% -> 11% of each run, Pallas kernels for 3% -> 7%
where the time goes in v2:
time: 196 us; the launch traced here: 195 us
  starting transfers between devices  62 us (32%)
  waiting for transfers between devices  60.4 us (31%)
  other arithmetic  17.3 us (9%)
  blocking collectives  16 us (8%)
  Pallas kernels  13.4 us (7%)
  matrix products  12.4 us (6%)
  local copies, waits for them, and re-layouts  10.3 us (5%)
  between operations  2.99 us (2%)
    ppermute x15, waiting for transfers between devices, shift(): lax.ppermute(value, axis, [(i, (i + ahead) % count) for i in range(count)])  24.1 us
    ppermute x15, starting transfers between devices, shift(): lax.ppermute(value, axis, [(i, (i + ahead) % count) for i in range(count)])  21.9 us
    all_to_all x1, blocking collectives, shards(): squares = lax.all_to_all(squares, ('x', 'c', 'mp'), 0, 0, tiled=True)  16 us
    all_to_all x1, waiting for transfers between devices, shards(): lax.all_to_all(jnp.concatenate([grads_x, stats_x], axis=1), 'z', 0, 0, ti...  14.4 us
    all_to_all x1, waiting for transfers between devices, gather(): return lax.all_to_all(wide, axes, 0, 0, tiled=True)  13.9 us
    all_to_all x1, starting transfers between devices, gather(): return lax.all_to_all(wide, axes, 0, 0, tiled=True)  13.3 us
    pallas_call x1, Pallas kernels, embed(): pl.pallas_call(embed_kernel, out_shape=jax.ShapeDtypeStruct((rows, table....  8.49 us
    all_to_all x1, starting transfers between devices, shards(): lax.all_to_all(jnp.concatenate([grads_x, stats_x], axis=1), 'z', 0, 0, ti...  5.75 us
  transfers between devices with their start and end apart: 26, of which 12 were waited for; matrix products, arithmetic and copies ran while one was open for 11% of the time, Pallas kernels for 7%

profile of v2, /device:TPU:1, one launch (start us, length us, event | category | flops | bytes accessed | tf_op | source)
XLA Modules:
  0.0 194.8 jit_solution(7393268390245756979)
XLA Ops:
  1.4 1.1 broadcast_in_dim.28
  2.5 13.3 %all-to-all-start = ((bf16[64,32,256]{2,1,0:T(8,128)(2,1)}), bf16[64,32,256]{2,1,0:T(8,128)(2,1)}, u32[]{:S(2)}, u32[]{:S(2)}) async-start(bf16[64,32,256]{2,1,0:T(8,128)(2,1)} %broadcast_in_dim.28), calls=%async_computation | async-start | bytes 2097152 | tf_op jit(solution)/shard_map/weights_dp/all_to_all | solution.py:112
  16.1 8.5 %embed.1 = bf16[1024,256]{1,0:T(8,128)(2,1)S(1)} custom-call(s32[1024,8]{1,0:T(8,128)S(1)} %copy.139.ids_ref, bf16[4096,256]{1,0:T(8,128)(2,1)S(1)} %copy-done.1), custom_call_target="tpu_custom_call" | custom-call | tf_op jit(solution)/shard_map/embed/pallas_call | solution.py:59
  24.6 1.4 collective-permute-start.2
  25.9 2.6 %collective-permute-start.1 = (bf16[1024,256]{1,0:T(8,128)(2,1)S(1)}, bf16[1024,256]{1,0:T(8,128)(2,1)}, u32[]{:S(2)}, u32[]{:S(2)}) collective-permute-start(bf16[1024,256]{1,0:T(8,128)(2,1)S(1)} %embed.1), channel_id=1, source_target_pairs={{0,2},{1,3},{2,0},{3,1},{4,6},{5,7},{6,4},{7,5},{8,10},{9,11},{10,... | collective-permute-start | bytes 1572872 | tf_op jit(solution)/shard_map/base_mp/ppermute | solution.py:116
  28.5 1.1 collective-permute-start
  29.8 13.9 %all-to-all-done = bf16[64,32,256]{2,1,0:T(8,128)(2,1)} async-done(((bf16[64,32,256]{2,1,0:T(8,128)(2,1)}), bf16[64,32,256]{2,1,0:T(8,128)(2,1)}, u32[]{:S(2)}, u32[]{:S(2)}) %all-to-all-start) | async-done | bytes 1048608 | tf_op jit(solution)/shard_map/weights_dp/all_to_all | solution.py:112
  43.7 1.3 fusion.86
  45.0 1.4 collective-permute-start.5
  46.4 2.6 %collective-permute-start.4 = (bf16[512,256]{1,0:T(8,128)(2,1)S(1)}, bf16[512,256]{1,0:T(8,128)(2,1)}, u32[]{:S(2)}, u32[]{:S(2)}) collective-permute-start(bf16[512,256]{1,0:T(8,128)(2,1)S(1)} %constant_dynamic-slice_fusion.6), channel_id=1, source_target_pairs={{0,2},{1,3},{2,0},{3,1},{4,6},{5,7},{6,4},{7,5},{8,10},{9,11},{10,... | collective-permute-start | bytes 786440 | tf_op jit(solution)/shard_map/deep_weight_mp/ppermute | solution.py:116
  51.5 1.1 collective-permute-start.3
  52.9 1.3 fusion.51
  56.3 3.5 %all-to-all-start.1 = ((bf16[4,272,256]{2,1,0:T(8,128)(2,1)}), bf16[4,272,256]{2,1,0:T(8,128)(2,1)S(1)}, u32[]{:S(2)}, u32[]{:S(2)}) async-start(bf16[4,272,256]{2,1,0:T(8,128)(2,1)} %pad_maximum_fusion.1), calls=%async_computation.1 | async-start | bytes 1114112 | tf_op jit(solution)/shard_map/crossed_mp/all_to_all | solution.py:249
  59.8 2.9 %collective-permute-done.4 = bf16[512,256]{1,0:T(8,128)(2,1)} collective-permute-done((bf16[512,256]{1,0:T(8,128)(2,1)S(1)}, bf16[512,256]{1,0:T(8,128)(2,1)}, u32[]{:S(2)}, u32[]{:S(2)}) %collective-permute-start.4) | collective-permute-done | bytes 262176 | tf_op jit(solution)/shard_map/deep_weight_mp/ppermute | solution.py:116
  62.7 1.0 constant_dynamic-update-slice_fusion.2
  63.7 1.0 constant_dynamic-update-slice_fusion.1
  64.7 1.6 collective-permute-start.6
  67.5 1.3 collective-permute-done.6
  68.8 1.4 broadcast_select_fusion.1
  74.8 4.3 %all-to-all-start.2 = ((bf16[4,264,256]{2,1,0:T(8,128)(2,1)}), bf16[4,264,256]{2,1,0:T(8,128)(2,1)}, u32[]{:S(2)}, u32[]{:S(2)}) async-start(bf16[4,264,256]{2,1,0:T(8,128)(2,1)} %pad_maximum_fusion.2), calls=%async_computation.2 | async-start | bytes 1081344 | tf_op jit(solution)/shard_map/crossed_grad/all_to_all | solution.py:299
  79.0 1.5 collective-permute-start.10
  80.5 2.4 %collective-permute-start.9 = (f32[256]{0:T(256)S(1)}, f32[256]{0:T(256)S(1)}, u32[]{:S(2)}, u32[]{:S(2)}) collective-permute-start(f32[256]{0:T(256)S(1)} %get-tuple-element.29), channel_id=1, source_target_pairs={{0,2},{1,3},{2,0},{3,1},{4,6},{5,7},{6,4},{7,5},{8,10},{9,11},{10,... | collective-permute-start | bytes 3080 | tf_op jit(solution)/shard_map/stats/ppermute | solution.py:116
  82.9 1.2 collective-permute-start.8
  84.1 1.1 constant_dynamic-slice_fusion.5
  86.7 1.2 fusion.18
  88.4 3.1 %collective-permute-start.7 = (bf16[4,32,16,256]{3,2,1,0:T(8,128)(2,1)}, bf16[4,32,16,256]{3,2,1,0:T(8,128)(2,1)}, u32[]{:S(2)}, u32[]{:S(2)}) collective-permute-start(bf16[4,32,16,256]{3,2,1,0:T(8,128)(2,1)} %fusion.18), channel_id=1, source_target_pairs={{0,4},{4,0},{1,5},{5,1},{2,6},{6,2},{3,7},{7,3},{8,12},{12,8},{9,1... | collective-permute-start | bytes 3145736 | tf_op jit(solution)/shard_map/deep_grad/ppermute | solution.py:107
  93.3 4.9 %stats.1 = (bf16[32,80,256]{2,1,0:T(8,128)(2,1)S(1)}, bf16[32,80,256]{2,1,0:T(8,128)(2,1)S(1)}) custom-call(s32[1]{0:T(128)} %bitcast.22.core_ref, f32[64,1024]{1,0:T(8,128)S(1)} %bitcast.170, bf16[1024,256]{1,0:T(8,128)(2,1)S(1)} %pad_maximum_fusion.3.weights_ref, f32[64,256]{1,0:T(8,128)S(1)} %fusion.19.grads_ref), custom_call_target="tpu_custom_call" | custom-call | flops 1000 | bytes 1000 | tf_op jit(solution)/shard_map/stats/pallas_call | solution.py:96
  98.3 1.2 slice.153
  100.4 2.6 %fusion = bf16[4,32,16,256]{3,2,1,0:T(8,128)(2,1)} fusion(bf16[4,32,16,256]{3,2,1,0:T(8,128)(2,1)} %collective-permute-done.7, pred[]{:T(512)S(6)} %eq.70, bf16[4,32,2,16,256]{4,3,2,1,0:T(8,128)(2,1)S(1)} %copy-done.3), kind=kLoop, calls=%fused_computation.3 | loop fusion | flops 2621440 | bytes 4194305 | tf_op jit(solution)/shard_map/deep_grad/convert_element_type | solution.py:339
  103.0 1.0 fusion.25
  104.0 4.2 %all-to-all-start.3 = ((bf16[4,32,16,256]{3,2,1,0:T(8,128)(2,1)}), bf16[4,32,16,256]{3,2,1,0:T(8,128)(2,1)}, u32[]{:S(2)}, u32[]{:S(2)}) async-start(bf16[4,32,16,256]{3,2,1,0:T(8,128)(2,1)} %fusion), calls=%async_computation.3 | async-start | bytes 2097152 | tf_op jit(solution)/shard_map/deep_grad/all_to_all | solution.py:343
  108.6 1.4 constant_dynamic-update-slice_fusion.11
  110.9 1.4 constant_dynamic-update-slice_fusion.9
  113.6 1.0 collective-permute-start.13
  114.6 1.8 collective-permute-start.15
  116.4 1.2 collective-permute-start.14
  117.7 6.2 %collective-permute-done.13 = bf16[8,80,256]{2,1,0:T(8,128)(2,1)S(1)} collective-permute-done((bf16[8,80,256]{2,1,0:T(8,128)(2,1)S(1)}, bf16[8,80,256]{2,1,0:T(8,128)(2,1)S(1)}, u32[]{:S(2)}, u32[]{:S(2)}) %collective-permute-start.13) | collective-permute-done | bytes 327712 | tf_op jit(solution)/shard_map/stats_sum/ppermute | solution.py:116
  123.9 7.6 %collective-permute-done.14 = bf16[8,80,256]{2,1,0:T(8,128)(2,1)S(1)} collective-permute-done((bf16[8,80,256]{2,1,0:T(8,128)(2,1)S(1)}, bf16[8,80,256]{2,1,0:T(8,128)(2,1)S(1)}, u32[]{:S(2)}, u32[]{:S(2)}) %collective-permute-start.14) | collective-permute-done | bytes 327712 | tf_op jit(solution)/shard_map/stats_sum/ppermute | solution.py:116
  131.7 1.5 reduce_sum.135
  134.1 2.1 %collective-permute-start.19 = (bf16[8,40,256]{2,1,0:T(8,128)(2,1)S(1)}, bf16[8,40,256]{2,1,0:T(8,128)(2,1)S(1)}, u32[]{:S(2)}, u32[]{:S(2)}) collective-permute-start(bf16[8,40,256]{2,1,0:T(8,128)(2,1)S(1)} %get-tuple-element.108), channel_id=1, source_target_pairs={{0,24},{8,0},{16,8},{24,16},{1,25},{9,1},{17,9},{25,17},{2,26},{10... | collective-permute-start | bytes 491528 | tf_op jit(solution)/shard_map/grads_x/ppermute | solution.py:116
  136.2 3.0 %collective-permute-done.17 = bf16[8,40,256]{2,1,0:T(8,128)(2,1)S(1)} collective-permute-done((bf16[8,40,256]{2,1,0:T(8,128)(2,1)S(1)}, bf16[8,40,256]{2,1,0:T(8,128)(2,1)S(1)}, u32[]{:S(2)}, u32[]{:S(2)}) %collective-permute-start.17) | collective-permute-done | bytes 163872 | tf_op jit(solution)/shard_map/grads_x/ppermute | solution.py:116
  139.2 1.5 collective-permute-done.19
  140.7 3.0 %collective-permute-done.18 = bf16[8,40,256]{2,1,0:T(8,128)(2,1)S(1)} collective-permute-done((bf16[8,40,256]{2,1,0:T(8,128)(2,1)S(1)}, bf16[8,40,256]{2,1,0:T(8,128)(2,1)S(1)}, u32[]{:S(2)}, u32[]{:S(2)}) %collective-permute-start.18) | collective-permute-done | bytes 163872 | tf_op jit(solution)/shard_map/grads_x/ppermute | solution.py:116
  144.6 5.8 %all-to-all-start.4 = ((bf16[8,120,256]{2,1,0:T(8,128)(2,1)}), bf16[8,120,256]{2,1,0:T(8,128)(2,1)S(1)}, u32[]{:S(2)}, u32[]{:S(2)}) async-start(bf16[8,120,256]{2,1,0:T(8,128)(2,1)} %pad_maximum_fusion.4), calls=%async_computation.4 | async-start | bytes 983040 | tf_op jit(solution)/shard_map/sums_z/all_to_all | solution.py:384
  150.3 14.4 %all-to-all-done.4 = bf16[8,120,256]{2,1,0:T(8,128)(2,1)S(1)} async-done(((bf16[8,120,256]{2,1,0:T(8,128)(2,1)}), bf16[8,120,256]{2,1,0:T(8,128)(2,1)S(1)}, u32[]{:S(2)}, u32[]{:S(2)}) %all-to-all-start.4) | async-done | bytes 491552 | tf_op jit(solution)/shard_map/sums_z/all_to_all | solution.py:384
  167.3 16.0 %all_to_all.37 = f32[32,1,128]{2,1,0:T(1,128)S(1)} all-to-all(f32[32,1,128]{2,1,0:T(1,128)S(1)} %broadcast_in_dim.36), channel_id=1, replica_groups=mesh['z'=8,'x'=4,'c'=2,'mp'=4] {'x','c','mp'}, dimensions={0} | all-to-all | bytes 32768 | tf_op jit(solution)/shard_map/norm/all_to_all | solution.py:395
  183.8 3.3 %all-to-all-start.6 = ((f32[8,1,128]{2,1,0:T(1,128)}), f32[8,1,128]{2,1,0:T(1,128)S(1)}, u32[]{:S(2)}, u32[]{:S(2)}) async-start(f32[8,1,128]{2,1,0:T(1,128)} %broadcast_in_dim.37), calls=%async_computation.6 | async-start | bytes 8192 | tf_op jit(solution)/shard_map/norm/all_to_all | solution.py:397
  187.9 5.7 %all-to-all-done.6 = f32[8,1,128]{2,1,0:T(1,128)S(1)} async-done(((f32[8,1,128]{2,1,0:T(1,128)}), f32[8,1,128]{2,1,0:T(1,128)S(1)}, u32[]{:S(2)}, u32[]{:S(2)}) %all-to-all-start.6) | async-done | bytes 4128 | tf_op jit(solution)/shard_map/norm/all_to_all | solution.py:397
  (170 shorter events, 24.3 us)
Async XLA Ops:
  0.6 48.4 %copy-start = (f32[64,64]{1,0:T(8,128)S(1)}, f32[64,64]{1,0:T(8,128)}, u32[]{:S(2)}) copy-start(f32[64,64]{1,0:T(8,128)} %param.26) | copy-start | bytes 49156
  1.4 14.4 %copy-start.12 = (s32[1024,8]{0,1:T(8,128)S(1)}, s32[1024,8]{0,1:T(8,128)}, u32[]{:S(2)}) copy-start(s32[1024,8]{0,1:T(8,128)} %param.15) | copy-start | bytes 98308
  2.5 13.5 %copy-start.1 = (bf16[4096,256]{1,0:T(8,128)(2,1)S(1)}, bf16[4096,256]{1,0:T(8,128)(2,1)}, u32[]{:S(2)}) copy-start(bf16[4096,256]{1,0:T(8,128)(2,1)} %table_ref.1) | copy-start | bytes 6291460
  2.5 41.2 %all-to-all-start = ((bf16[64,32,256]{2,1,0:T(8,128)(2,1)}), bf16[64,32,256]{2,1,0:T(8,128)(2,1)}, u32[]{:S(2)}, u32[]{:S(2)}) async-start(bf16[64,32,256]{2,1,0:T(8,128)(2,1)} %broadcast_in_dim.28), calls=%async_computation | async-start | bytes 2097152 | tf_op jit(solution)/shard_map/weights_dp/all_to_all | solution.py:112
  16.0 13.6 %copy-start.11 = (s32[1024]{0:T(1024)S(1)}, s32[1024]{0:T(1024)}, u32[]{:S(2)}) copy-start(s32[1024]{0:T(1024)} %param.19) | copy-start | bytes 12292
  16.0 13.7 %copy-start.19 = (f32[256]{0:T(256)S(1)}, f32[256]{0:T(256)}, u32[]{:S(2)}) copy-start(f32[256]{0:T(256)} %param.25) | copy-start | bytes 3076
  16.0 13.7 %copy-start.20 = (f32[256]{0:T(256)S(1)}, f32[256]{0:T(256)}, u32[]{:S(2)}) copy-start(f32[256]{0:T(256)} %param.24) | copy-start | bytes 3076
  24.6 26.9 %collective-permute-start.2 = (bf16[1024,256]{1,0:T(8,128)(2,1)S(1)}, bf16[1024,256]{1,0:T(8,128)(2,1)S(1)}, u32[]{:S(2)}, u32[]{:S(2)}) collective-permute-start(bf16[1024,256]{1,0:T(8,128)(2,1)S(1)} %embed.1), channel_id=1, source_target_pairs={{0,1},{1,2},{2,3},{3,0},{4,5},{5,6},{6,7},{7,4},{8,9},{9,10},{10,1... | collective-permute-start | bytes 1572872 | tf_op jit(solution)/shard_map/base_mp/ppermute | solution.py:116
  25.9 27.0 %collective-permute-start.1 = (bf16[1024,256]{1,0:T(8,128)(2,1)S(1)}, bf16[1024,256]{1,0:T(8,128)(2,1)}, u32[]{:S(2)}, u32[]{:S(2)}) collective-permute-start(bf16[1024,256]{1,0:T(8,128)(2,1)S(1)} %embed.1), channel_id=1, source_target_pairs={{0,2},{1,3},{2,0},{3,1},{4,6},{5,7},{6,4},{7,5},{8,10},{9,11},{10,... | collective-permute-start | bytes 1572872 | tf_op jit(solution)/shard_map/base_mp/ppermute | solution.py:116
  28.5 26.0 %collective-permute-start = (bf16[1024,256]{1,0:T(8,128)(2,1)S(1)}, bf16[1024,256]{1,0:T(8,128)(2,1)S(1)}, u32[]{:S(2)}, u32[]{:S(2)}) collective-permute-start(bf16[1024,256]{1,0:T(8,128)(2,1)S(1)} %embed.1), channel_id=1, source_target_pairs={{0,3},{1,0},{2,1},{3,2},{4,7},{5,4},{6,5},{7,6},{8,11},{9,8},{10,9... | collective-permute-start | bytes 1572872 | tf_op jit(solution)/shard_map/base_mp/ppermute | solution.py:116
  29.7 19.3 %copy-start.18 = (s32[1024]{0:T(1024)S(1)}, s32[1024]{0:T(1024)}, u32[]{:S(2)}) copy-start(s32[1024]{0:T(1024)} %param.16) | copy-start | bytes 12292
  29.7 19.3 %copy-start.16 = (s32[1024]{0:T(1024)S(1)}, s32[1024]{0:T(1024)}, u32[]{:S(2)}) copy-start(s32[1024]{0:T(1024)} %param.17) | copy-start | bytes 12292
  29.7 19.9 %copy-start.13 = (f32[64,64]{1,0:T(8,128)S(1)}, f32[64,64]{1,0:T(8,128)}, u32[]{:S(2)}) copy-start(f32[64,64]{1,0:T(8,128)} %param.27) | copy-start | bytes 49156
  29.8 19.9 %copy-start.17 = (s32[1024]{0:T(1024)S(1)}, s32[1024]{0:T(1024)}, u32[]{:S(2)}) copy-start(s32[1024]{0:T(1024)} %param.18) | copy-start | bytes 12292
  29.8 20.5 %copy-start.14 = (f32[128,64]{0,1:T(8,128)S(1)}, f32[128,64]{0,1:T(8,128)}, u32[]{:S(2)}) copy-start(f32[128,64]{0,1:T(8,128)} %param.28) | copy-start | bytes 98308
  45.0 5.8 %copy-start.15 = (f32[128,64]{0,1:T(8,128)S(1)}, f32[128,64]{0,1:T(8,128)}, u32[]{:S(2)}) copy-start(f32[128,64]{0,1:T(8,128)} %param.29) | copy-start | bytes 98308
  45.0 14.8 %collective-permute-start.5 = (bf16[512,256]{1,0:T(8,128)(2,1)S(1)}, bf16[512,256]{1,0:T(8,128)(2,1)S(1)}, u32[]{:S(2)}, u32[]{:S(2)}) collective-permute-start(bf16[512,256]{1,0:T(8,128)(2,1)S(1)} %constant_dynamic-slice_fusion.6), channel_id=1, source_target_pairs={{0,1},{1,2},{2,3},{3,0},{4,5},{5,6},{6,7},{7,4},{8,9},{9,10},{10,1... | collective-permute-start | bytes 786440 | tf_op jit(solution)/shard_map/deep_weight_mp/ppermute | solution.py:116
  46.4 16.3 %collective-permute-start.4 = (bf16[512,256]{1,0:T(8,128)(2,1)S(1)}, bf16[512,256]{1,0:T(8,128)(2,1)}, u32[]{:S(2)}, u32[]{:S(2)}) collective-permute-start(bf16[512,256]{1,0:T(8,128)(2,1)S(1)} %constant_dynamic-slice_fusion.6), channel_id=1, source_target_pairs={{0,2},{1,3},{2,0},{3,1},{4,6},{5,7},{6,4},{7,5},{8,10},{9,11},{10,... | collective-permute-start | bytes 786440 | tf_op jit(solution)/shard_map/deep_weight_mp/ppermute | solution.py:116
  51.4 2.8 %copy-start.6 = (bf16[1024,256]{1,0:T(8,128)(2,1)}, bf16[1024,256]{1,0:T(8,128)(2,1)S(1)}, u32[]{:S(2)}) copy-start(bf16[1024,256]{1,0:T(8,128)(2,1)S(1)} %collective-permute-done.2) | copy-start | bytes 1572868
  51.5 11.2 %collective-permute-start.3 = (bf16[512,256]{1,0:T(8,128)(2,1)S(1)}, bf16[512,256]{1,0:T(8,128)(2,1)}, u32[]{:S(2)}, u32[]{:S(2)}) collective-permute-start(bf16[512,256]{1,0:T(8,128)(2,1)S(1)} %constant_dynamic-slice_fusion.6), channel_id=1, source_target_pairs={{0,3},{1,0},{2,1},{3,2},{4,7},{5,4},{6,5},{7,6},{8,11},{9,8},{10,9... | collective-permute-start | bytes 786440 | tf_op jit(solution)/shard_map/deep_weight_mp/ppermute | solution.py:116
  52.6 1.7 copy-start.21
  54.6 0.8 copy-start.4
  56.3 10.8 %all-to-all-start.1 = ((bf16[4,272,256]{2,1,0:T(8,128)(2,1)}), bf16[4,272,256]{2,1,0:T(8,128)(2,1)S(1)}, u32[]{:S(2)}, u32[]{:S(2)}) async-start(bf16[4,272,256]{2,1,0:T(8,128)(2,1)} %pad_maximum_fusion.1), calls=%async_computation.1 | async-start | bytes 1114112 | tf_op jit(solution)/shard_map/crossed_mp/all_to_all | solution.py:249
  59.8 2.9 %copy-start.9 = (bf16[512,256]{1,0:T(8,128)(2,1)}, bf16[512,256]{1,0:T(8,128)(2,1)S(1)}, u32[]{:S(2)}) copy-start(bf16[512,256]{1,0:T(8,128)(2,1)S(1)} %collective-permute-done.5) | copy-start | bytes 786436
  62.7 2.0 %copy-start.10 = (bf16[512,256]{1,0:T(8,128)(2,1)S(1)}, bf16[512,256]{1,0:T(8,128)(2,1)}, u32[]{:S(2)}) copy-start(bf16[512,256]{1,0:T(8,128)(2,1)} %copy-done.9) | copy-start | bytes 786436
  64.7 4.1 %collective-permute-start.6 = (bf16[512,1024]{1,0:T(8,128)(2,1)S(1)}, bf16[512,1024]{1,0:T(8,128)(2,1)}, u32[]{:S(2)}, u32[]{:S(2)}) collective-permute-start(bf16[512,1024]{1,0:T(8,128)(2,1)S(1)} %constant_dynamic-update-slice_fusion), channel_id=1, source_target_pairs={{0,4},{4,0},{1,5},{5,1},{2,6},{6,2},{3,7},{7,3},{8,12},{12,8},{9,1... | collective-permute-start | bytes 3145736 | tf_op jit(solution)/shard_map/deep_weight_core/ppermute | solution.py:107
  74.8 23.5 %all-to-all-start.2 = ((bf16[4,264,256]{2,1,0:T(8,128)(2,1)}), bf16[4,264,256]{2,1,0:T(8,128)(2,1)}, u32[]{:S(2)}, u32[]{:S(2)}) async-start(bf16[4,264,256]{2,1,0:T(8,128)(2,1)} %pad_maximum_fusion.2), calls=%async_computation.2 | async-start | bytes 1081344 | tf_op jit(solution)/shard_map/crossed_grad/all_to_all | solution.py:299
  79.0 12.5 %collective-permute-start.10 = (f32[256]{0:T(256)S(1)}, f32[256]{0:T(256)S(1)}, u32[]{:S(2)}, u32[]{:S(2)}) collective-permute-start(f32[256]{0:T(256)S(1)} %get-tuple-element.29), channel_id=1, source_target_pairs={{0,1},{1,2},{2,3},{3,0},{4,5},{5,6},{6,7},{7,4},{8,9},{9,10},{10,1... | collective-permute-start | bytes 3080 | tf_op jit(solution)/shard_map/stats/ppermute | solution.py:116
  80.5 11.0 %collective-permute-start.9 = (f32[256]{0:T(256)S(1)}, f32[256]{0:T(256)S(1)}, u32[]{:S(2)}, u32[]{:S(2)}) collective-permute-start(f32[256]{0:T(256)S(1)} %get-tuple-element.29), channel_id=1, source_target_pairs={{0,2},{1,3},{2,0},{3,1},{4,6},{5,7},{6,4},{7,5},{8,10},{9,11},{10,... | collective-permute-start | bytes 3080 | tf_op jit(solution)/shard_map/stats/ppermute | solution.py:116
  82.9 8.6 %collective-permute-start.8 = (f32[256]{0:T(256)S(1)}, f32[256]{0:T(256)S(1)}, u32[]{:S(2)}, u32[]{:S(2)}) collective-permute-start(f32[256]{0:T(256)S(1)} %get-tuple-element.29), channel_id=1, source_target_pairs={{0,3},{1,0},{2,1},{3,2},{4,7},{5,4},{6,5},{7,6},{8,11},{9,8},{10,9... | collective-permute-start | bytes 3080 | tf_op jit(solution)/shard_map/stats/ppermute | solution.py:116
  86.7 1.8 copy-start.2
  88.4 11.9 %collective-permute-start.7 = (bf16[4,32,16,256]{3,2,1,0:T(8,128)(2,1)}, bf16[4,32,16,256]{3,2,1,0:T(8,128)(2,1)}, u32[]{:S(2)}, u32[]{:S(2)}) collective-permute-start(bf16[4,32,16,256]{3,2,1,0:T(8,128)(2,1)} %fusion.18), channel_id=1, source_target_pairs={{0,4},{4,0},{1,5},{5,1},{2,6},{6,2},{3,7},{7,3},{8,12},{12,8},{9,1... | collective-permute-start | bytes 3145736 | tf_op jit(solution)/shard_map/deep_grad/ppermute | solution.py:107
  98.2 2.1 %copy-start.3 = (bf16[4,32,2,16,256]{4,3,2,1,0:T(8,128)(2,1)S(1)}, bf16[4,32,2,16,256]{4,3,2,1,0:T(8,128)(2,1)}, u32[]{:S(2)}) copy-start(bf16[4,32,2,16,256]{4,3,2,1,0:T(8,128)(2,1)} %copy-done.2) | copy-start | bytes 6291460
  104.0 27.7 %all-to-all-start.3 = ((bf16[4,32,16,256]{3,2,1,0:T(8,128)(2,1)}), bf16[4,32,16,256]{3,2,1,0:T(8,128)(2,1)}, u32[]{:S(2)}, u32[]{:S(2)}) async-start(bf16[4,32,16,256]{3,2,1,0:T(8,128)(2,1)} %fusion), calls=%async_computation.3 | async-start | bytes 2097152 | tf_op jit(solution)/shard_map/deep_grad/all_to_all | solution.py:343
  108.2 2.3 %copy-start.5 = (bf16[1024,256]{1,0:T(8,128)(2,1)S(1)}, bf16[1024,256]{1,0:T(8,128)(2,1)}, u32[]{:S(2)}) copy-start(bf16[1024,256]{1,0:T(8,128)(2,1)} %copy-done.4) | copy-start | bytes 1572868
  108.2 2.3 %copy-start.8 = (bf16[1024,256]{1,0:T(8,128)(2,1)S(1)}, bf16[1024,256]{1,0:T(8,128)(2,1)}, u32[]{:S(2)}) copy-start(bf16[1024,256]{1,0:T(8,128)(2,1)} %get-tuple-element.100) | copy-start | bytes 1572868
  108.2 9.3 %collective-permute-start.16 = (f32[3,256]{1,0:T(4,128)S(1)}, f32[3,256]{1,0:T(4,128)S(1)}, u32[]{:S(2)}, u32[]{:S(2)}) collective-permute-start(f32[3,256]{1,0:T(4,128)S(1)} %pad_maximum_fusion.7), channel_id=1, source_target_pairs={{0,4},{4,0},{1,5},{5,1},{2,6},{6,2},{3,7},{7,3},{8,12},{12,8},{9,1... | collective-permute-start | bytes 9224 | tf_op jit(solution)/shard_map/cross_grad/ppermute | solution.py:107
  109.9 3.2 %collective-permute-start.12 = (bf16[32,80,256]{2,1,0:T(8,128)(2,1)S(1)}, bf16[32,80,256]{2,1,0:T(8,128)(2,1)S(1)}, u32[]{:S(2)}, u32[]{:S(2)}) collective-permute-start(bf16[32,80,256]{2,1,0:T(8,128)(2,1)S(1)} %get-tuple-element.34), channel_id=1, source_target_pairs={{0,4},{4,0},{1,5},{5,1},{2,6},{6,2},{3,7},{7,3},{8,12},{12,8},{9,1... | collective-permute-start | bytes 3932168 | tf_op jit(solution)/shard_map/stats_sum/ppermute | solution.py:107
  110.5 1.8 copy-start.7
  112.8 4.7 %collective-permute-start.11 = (bf16[32,16,256]{2,1,0:T(8,128)(2,1)S(1)}, bf16[32,16,256]{2,1,0:T(8,128)(2,1)S(1)}, u32[]{:S(2)}, u32[]{:S(2)}) collective-permute-start(bf16[32,16,256]{2,1,0:T(8,128)(2,1)S(1)} %fusion.40), channel_id=1, source_target_pairs={{0,4},{4,0},{1,5},{5,1},{2,6},{6,2},{3,7},{7,3},{8,12},{12,8},{9,1... | collective-permute-start | bytes 786440 | tf_op jit(solution)/shard_map/cross_grad/ppermute | solution.py:107
  113.6 10.3 %collective-permute-start.13 = (bf16[8,80,256]{2,1,0:T(8,128)(2,1)S(1)}, bf16[8,80,256]{2,1,0:T(8,128)(2,1)S(1)}, u32[]{:S(2)}, u32[]{:S(2)}) collective-permute-start(bf16[8,80,256]{2,1,0:T(8,128)(2,1)S(1)} %get-tuple-element.102), channel_id=1, source_target_pairs={{0,8},{8,16},{16,24},{24,0},{1,9},{9,17},{17,25},{25,1},{2,10},{10... | collective-permute-start | bytes 983048 | tf_op jit(solution)/shard_map/stats_sum/ppermute | solution.py:116
  114.6 9.3 %collective-permute-start.15 = (bf16[8,80,256]{2,1,0:T(8,128)(2,1)S(1)}, bf16[8,80,256]{2,1,0:T(8,128)(2,1)S(1)}, u32[]{:S(2)}, u32[]{:S(2)}) collective-permute-start(bf16[8,80,256]{2,1,0:T(8,128)(2,1)S(1)} %get-tuple-element.103), channel_id=1, source_target_pairs={{0,24},{8,0},{16,8},{24,16},{1,25},{9,1},{17,9},{25,17},{2,26},{10... | collective-permute-start | bytes 983048 | tf_op jit(solution)/shard_map/stats_sum/ppermute | solution.py:116
  116.4 15.1 %collective-permute-start.14 = (bf16[8,80,256]{2,1,0:T(8,128)(2,1)S(1)}, bf16[8,80,256]{2,1,0:T(8,128)(2,1)S(1)}, u32[]{:S(2)}, u32[]{:S(2)}) collective-permute-start(bf16[8,80,256]{2,1,0:T(8,128)(2,1)S(1)} %get-tuple-element.104), channel_id=1, source_target_pairs={{0,16},{8,24},{16,0},{24,8},{1,17},{9,25},{17,1},{25,9},{2,18},{10... | collective-permute-start | bytes 983048 | tf_op jit(solution)/shard_map/stats_sum/ppermute | solution.py:116
  133.4 5.8 %collective-permute-start.17 = (bf16[8,40,256]{2,1,0:T(8,128)(2,1)S(1)}, bf16[8,40,256]{2,1,0:T(8,128)(2,1)S(1)}, u32[]{:S(2)}, u32[]{:S(2)}) collective-permute-start(bf16[8,40,256]{2,1,0:T(8,128)(2,1)S(1)} %get-tuple-element.107), channel_id=1, source_target_pairs={{0,8},{8,16},{16,24},{24,0},{1,9},{9,17},{17,25},{25,1},{2,10},{10... | collective-permute-start | bytes 491528 | tf_op jit(solution)/shard_map/grads_x/ppermute | solution.py:116
  134.1 6.6 %collective-permute-start.19 = (bf16[8,40,256]{2,1,0:T(8,128)(2,1)S(1)}, bf16[8,40,256]{2,1,0:T(8,128)(2,1)S(1)}, u32[]{:S(2)}, u32[]{:S(2)}) collective-permute-start(bf16[8,40,256]{2,1,0:T(8,128)(2,1)S(1)} %get-tuple-element.108), channel_id=1, source_target_pairs={{0,24},{8,0},{16,8},{24,16},{1,25},{9,1},{17,9},{25,17},{2,26},{10... | collective-permute-start | bytes 491528 | tf_op jit(solution)/shard_map/grads_x/ppermute | solution.py:116
  136.2 7.4 %collective-permute-start.18 = (bf16[8,40,256]{2,1,0:T(8,128)(2,1)S(1)}, bf16[8,40,256]{2,1,0:T(8,128)(2,1)S(1)}, u32[]{:S(2)}, u32[]{:S(2)}) collective-permute-start(bf16[8,40,256]{2,1,0:T(8,128)(2,1)S(1)} %get-tuple-element.109), channel_id=1, source_target_pairs={{0,16},{8,24},{16,0},{24,8},{1,17},{9,25},{17,1},{25,9},{2,18},{10... | collective-permute-start | bytes 491528 | tf_op jit(solution)/shard_map/grads_x/ppermute | solution.py:116
  144.6 20.1 %all-to-all-start.4 = ((bf16[8,120,256]{2,1,0:T(8,128)(2,1)}), bf16[8,120,256]{2,1,0:T(8,128)(2,1)S(1)}, u32[]{:S(2)}, u32[]{:S(2)}) async-start(bf16[8,120,256]{2,1,0:T(8,128)(2,1)} %pad_maximum_fusion.4), calls=%async_computation.4 | async-start | bytes 983040 | tf_op jit(solution)/shard_map/sums_z/all_to_all | solution.py:384
  183.8 9.7 %all-to-all-start.6 = ((f32[8,1,128]{2,1,0:T(1,128)}), f32[8,1,128]{2,1,0:T(1,128)S(1)}, u32[]{:S(2)}, u32[]{:S(2)}) async-start(f32[8,1,128]{2,1,0:T(1,128)} %broadcast_in_dim.37), calls=%async_computation.6 | async-start | bytes 8192 | tf_op jit(solution)/shard_map/norm/all_to_all | solution.py:397

commit v3 on v2

--- a/solution.py
+++ b/solution.py
@@ -337,17 +337,18 @@
         deep_keep = by_core(core, deep_part[:, :, 0], deep_part[:, :, 1])
         deep_send = by_core(core, deep_part[:, :, 1], deep_part[:, :, 0])
         deep_pair = (deep_keep.astype(F32) + swap(deep_send).astype(F32)).astype(BF16)
-        deep_pair, stats_send, crossed_back = lax.optimization_barrier(
-            (deep_pair, stats_send, crossed_back)
-        )
         deep_sum = lax.all_to_all(deep_pair, "mp", 0, 0, tiled=True)
     with jax.named_scope("stats_sum"):
         stats_pair = (stats_keep.astype(F32) + swap(stats_send).astype(F32)).astype(BF16)
-        stats_pair = stats_pair.reshape(n_z, n_x, feats + 16, 2 * ctx_count)
-        stats_x = scatter_ahead(
-            [block_ahead(stats_pair, my_x, t, 1) for t in range(n_x)], "x"
-        ).astype(BF16)
-        deep_sum, stats_x = lax.optimization_barrier((deep_sum, stats_x))
+        stats_pair = stats_pair[:, : feats + 8].reshape(n_z, n_x, feats + 8, 2 * ctx_count)
+        crossed_back = after(crossed_back, stats_pair, deep_pair)
+        stats_parts = [block_ahead(stats_pair, my_x, t, 1) for t in range(n_x)]
+        stats_parts = stats_parts[:1] + [
+            shift(stats_parts[t], "x", n_x, t) for t in range(1, n_x)
+        ]
+        deep_sum, stats_parts[1], stats_parts[-1] = lax.optimization_barrier(
+            (deep_sum, stats_parts[1], stats_parts[-1])
+        )
         deep_sum = jnp.sum(deep_sum.astype(F32), axis=0).astype(BF16)
 
     with jax.named_scope("cross_grad"):
@@ -381,6 +382,7 @@
             [block_ahead(message, my_x, t, 1) for t in range(n_x)], "x"
         ).astype(BF16)
     with jax.named_scope("sums_z"):
+        stats_x = sum(p.astype(F32) for p in stats_parts).astype(BF16)
         got = lax.all_to_all(jnp.concatenate([grads_x, stats_x], axis=1), "z", 0, 0, tiled=True)
         got_sum = jnp.sum(got.astype(F32), axis=0)
         matrix_shards = got_sum[: 2 * depth]

time: 196 us -> 192 us (0.980)
  waiting for transfers between devices: 60.4 us -> 46.7 us
  blocking collectives: 16 us -> 24.2 us
  other arithmetic: 17.3 us -> 19.8 us
    ppermute x15, waiting for transfers between devices: 24.1 us -> 13.6 us  [shift(): lax.ppermute(value, axis, [(i, (i + ahead) % count) for i in range(count)])]
    all_to_all x1, blocking collectives: 16 us -> 24.2 us  [shards(): squares = lax.all_to_all(squares, ('x', 'c', 'mp'), 0, 0, tiled=True)]
    all_to_all x1, waiting for transfers between devices: 14.4 us -> 11.4 us  [shards(): lax.all_to_all(jnp.concatenate([grads_x, stats_x], axis=1), 'z', 0, 0, ti...]
    unnamed x58 -> x54, local copies, waits for them, and re-layouts: 4.14 us -> 4.46 us
  transfers between devices with their start and end apart: 26 -> 26, of which waited for: 12 -> 9; matrix products, arithmetic and copies ran while one was open for 11% -> 16% of each run, Pallas kernels for 7% -> 7%
where the time goes in v3:
time: 192 us; the launch traced here: 191 us
  starting transfers between devices  61 us (32%)
  waiting for transfers between devices  46.7 us (24%)
  blocking collectives  24.2 us (13%)
  other arithmetic  19.8 us (10%)
  Pallas kernels  13.4 us (7%)
  local copies, waits for them, and re-layouts  11.6 us (6%)
  matrix products  11.4 us (6%)
  between operations  3 us (2%)
    all_to_all x1, blocking collectives, shards(): squares = lax.all_to_all(squares, ('x', 'c', 'mp'), 0, 0, tiled=True)  24.2 us
    ppermute x15, starting transfers between devices, shift(): lax.ppermute(value, axis, [(i, (i + ahead) % count) for i in range(count)])  21.7 us
    all_to_all x1, waiting for transfers between devices, gather(): return lax.all_to_all(wide, axes, 0, 0, tiled=True)  14 us
    ppermute x15, waiting for transfers between devices, shift(): lax.ppermute(value, axis, [(i, (i + ahead) % count) for i in range(count)])  13.6 us
    all_to_all x1, starting transfers between devices, gather(): return lax.all_to_all(wide, axes, 0, 0, tiled=True)  13.3 us
    all_to_all x1, waiting for transfers between devices, shards(): lax.all_to_all(jnp.concatenate([grads_x, stats_x], axis=1), 'z', 0, 0, ti...  11.4 us
    pallas_call x1, Pallas kernels, embed(): pl.pallas_call(embed_kernel, out_shape=jax.ShapeDtypeStruct((rows, table....  8.49 us
    all_to_all x1, starting transfers between devices, shards(): lax.all_to_all(jnp.concatenate([grads_x, stats_x], axis=1), 'z', 0, 0, ti...  6.49 us
  transfers between devices with their start and end apart: 26, of which 9 were waited for; matrix products, arithmetic and copies ran while one was open for 16% of the time, Pallas kernels for 7%

profile of v3, /device:TPU:1, one launch (start us, length us, event | category | flops | bytes accessed | tf_op | source)
XLA Modules:
  0.0 191.2 jit_solution(16633747142108960353)
XLA Ops:
  1.4 1.1 broadcast_in_dim.28
  2.5 13.3 %all-to-all-start = ((bf16[64,32,256]{2,1,0:T(8,128)(2,1)}), bf16[64,32,256]{2,1,0:T(8,128)(2,1)}, u32[]{:S(2)}, u32[]{:S(2)}) async-start(bf16[64,32,256]{2,1,0:T(8,128)(2,1)} %broadcast_in_dim.28), calls=%async_computation | async-start | bytes 2097152 | tf_op jit(solution)/shard_map/weights_dp/all_to_all | solution.py:112
  16.0 8.5 %embed.1 = bf16[1024,256]{1,0:T(8,128)(2,1)S(1)} custom-call(s32[1024,8]{1,0:T(8,128)S(1)} %copy.139.ids_ref, bf16[4096,256]{1,0:T(8,128)(2,1)S(1)} %copy-done.1), custom_call_target="tpu_custom_call" | custom-call | tf_op jit(solution)/shard_map/embed/pallas_call | solution.py:59
  24.5 1.4 collective-permute-start.2
  25.9 2.6 %collective-permute-start.1 = (bf16[1024,256]{1,0:T(8,128)(2,1)S(1)}, bf16[1024,256]{1,0:T(8,128)(2,1)}, u32[]{:S(2)}, u32[]{:S(2)}) collective-permute-start(bf16[1024,256]{1,0:T(8,128)(2,1)S(1)} %embed.1), channel_id=1, source_target_pairs={{0,2},{1,3},{2,0},{3,1},{4,6},{5,7},{6,4},{7,5},{8,10},{9,11},{10,... | collective-permute-start | bytes 1572872 | tf_op jit(solution)/shard_map/base_mp/ppermute | solution.py:116
  28.5 1.1 collective-permute-start
  29.7 14.0 %all-to-all-done = bf16[64,32,256]{2,1,0:T(8,128)(2,1)} async-done(((bf16[64,32,256]{2,1,0:T(8,128)(2,1)}), bf16[64,32,256]{2,1,0:T(8,128)(2,1)}, u32[]{:S(2)}, u32[]{:S(2)}) %all-to-all-start) | async-done | bytes 1048608 | tf_op jit(solution)/shard_map/weights_dp/all_to_all | solution.py:112
  43.7 1.3 fusion.86
  45.0 2.8 %collective-permute-start.3 = (bf16[512,256]{1,0:T(8,128)(2,1)S(1)}, bf16[512,256]{1,0:T(8,128)(2,1)}, u32[]{:S(2)}, u32[]{:S(2)}) collective-permute-start(bf16[512,256]{1,0:T(8,128)(2,1)S(1)} %constant_dynamic-slice_fusion.6), channel_id=1, source_target_pairs={{0,3},{1,0},{2,1},{3,2},{4,7},{5,4},{6,5},{7,6},{8,11},{9,8},{10,9... | collective-permute-start | bytes 786440 | tf_op jit(solution)/shard_map/deep_weight_mp/ppermute | solution.py:116
  51.7 1.3 fusion.51
  54.3 0.8 pad_maximum_fusion.1
  55.1 3.5 %all-to-all-start.1 = ((bf16[4,272,256]{2,1,0:T(8,128)(2,1)}), bf16[4,272,256]{2,1,0:T(8,128)(2,1)S(1)}, u32[]{:S(2)}, u32[]{:S(2)}) async-start(bf16[4,272,256]{2,1,0:T(8,128)(2,1)} %pad_maximum_fusion.1), calls=%async_computation.1 | async-start | bytes 1114112 | tf_op jit(solution)/shard_map/crossed_mp/all_to_all | solution.py:249
  58.6 4.3 %collective-permute-done.5 = bf16[512,256]{1,0:T(8,128)(2,1)} collective-permute-done((bf16[512,256]{1,0:T(8,128)(2,1)S(1)}, bf16[512,256]{1,0:T(8,128)(2,1)}, u32[]{:S(2)}, u32[]{:S(2)}) %collective-permute-start.5) | collective-permute-done | bytes 262176 | tf_op jit(solution)/shard_map/deep_weight_mp/ppermute | solution.py:116
  63.0 1.0 constant_dynamic-update-slice_fusion.2
  64.0 1.0 constant_dynamic-update-slice_fusion.1
  65.0 1.0 constant_dynamic-update-slice_fusion
  66.0 1.9 collective-permute-start.6
  68.2 2.0 %collective-permute-done.6 = bf16[512,1024]{1,0:T(8,128)(2,1)} collective-permute-done((bf16[512,1024]{1,0:T(8,128)(2,1)S(1)}, bf16[512,1024]{1,0:T(8,128)(2,1)}, u32[]{:S(2)}, u32[]{:S(2)}) %collective-permute-start.6) | collective-permute-done | bytes 1048608 | tf_op jit(solution)/shard_map/deep_weight_core/ppermute | solution.py:107
  70.2 1.4 broadcast_select_fusion.1
  75.8 2.5 %collective-permute-start.7 = (f32[256]{0:T(256)S(1)}, f32[256]{0:T(256)S(1)}, u32[]{:S(2)}, u32[]{:S(2)}) collective-permute-start(f32[256]{0:T(256)S(1)} %get-tuple-element.28), channel_id=1, source_target_pairs={{0,3},{1,0},{2,1},{3,2},{4,7},{5,4},{6,5},{7,6},{8,11},{9,8},{10,9... | collective-permute-start | bytes 3080 | tf_op jit(solution)/shard_map/stats/ppermute | solution.py:116
  78.3 1.7 collective-permute-start.8
  79.9 4.2 %all-to-all-start.2 = ((bf16[4,264,256]{2,1,0:T(8,128)(2,1)}), bf16[4,264,256]{2,1,0:T(8,128)(2,1)}, u32[]{:S(2)}, u32[]{:S(2)}) async-start(bf16[4,264,256]{2,1,0:T(8,128)(2,1)} %pad_maximum_fusion.2), calls=%async_computation.2 | async-start | bytes 1081344 | tf_op jit(solution)/shard_map/crossed_grad/all_to_all | solution.py:299
  84.5 1.1 constant_dynamic-slice_fusion.4
  87.1 1.2 fusion.18
  88.7 1.3 collective-permute-start.11
  91.8 4.9 %stats.1 = (bf16[32,80,256]{2,1,0:T(8,128)(2,1)S(1)}, bf16[32,80,256]{2,1,0:T(8,128)(2,1)S(1)}) custom-call(s32[1]{0:T(128)} %bitcast.15.core_ref, f32[64,1024]{1,0:T(8,128)S(1)} %bitcast.170, bf16[1024,256]{1,0:T(8,128)(2,1)S(1)} %pad_maximum_fusion.3.weights_ref, f32[64,256]{1,0:T(8,128)S(1)} %fusion.19.grads_ref), custom_call_target="tpu_custom_call" | custom-call | flops 1000 | bytes 1000 | tf_op jit(solution)/shard_map/stats/pallas_call | solution.py:96
  97.0 1.2 slice.155
  98.9 1.1 bitcast_convert_fusion
  100.1 2.6 %fusion = bf16[4,32,16,256]{3,2,1,0:T(8,128)(2,1)} fusion(bf16[4,32,16,256]{3,2,1,0:T(8,128)(2,1)} %collective-permute-done.11, pred[]{:T(512)S(6)} %eq.70, bf16[4,32,2,16,256]{4,3,2,1,0:T(8,128)(2,1)S(1)} %copy-done.3), kind=kLoop, calls=%fused_computation.3 | loop fusion | flops 2621440 | bytes 4194305 | tf_op jit(solution)/shard_map/deep_grad/convert_element_type | solution.py:339
  102.7 4.5 %all-to-all-start.3 = ((bf16[4,32,16,256]{3,2,1,0:T(8,128)(2,1)}), bf16[4,32,16,256]{3,2,1,0:T(8,128)(2,1)}, u32[]{:S(2)}, u32[]{:S(2)}) async-start(bf16[4,32,16,256]{3,2,1,0:T(8,128)(2,1)} %fusion), calls=%async_computation.3 | async-start | bytes 2097152 | tf_op jit(solution)/shard_map/deep_grad/all_to_all | solution.py:340
  107.2 1.7 add_convert_fusion
  110.3 1.4 constant_dynamic-update-slice_fusion.9
  113.2 1.3 collective-permute-start.13
  114.5 1.5 collective-permute-start.14
  116.0 1.5 collective-permute-start.19
  117.6 5.2 %collective-permute-done.13 = bf16[8,72,256]{2,1,0:T(8,128)(2,1)S(1)} collective-permute-done((bf16[8,72,256]{2,1,0:T(8,128)(2,1)S(1)}, bf16[8,72,256]{2,1,0:T(8,128)(2,1)S(1)}, u32[]{:S(2)}, u32[]{:S(2)}) %collective-permute-start.13) | collective-permute-done | bytes 294944 | tf_op jit(solution)/shard_map/stats_sum/ppermute | solution.py:116
  122.8 1.5 reduce_sum.135
  124.6 0.9 collective-permute-start.16
  125.5 2.9 %collective-permute-start.17 = (bf16[8,40,256]{2,1,0:T(8,128)(2,1)S(1)}, bf16[8,40,256]{2,1,0:T(8,128)(2,1)S(1)}, u32[]{:S(2)}, u32[]{:S(2)}) collective-permute-start(bf16[8,40,256]{2,1,0:T(8,128)(2,1)S(1)} %get-tuple-element.107), channel_id=1, source_target_pairs={{0,16},{8,24},{16,0},{24,8},{1,17},{9,25},{17,1},{25,9},{2,18},{10... | collective-permute-start | bytes 491528 | tf_op jit(solution)/shard_map/grads_x/ppermute | solution.py:116
  128.9 1.2 collective-permute-done.19
  130.1 1.1 fusion.28
  131.2 1.1 collective-permute-done.16
  132.3 1.8 collective-permute-done.17
  134.9 6.5 %all-to-all-start.4 = ((bf16[8,112,256]{2,1,0:T(8,128)(2,1)}), bf16[8,112,256]{2,1,0:T(8,128)(2,1)S(1)}, u32[]{:S(2)}, u32[]{:S(2)}) async-start(bf16[8,112,256]{2,1,0:T(8,128)(2,1)} %pad_maximum_fusion.4), calls=%async_computation.4 | async-start | bytes 917504 | tf_op jit(solution)/shard_map/sums_z/all_to_all | solution.py:386
  141.4 11.4 %all-to-all-done.4 = bf16[8,112,256]{2,1,0:T(8,128)(2,1)S(1)} async-done(((bf16[8,112,256]{2,1,0:T(8,128)(2,1)}), bf16[8,112,256]{2,1,0:T(8,128)(2,1)S(1)}, u32[]{:S(2)}, u32[]{:S(2)}) %all-to-all-start.4) | async-done | bytes 458784 | tf_op jit(solution)/shard_map/sums_z/all_to_all | solution.py:386
  155.4 24.2 %all_to_all.37 = f32[32,1,128]{2,1,0:T(1,128)S(1)} all-to-all(f32[32,1,128]{2,1,0:T(1,128)S(1)} %broadcast_in_dim.36), channel_id=1, replica_groups=mesh['z'=8,'x'=4,'c'=2,'mp'=4] {'x','c','mp'}, dimensions={0} | all-to-all | bytes 32768 | tf_op jit(solution)/shard_map/norm/all_to_all | solution.py:397
  180.2 3.3 %all-to-all-start.6 = ((f32[8,1,128]{2,1,0:T(1,128)}), f32[8,1,128]{2,1,0:T(1,128)S(1)}, u32[]{:S(2)}, u32[]{:S(2)}) async-start(f32[8,1,128]{2,1,0:T(1,128)} %broadcast_in_dim.37), calls=%async_computation.6 | async-start | bytes 8192 | tf_op jit(solution)/shard_map/norm/all_to_all | solution.py:399
  184.2 5.7 %all-to-all-done.6 = f32[8,1,128]{2,1,0:T(1,128)S(1)} async-done(((f32[8,1,128]{2,1,0:T(1,128)}), f32[8,1,128]{2,1,0:T(1,128)S(1)}, u32[]{:S(2)}, u32[]{:S(2)}) %all-to-all-start.6) | async-done | bytes 4128 | tf_op jit(solution)/shard_map/norm/all_to_all | solution.py:399
  (166 shorter events, 23.7 us)
Async XLA Ops:
  0.6 47.5 %copy-start = (f32[64,64]{1,0:T(8,128)S(1)}, f32[64,64]{1,0:T(8,128)}, u32[]{:S(2)}) copy-start(f32[64,64]{1,0:T(8,128)} %param.26) | copy-start | bytes 49156
  1.4 14.4 %copy-start.10 = (s32[1024,8]{0,1:T(8,128)S(1)}, s32[1024,8]{0,1:T(8,128)}, u32[]{:S(2)}) copy-start(s32[1024,8]{0,1:T(8,128)} %param.15) | copy-start | bytes 98308
  2.5 13.5 %copy-start.1 = (bf16[4096,256]{1,0:T(8,128)(2,1)S(1)}, bf16[4096,256]{1,0:T(8,128)(2,1)}, u32[]{:S(2)}) copy-start(bf16[4096,256]{1,0:T(8,128)(2,1)} %table_ref.1) | copy-start | bytes 6291460
  2.5 41.2 %all-to-all-start = ((bf16[64,32,256]{2,1,0:T(8,128)(2,1)}), bf16[64,32,256]{2,1,0:T(8,128)(2,1)}, u32[]{:S(2)}, u32[]{:S(2)}) async-start(bf16[64,32,256]{2,1,0:T(8,128)(2,1)} %broadcast_in_dim.28), calls=%async_computation | async-start | bytes 2097152 | tf_op jit(solution)/shard_map/weights_dp/all_to_all | solution.py:112
  16.0 13.6 %copy-start.9 = (s32[1024]{0:T(1024)S(1)}, s32[1024]{0:T(1024)}, u32[]{:S(2)}) copy-start(s32[1024]{0:T(1024)} %param.19) | copy-start | bytes 12292
  16.0 13.6 %copy-start.17 = (f32[256]{0:T(256)S(1)}, f32[256]{0:T(256)}, u32[]{:S(2)}) copy-start(f32[256]{0:T(256)} %param.25) | copy-start | bytes 3076
  16.0 13.6 %copy-start.18 = (f32[256]{0:T(256)S(1)}, f32[256]{0:T(256)}, u32[]{:S(2)}) copy-start(f32[256]{0:T(256)} %param.24) | copy-start | bytes 3076
  24.5 26.0 %collective-permute-start.2 = (bf16[1024,256]{1,0:T(8,128)(2,1)S(1)}, bf16[1024,256]{1,0:T(8,128)(2,1)S(1)}, u32[]{:S(2)}, u32[]{:S(2)}) collective-permute-start(bf16[1024,256]{1,0:T(8,128)(2,1)S(1)} %embed.1), channel_id=1, source_target_pairs={{0,1},{1,2},{2,3},{3,0},{4,5},{5,6},{6,7},{7,4},{8,9},{9,10},{10,1... | collective-permute-start | bytes 1572872 | tf_op jit(solution)/shard_map/base_mp/ppermute | solution.py:116
  25.9 25.8 %collective-permute-start.1 = (bf16[1024,256]{1,0:T(8,128)(2,1)S(1)}, bf16[1024,256]{1,0:T(8,128)(2,1)}, u32[]{:S(2)}, u32[]{:S(2)}) collective-permute-start(bf16[1024,256]{1,0:T(8,128)(2,1)S(1)} %embed.1), channel_id=1, source_target_pairs={{0,2},{1,3},{2,0},{3,1},{4,6},{5,7},{6,4},{7,5},{8,10},{9,11},{10,... | collective-permute-start | bytes 1572872 | tf_op jit(solution)/shard_map/base_mp/ppermute | solution.py:116
  28.5 24.8 %collective-permute-start = (bf16[1024,256]{1,0:T(8,128)(2,1)S(1)}, bf16[1024,256]{1,0:T(8,128)(2,1)S(1)}, u32[]{:S(2)}, u32[]{:S(2)}) collective-permute-start(bf16[1024,256]{1,0:T(8,128)(2,1)S(1)} %embed.1), channel_id=1, source_target_pairs={{0,3},{1,0},{2,1},{3,2},{4,7},{5,4},{6,5},{7,6},{8,11},{9,8},{10,9... | collective-permute-start | bytes 1572872 | tf_op jit(solution)/shard_map/base_mp/ppermute | solution.py:116
  29.6 18.5 %copy-start.16 = (s32[1024]{0:T(1024)S(1)}, s32[1024]{0:T(1024)}, u32[]{:S(2)}) copy-start(s32[1024]{0:T(1024)} %param.16) | copy-start | bytes 12292
  29.6 18.6 %copy-start.14 = (s32[1024]{0:T(1024)S(1)}, s32[1024]{0:T(1024)}, u32[]{:S(2)}) copy-start(s32[1024]{0:T(1024)} %param.17) | copy-start | bytes 12292
  29.6 19.1 %copy-start.11 = (f32[64,64]{1,0:T(8,128)S(1)}, f32[64,64]{1,0:T(8,128)}, u32[]{:S(2)}) copy-start(f32[64,64]{1,0:T(8,128)} %param.27) | copy-start | bytes 49156
  29.7 19.1 %copy-start.15 = (s32[1024]{0:T(1024)S(1)}, s32[1024]{0:T(1024)}, u32[]{:S(2)}) copy-start(s32[1024]{0:T(1024)} %param.18) | copy-start | bytes 12292
  29.7 19.7 %copy-start.12 = (f32[128,64]{0,1:T(8,128)S(1)}, f32[128,64]{0,1:T(8,128)}, u32[]{:S(2)}) copy-start(f32[128,64]{0,1:T(8,128)} %param.29) | copy-start | bytes 98308
  45.0 5.0 %copy-start.13 = (f32[128,64]{0,1:T(8,128)S(1)}, f32[128,64]{0,1:T(8,128)}, u32[]{:S(2)}) copy-start(f32[128,64]{0,1:T(8,128)} %param.28) | copy-start | bytes 98308
  45.0 13.6 %collective-permute-start.3 = (bf16[512,256]{1,0:T(8,128)(2,1)S(1)}, bf16[512,256]{1,0:T(8,128)(2,1)}, u32[]{:S(2)}, u32[]{:S(2)}) collective-permute-start(bf16[512,256]{1,0:T(8,128)(2,1)S(1)} %constant_dynamic-slice_fusion.6), channel_id=1, source_target_pairs={{0,3},{1,0},{2,1},{3,2},{4,7},{5,4},{6,5},{7,6},{8,11},{9,8},{10,9... | collective-permute-start | bytes 786440 | tf_op jit(solution)/shard_map/deep_weight_mp/ppermute | solution.py:116
  47.8 10.8 %collective-permute-start.4 = (bf16[512,256]{1,0:T(8,128)(2,1)S(1)}, bf16[512,256]{1,0:T(8,128)(2,1)}, u32[]{:S(2)}, u32[]{:S(2)}) collective-permute-start(bf16[512,256]{1,0:T(8,128)(2,1)S(1)} %constant_dynamic-slice_fusion.6), channel_id=1, source_target_pairs={{0,2},{1,3},{2,0},{3,1},{4,6},{5,7},{6,4},{7,5},{8,10},{9,11},{10,... | collective-permute-start | bytes 786440 | tf_op jit(solution)/shard_map/deep_weight_mp/ppermute | solution.py:116
  50.6 2.4 %copy-start.7 = (bf16[1024,256]{1,0:T(8,128)(2,1)}, bf16[1024,256]{1,0:T(8,128)(2,1)S(1)}, u32[]{:S(2)}) copy-start(bf16[1024,256]{1,0:T(8,128)(2,1)S(1)} %collective-permute-done.2) | copy-start | bytes 1572868
  50.6 12.4 %collective-permute-start.5 = (bf16[512,256]{1,0:T(8,128)(2,1)S(1)}, bf16[512,256]{1,0:T(8,128)(2,1)}, u32[]{:S(2)}, u32[]{:S(2)}) collective-permute-start(bf16[512,256]{1,0:T(8,128)(2,1)S(1)} %constant_dynamic-slice_fusion.6), channel_id=1, source_target_pairs={{0,1},{1,2},{2,3},{3,0},{4,5},{5,6},{6,7},{7,4},{8,9},{9,10},{10,1... | collective-permute-start | bytes 786440 | tf_op jit(solution)/shard_map/deep_weight_mp/ppermute | solution.py:116
  51.4 1.7 copy-start.19
  53.4 0.9 copy-start.5
  55.1 12.7 %all-to-all-start.1 = ((bf16[4,272,256]{2,1,0:T(8,128)(2,1)}), bf16[4,272,256]{2,1,0:T(8,128)(2,1)S(1)}, u32[]{:S(2)}, u32[]{:S(2)}) async-start(bf16[4,272,256]{2,1,0:T(8,128)(2,1)} %pad_maximum_fusion.1), calls=%async_computation.1 | async-start | bytes 1114112 | tf_op jit(solution)/shard_map/crossed_mp/all_to_all | solution.py:249
  66.0 4.3 %collective-permute-start.6 = (bf16[512,1024]{1,0:T(8,128)(2,1)S(1)}, bf16[512,1024]{1,0:T(8,128)(2,1)}, u32[]{:S(2)}, u32[]{:S(2)}) collective-permute-start(bf16[512,1024]{1,0:T(8,128)(2,1)S(1)} %constant_dynamic-update-slice_fusion), channel_id=1, source_target_pairs={{0,4},{4,0},{1,5},{5,1},{2,6},{6,2},{3,7},{7,3},{8,12},{12,8},{9,1... | collective-permute-start | bytes 3145736 | tf_op jit(solution)/shard_map/deep_weight_core/ppermute | solution.py:107
  75.8 14.2 %collective-permute-start.7 = (f32[256]{0:T(256)S(1)}, f32[256]{0:T(256)S(1)}, u32[]{:S(2)}, u32[]{:S(2)}) collective-permute-start(f32[256]{0:T(256)S(1)} %get-tuple-element.28), channel_id=1, source_target_pairs={{0,3},{1,0},{2,1},{3,2},{4,7},{5,4},{6,5},{7,6},{8,11},{9,8},{10,9... | collective-permute-start | bytes 3080 | tf_op jit(solution)/shard_map/stats/ppermute | solution.py:116
  78.3 11.7 %collective-permute-start.8 = (f32[256]{0:T(256)S(1)}, f32[256]{0:T(256)S(1)}, u32[]{:S(2)}, u32[]{:S(2)}) collective-permute-start(f32[256]{0:T(256)S(1)} %get-tuple-element.28), channel_id=1, source_target_pairs={{0,2},{1,3},{2,0},{3,1},{4,6},{5,7},{6,4},{7,5},{8,10},{9,11},{10,... | collective-permute-start | bytes 3080 | tf_op jit(solution)/shard_map/stats/ppermute | solution.py:116
  79.9 10.1 %collective-permute-start.9 = (f32[256]{0:T(256)S(1)}, f32[256]{0:T(256)S(1)}, u32[]{:S(2)}, u32[]{:S(2)}) collective-permute-start(f32[256]{0:T(256)S(1)} %get-tuple-element.28), channel_id=1, source_target_pairs={{0,1},{1,2},{2,3},{3,0},{4,5},{5,6},{6,7},{7,4},{8,9},{9,10},{10,1... | collective-permute-start | bytes 3080 | tf_op jit(solution)/shard_map/stats/ppermute | solution.py:116
  79.9 17.0 %all-to-all-start.2 = ((bf16[4,264,256]{2,1,0:T(8,128)(2,1)}), bf16[4,264,256]{2,1,0:T(8,128)(2,1)}, u32[]{:S(2)}, u32[]{:S(2)}) async-start(bf16[4,264,256]{2,1,0:T(8,128)(2,1)} %pad_maximum_fusion.2), calls=%async_computation.2 | async-start | bytes 1081344 | tf_op jit(solution)/shard_map/crossed_grad/all_to_all | solution.py:299
  87.1 1.6 copy-start.2
  88.7 11.3 %collective-permute-start.11 = (bf16[4,32,16,256]{3,2,1,0:T(8,128)(2,1)}, bf16[4,32,16,256]{3,2,1,0:T(8,128)(2,1)}, u32[]{:S(2)}, u32[]{:S(2)}) collective-permute-start(bf16[4,32,16,256]{3,2,1,0:T(8,128)(2,1)} %fusion.18), channel_id=1, source_target_pairs={{0,4},{4,0},{1,5},{5,1},{2,6},{6,2},{3,7},{7,3},{8,12},{12,8},{9,1... | collective-permute-start | bytes 3145736 | tf_op jit(solution)/shard_map/deep_grad/ppermute | solution.py:107
  96.7 10.5 %collective-permute-start.10 = (bf16[32,80,256]{2,1,0:T(8,128)(2,1)S(1)}, bf16[32,80,256]{2,1,0:T(8,128)(2,1)}, u32[]{:S(2)}, u32[]{:S(2)}) collective-permute-start(bf16[32,80,256]{2,1,0:T(8,128)(2,1)S(1)} %get-tuple-element.30), channel_id=1, source_target_pairs={{0,4},{4,0},{1,5},{5,1},{2,6},{6,2},{3,7},{7,3},{8,12},{12,8},{9,1... | collective-permute-start | bytes 3932168 | tf_op jit(solution)/shard_map/stats_sum/ppermute | solution.py:107
  97.0 3.1 %copy-start.3 = (bf16[4,32,2,16,256]{4,3,2,1,0:T(8,128)(2,1)S(1)}, bf16[4,32,2,16,256]{4,3,2,1,0:T(8,128)(2,1)}, u32[]{:S(2)}) copy-start(bf16[4,32,2,16,256]{4,3,2,1,0:T(8,128)(2,1)} %copy-done.2) | copy-start | bytes 6291460
  102.7 20.1 %all-to-all-start.3 = ((bf16[4,32,16,256]{3,2,1,0:T(8,128)(2,1)}), bf16[4,32,16,256]{3,2,1,0:T(8,128)(2,1)}, u32[]{:S(2)}, u32[]{:S(2)}) async-start(bf16[4,32,16,256]{3,2,1,0:T(8,128)(2,1)} %fusion), calls=%async_computation.3 | async-start | bytes 2097152 | tf_op jit(solution)/shard_map/deep_grad/all_to_all | solution.py:340
  107.2 1.7 copy-start.4
  108.9 1.0 copy-start.6
  109.9 1.8 copy-start.8
  112.2 5.3 %collective-permute-start.12 = (bf16[32,16,256]{2,1,0:T(8,128)(2,1)S(1)}, bf16[32,16,256]{2,1,0:T(8,128)(2,1)S(1)}, u32[]{:S(2)}, u32[]{:S(2)}) collective-permute-start(bf16[32,16,256]{2,1,0:T(8,128)(2,1)S(1)} %fusion.40), channel_id=1, source_target_pairs={{0,4},{4,0},{1,5},{5,1},{2,6},{6,2},{3,7},{7,3},{8,12},{12,8},{9,1... | collective-permute-start | bytes 786440 | tf_op jit(solution)/shard_map/cross_grad/ppermute | solution.py:107
  113.0 4.5 %collective-permute-start.15 = (f32[3,256]{1,0:T(4,128)S(1)}, f32[3,256]{1,0:T(4,128)S(1)}, u32[]{:S(2)}, u32[]{:S(2)}) collective-permute-start(f32[3,256]{1,0:T(4,128)S(1)} %pad_maximum_fusion.7), channel_id=1, source_target_pairs={{0,4},{4,0},{1,5},{5,1},{2,6},{6,2},{3,7},{7,3},{8,12},{12,8},{9,1... | collective-permute-start | bytes 9224 | tf_op jit(solution)/shard_map/cross_grad/ppermute | solution.py:107
  113.2 9.6 %collective-permute-start.13 = (bf16[8,72,256]{2,1,0:T(8,128)(2,1)S(1)}, bf16[8,72,256]{2,1,0:T(8,128)(2,1)S(1)}, u32[]{:S(2)}, u32[]{:S(2)}) collective-permute-start(bf16[8,72,256]{2,1,0:T(8,128)(2,1)S(1)} %get-tuple-element.102), channel_id=1, source_target_pairs={{0,8},{8,16},{16,24},{24,0},{1,9},{9,17},{17,25},{25,1},{2,10},{10... | collective-permute-start | bytes 884744 | tf_op jit(solution)/shard_map/stats_sum/ppermute | solution.py:116
  114.5 8.3 %collective-permute-start.14 = (bf16[8,72,256]{2,1,0:T(8,128)(2,1)S(1)}, bf16[8,72,256]{2,1,0:T(8,128)(2,1)S(1)}, u32[]{:S(2)}, u32[]{:S(2)}) collective-permute-start(bf16[8,72,256]{2,1,0:T(8,128)(2,1)S(1)} %get-tuple-element.101), channel_id=1, source_target_pairs={{0,24},{8,0},{16,8},{24,16},{1,25},{9,1},{17,9},{25,17},{2,26},{10... | collective-permute-start | bytes 884744 | tf_op jit(solution)/shard_map/stats_sum/ppermute | solution.py:116
  116.0 14.1 %collective-permute-start.19 = (bf16[8,72,256]{2,1,0:T(8,128)(2,1)S(1)}, bf16[8,72,256]{2,1,0:T(8,128)(2,1)}, u32[]{:S(2)}, u32[]{:S(2)}) collective-permute-start(bf16[8,72,256]{2,1,0:T(8,128)(2,1)S(1)} %get-tuple-element.100), channel_id=1, source_target_pairs={{0,16},{8,24},{16,0},{24,8},{1,17},{9,25},{17,1},{25,9},{2,18},{10... | collective-permute-start | bytes 884744 | tf_op jit(solution)/shard_map/stats_sum/ppermute | solution.py:116
  124.6 7.7 %collective-permute-start.16 = (bf16[8,40,256]{2,1,0:T(8,128)(2,1)S(1)}, bf16[8,40,256]{2,1,0:T(8,128)(2,1)S(1)}, u32[]{:S(2)}, u32[]{:S(2)}) collective-permute-start(bf16[8,40,256]{2,1,0:T(8,128)(2,1)S(1)} %get-tuple-element.105), channel_id=1, source_target_pairs={{0,8},{8,16},{16,24},{24,0},{1,9},{9,17},{17,25},{25,1},{2,10},{10... | collective-permute-start | bytes 491528 | tf_op jit(solution)/shard_map/grads_x/ppermute | solution.py:116
  125.5 8.5 %collective-permute-start.17 = (bf16[8,40,256]{2,1,0:T(8,128)(2,1)S(1)}, bf16[8,40,256]{2,1,0:T(8,128)(2,1)S(1)}, u32[]{:S(2)}, u32[]{:S(2)}) collective-permute-start(bf16[8,40,256]{2,1,0:T(8,128)(2,1)S(1)} %get-tuple-element.107), channel_id=1, source_target_pairs={{0,16},{8,24},{16,0},{24,8},{1,17},{9,25},{17,1},{25,9},{2,18},{10... | collective-permute-start | bytes 491528 | tf_op jit(solution)/shard_map/grads_x/ppermute | solution.py:116
  128.5 5.5 %collective-permute-start.18 = (bf16[8,40,256]{2,1,0:T(8,128)(2,1)S(1)}, bf16[8,40,256]{2,1,0:T(8,128)(2,1)S(1)}, u32[]{:S(2)}, u32[]{:S(2)}) collective-permute-start(bf16[8,40,256]{2,1,0:T(8,128)(2,1)S(1)} %get-tuple-element.106), channel_id=1, source_target_pairs={{0,24},{8,0},{16,8},{24,16},{1,25},{9,1},{17,9},{25,17},{2,26},{10... | collective-permute-start | bytes 491528 | tf_op jit(solution)/shard_map/grads_x/ppermute | solution.py:116
  134.9 17.9 %all-to-all-start.4 = ((bf16[8,112,256]{2,1,0:T(8,128)(2,1)}), bf16[8,112,256]{2,1,0:T(8,128)(2,1)S(1)}, u32[]{:S(2)}, u32[]{:S(2)}) async-start(bf16[8,112,256]{2,1,0:T(8,128)(2,1)} %pad_maximum_fusion.4), calls=%async_computation.4 | async-start | bytes 917504 | tf_op jit(solution)/shard_map/sums_z/all_to_all | solution.py:386
  180.2 9.7 %all-to-all-start.6 = ((f32[8,1,128]{2,1,0:T(1,128)}), f32[8,1,128]{2,1,0:T(1,128)S(1)}, u32[]{:S(2)}, u32[]{:S(2)}) async-start(f32[8,1,128]{2,1,0:T(1,128)} %broadcast_in_dim.37), calls=%async_computation.6 | async-start | bytes 8192 | tf_op jit(solution)/shard_map/norm/all_to_all | solution.py:399

commit v4 on v3

--- a/solution.py
+++ b/solution.py
@@ -343,12 +343,13 @@
         stats_pair = stats_pair[:, : feats + 8].reshape(n_z, n_x, feats + 8, 2 * ctx_count)
         crossed_back = after(crossed_back, stats_pair, deep_pair)
         stats_parts = [block_ahead(stats_pair, my_x, t, 1) for t in range(n_x)]
-        stats_parts = stats_parts[:1] + [
-            shift(stats_parts[t], "x", n_x, t) for t in range(1, n_x)
-        ]
+        stats_parts[1] = shift(stats_parts[1], "x", n_x, 1)
+        stats_parts[-1] = shift(stats_parts[-1], "x", n_x, n_x - 1)
         deep_sum, stats_parts[1], stats_parts[-1] = lax.optimization_barrier(
             (deep_sum, stats_parts[1], stats_parts[-1])
         )
+        for t in range(2, n_x - 1):
+            stats_parts[t] = shift(after(stats_parts[t], deep_sum), "x", n_x, t)
         deep_sum = jnp.sum(deep_sum.astype(F32), axis=0).astype(BF16)
 
     with jax.named_scope("cross_grad"):

time: 192 us -> 196 us (1.021)
  waiting for transfers between devices: 46.7 us -> 55.9 us
  blocking collectives: 24.2 us -> 17.5 us
    ppermute x15, waiting for transfers between devices: 13.6 us -> 21.3 us  [shift(): lax.ppermute(value, axis, [(i, (i + ahead) % count) for i in range(count)])]
    all_to_all x1, blocking collectives: 24.2 us -> 17.5 us  [shards(): squares = lax.all_to_all(squares, ('x', 'c', 'mp'), 0, 0, tiled=True)]
  transfers between devices with their start and end apart: 26 -> 26, of which waited for: 9 -> 9; matrix products, arithmetic and copies ran while one was open for 16% -> 15% of each run, Pallas kernels for 7% -> 7%
where the time goes in v4:
time: 196 us; the launch traced here: 195 us
  starting transfers between devices  60.3 us (31%)
  waiting for transfers between devices  55.9 us (29%)
  other arithmetic  20.7 us (11%)
  blocking collectives  17.5 us (9%)
  Pallas kernels  13.5 us (7%)
  local copies, waits for them, and re-layouts  12.3 us (6%)
  matrix products  11.4 us (6%)
  between operations  2.97 us (2%)
    ppermute x15, waiting for transfers between devices, shift(): lax.ppermute(value, axis, [(i, (i + ahead) % count) for i in range(count)])  21.3 us
    ppermute x15, starting transfers between devices, shift(): lax.ppermute(value, axis, [(i, (i + ahead) % count) for i in range(count)])  20.9 us
    all_to_all x1, blocking collectives, shards(): squares = lax.all_to_all(squares, ('x', 'c', 'mp'), 0, 0, tiled=True)  17.5 us
    all_to_all x1, waiting for transfers between devices, gather(): return lax.all_to_all(wide, axes, 0, 0, tiled=True)  14 us
    all_to_all x1, starting transfers between devices, gather(): return lax.all_to_all(wide, axes, 0, 0, tiled=True)  13.3 us
    all_to_all x1, waiting for transfers between devices, shards(): lax.all_to_all(jnp.concatenate([grads_x, stats_x], axis=1), 'z', 0, 0, ti...  12.9 us
    pallas_call x1, Pallas kernels, embed(): pl.pallas_call(embed_kernel, out_shape=jax.ShapeDtypeStruct((rows, table....  8.49 us
    all_to_all x1, starting transfers between devices, shards(): lax.all_to_all(jnp.concatenate([grads_x, stats_x], axis=1), 'z', 0, 0, ti...  6.49 us
  transfers between devices with their start and end apart: 26, of which 9 were waited for; matrix products, arithmetic and copies ran while one was open for 15% of the time, Pallas kernels for 7%

profile of v4, /device:TPU:1, one launch (start us, length us, event | category | flops | bytes accessed | tf_op | source)
XLA Modules:
  0.0 194.7 jit_solution(6436841477026893579)
XLA Ops:
  1.4 1.1 broadcast_in_dim.28
  2.5 13.3 %all-to-all-start = ((bf16[64,32,256]{2,1,0:T(8,128)(2,1)}), bf16[64,32,256]{2,1,0:T(8,128)(2,1)}, u32[]{:S(2)}, u32[]{:S(2)}) async-start(bf16[64,32,256]{2,1,0:T(8,128)(2,1)} %broadcast_in_dim.28), calls=%async_computation | async-start | bytes 2097152 | tf_op jit(solution)/shard_map/weights_dp/all_to_all | solution.py:112
  16.0 8.5 %embed.1 = bf16[1024,256]{1,0:T(8,128)(2,1)S(1)} custom-call(s32[1024,8]{1,0:T(8,128)S(1)} %copy.139.ids_ref, bf16[4096,256]{1,0:T(8,128)(2,1)S(1)} %copy-done.1), custom_call_target="tpu_custom_call" | custom-call | tf_op jit(solution)/shard_map/embed/pallas_call | solution.py:59
  24.5 1.4 collective-permute-start.2
  25.9 2.6 %collective-permute-start.1 = (bf16[1024,256]{1,0:T(8,128)(2,1)S(1)}, bf16[1024,256]{1,0:T(8,128)(2,1)}, u32[]{:S(2)}, u32[]{:S(2)}) collective-permute-start(bf16[1024,256]{1,0:T(8,128)(2,1)S(1)} %embed.1), channel_id=1, source_target_pairs={{0,2},{1,3},{2,0},{3,1},{4,6},{5,7},{6,4},{7,5},{8,10},{9,11},{10,... | collective-permute-start | bytes 1572872 | tf_op jit(solution)/shard_map/base_mp/ppermute | solution.py:116
  28.5 1.1 collective-permute-start
  29.7 14.0 %all-to-all-done = bf16[64,32,256]{2,1,0:T(8,128)(2,1)} async-done(((bf16[64,32,256]{2,1,0:T(8,128)(2,1)}), bf16[64,32,256]{2,1,0:T(8,128)(2,1)}, u32[]{:S(2)}, u32[]{:S(2)}) %all-to-all-start) | async-done | bytes 1048608 | tf_op jit(solution)/shard_map/weights_dp/all_to_all | solution.py:112
  43.7 1.3 fusion.86
  45.0 2.8 %collective-permute-start.3 = (bf16[512,256]{1,0:T(8,128)(2,1)S(1)}, bf16[512,256]{1,0:T(8,128)(2,1)}, u32[]{:S(2)}, u32[]{:S(2)}) collective-permute-start(bf16[512,256]{1,0:T(8,128)(2,1)S(1)} %constant_dynamic-slice_fusion.6), channel_id=1, source_target_pairs={{0,3},{1,0},{2,1},{3,2},{4,7},{5,4},{6,5},{7,6},{8,11},{9,8},{10,9... | collective-permute-start | bytes 786440 | tf_op jit(solution)/shard_map/deep_weight_mp/ppermute | solution.py:116
  51.7 1.3 fusion.51
  54.3 0.8 pad_maximum_fusion.1
  55.1 3.5 %all-to-all-start.1 = ((bf16[4,272,256]{2,1,0:T(8,128)(2,1)}), bf16[4,272,256]{2,1,0:T(8,128)(2,1)S(1)}, u32[]{:S(2)}, u32[]{:S(2)}) async-start(bf16[4,272,256]{2,1,0:T(8,128)(2,1)} %pad_maximum_fusion.1), calls=%async_computation.1 | async-start | bytes 1114112 | tf_op jit(solution)/shard_map/crossed_mp/all_to_all | solution.py:249
  58.6 4.3 %collective-permute-done.5 = bf16[512,256]{1,0:T(8,128)(2,1)} collective-permute-done((bf16[512,256]{1,0:T(8,128)(2,1)S(1)}, bf16[512,256]{1,0:T(8,128)(2,1)}, u32[]{:S(2)}, u32[]{:S(2)}) %collective-permute-start.5) | collective-permute-done | bytes 262176 | tf_op jit(solution)/shard_map/deep_weight_mp/ppermute | solution.py:116
  63.0 1.0 constant_dynamic-update-slice_fusion.2
  64.0 1.0 constant_dynamic-update-slice_fusion.1
  65.0 1.0 constant_dynamic-update-slice_fusion
  66.0 1.9 collective-permute-start.6
  68.2 2.0 %collective-permute-done.6 = bf16[512,1024]{1,0:T(8,128)(2,1)} collective-permute-done((bf16[512,1024]{1,0:T(8,128)(2,1)S(1)}, bf16[512,1024]{1,0:T(8,128)(2,1)}, u32[]{:S(2)}, u32[]{:S(2)}) %collective-permute-start.6) | collective-permute-done | bytes 1048608 | tf_op jit(solution)/shard_map/deep_weight_core/ppermute | solution.py:107
  70.2 1.4 broadcast_select_fusion.1
  75.8 2.5 %collective-permute-start.7 = (f32[256]{0:T(256)S(1)}, f32[256]{0:T(256)S(1)}, u32[]{:S(2)}, u32[]{:S(2)}) collective-permute-start(f32[256]{0:T(256)S(1)} %get-tuple-element.29), channel_id=1, source_target_pairs={{0,3},{1,0},{2,1},{3,2},{4,7},{5,4},{6,5},{7,6},{8,11},{9,8},{10,9... | collective-permute-start | bytes 3080 | tf_op jit(solution)/shard_map/stats/ppermute | solution.py:116
  78.3 1.7 collective-permute-start.8
  79.9 4.2 %all-to-all-start.2 = ((bf16[4,264,256]{2,1,0:T(8,128)(2,1)}), bf16[4,264,256]{2,1,0:T(8,128)(2,1)}, u32[]{:S(2)}, u32[]{:S(2)}) async-start(bf16[4,264,256]{2,1,0:T(8,128)(2,1)} %pad_maximum_fusion.2), calls=%async_computation.2 | async-start | bytes 1081344 | tf_op jit(solution)/shard_map/crossed_grad/all_to_all | solution.py:299
  84.5 1.1 constant_dynamic-slice_fusion.4
  87.1 1.2 fusion.18
  88.7 1.3 collective-permute-start.11
  91.8 5.0 %stats.1 = (bf16[32,80,256]{2,1,0:T(8,128)(2,1)S(1)}, bf16[32,80,256]{2,1,0:T(8,128)(2,1)S(1)}) custom-call(s32[1]{0:T(128)} %bitcast.15.core_ref, f32[64,1024]{1,0:T(8,128)S(1)} %bitcast.170, bf16[1024,256]{1,0:T(8,128)(2,1)S(1)} %pad_maximum_fusion.3.weights_ref, f32[64,256]{1,0:T(8,128)S(1)} %fusion.19.grads_ref), custom_call_target="tpu_custom_call" | custom-call | flops 1000 | bytes 1000 | tf_op jit(solution)/shard_map/stats/pallas_call | solution.py:96
  97.0 1.2 slice.155
  99.0 1.1 bitcast_convert_fusion
  100.1 2.6 %fusion = bf16[4,32,16,256]{3,2,1,0:T(8,128)(2,1)} fusion(bf16[4,32,16,256]{3,2,1,0:T(8,128)(2,1)} %collective-permute-done.11, pred[]{:T(512)S(6)} %eq.70, bf16[4,32,2,16,256]{4,3,2,1,0:T(8,128)(2,1)S(1)} %copy-done.3), kind=kLoop, calls=%fused_computation.3 | loop fusion | flops 2621440 | bytes 4194305 | tf_op jit(solution)/shard_map/deep_grad/convert_element_type | solution.py:339
  102.8 4.5 %all-to-all-start.3 = ((bf16[4,32,16,256]{3,2,1,0:T(8,128)(2,1)}), bf16[4,32,16,256]{3,2,1,0:T(8,128)(2,1)}, u32[]{:S(2)}, u32[]{:S(2)}) async-start(bf16[4,32,16,256]{3,2,1,0:T(8,128)(2,1)} %fusion), calls=%async_computation.3 | async-start | bytes 2097152 | tf_op jit(solution)/shard_map/deep_grad/all_to_all | solution.py:340
  107.3 1.7 add_convert_fusion
  110.4 1.4 constant_dynamic-update-slice_fusion.9
  113.3 1.3 collective-permute-start.13
  114.6 1.5 collective-permute-start.14
  116.2 6.7 %collective-permute-done.13 = bf16[8,72,256]{2,1,0:T(8,128)(2,1)S(1)} collective-permute-done((bf16[8,72,256]{2,1,0:T(8,128)(2,1)S(1)}, bf16[8,72,256]{2,1,0:T(8,128)(2,1)S(1)}, u32[]{:S(2)}, u32[]{:S(2)}) %collective-permute-start.13) | collective-permute-done | bytes 294944 | tf_op jit(solution)/shard_map/stats_sum/ppermute | solution.py:116
  122.9 1.5 reduce_sum.135
  125.3 0.9 collective-permute-start.16
  126.2 2.7 %collective-permute-start.17 = (bf16[8,40,256]{2,1,0:T(8,128)(2,1)S(1)}, bf16[8,40,256]{2,1,0:T(8,128)(2,1)S(1)}, u32[]{:S(2)}, u32[]{:S(2)}) collective-permute-start(bf16[8,40,256]{2,1,0:T(8,128)(2,1)S(1)} %get-tuple-element.109), channel_id=1, source_target_pairs={{0,16},{8,24},{16,0},{24,8},{1,17},{9,25},{17,1},{25,9},{2,18},{10... | collective-permute-start | bytes 491528 | tf_op jit(solution)/shard_map/grads_x/ppermute | solution.py:116
  129.5 0.9 collective-permute-start.19
  130.9 4.0 %collective-permute-done.17 = bf16[8,40,256]{2,1,0:T(8,128)(2,1)S(1)} collective-permute-done((bf16[8,40,256]{2,1,0:T(8,128)(2,1)S(1)}, bf16[8,40,256]{2,1,0:T(8,128)(2,1)S(1)}, u32[]{:S(2)}, u32[]{:S(2)}) %collective-permute-start.17) | collective-permute-done | bytes 163872 | tf_op jit(solution)/shard_map/grads_x/ppermute | solution.py:116
  135.0 1.0 fusion.39
  136.0 5.6 %collective-permute-done.19 = bf16[8,72,256]{2,1,0:T(8,128)(2,1)S(1)} collective-permute-done((bf16[8,72,256]{2,1,0:T(8,128)(2,1)S(1)}, bf16[8,72,256]{2,1,0:T(8,128)(2,1)S(1)}, u32[]{:S(2)}, u32[]{:S(2)}) %collective-permute-start.19) | collective-permute-done | bytes 294944 | tf_op jit(solution)/shard_map/stats_sum/ppermute | solution.py:116
  141.6 1.1 fusion.28
  143.5 6.5 %all-to-all-start.4 = ((bf16[8,112,256]{2,1,0:T(8,128)(2,1)}), bf16[8,112,256]{2,1,0:T(8,128)(2,1)S(1)}, u32[]{:S(2)}, u32[]{:S(2)}) async-start(bf16[8,112,256]{2,1,0:T(8,128)(2,1)} %pad_maximum_fusion.4), calls=%async_computation.4 | async-start | bytes 917504 | tf_op jit(solution)/shard_map/sums_z/all_to_all | solution.py:387
  150.0 12.9 %all-to-all-done.4 = bf16[8,112,256]{2,1,0:T(8,128)(2,1)S(1)} async-done(((bf16[8,112,256]{2,1,0:T(8,128)(2,1)}), bf16[8,112,256]{2,1,0:T(8,128)(2,1)S(1)}, u32[]{:S(2)}, u32[]{:S(2)}) %all-to-all-start.4) | async-done | bytes 458784 | tf_op jit(solution)/shard_map/sums_z/all_to_all | solution.py:387
  165.5 17.5 %all_to_all.37 = f32[32,1,128]{2,1,0:T(1,128)S(1)} all-to-all(f32[32,1,128]{2,1,0:T(1,128)S(1)} %broadcast_in_dim.36), channel_id=1, replica_groups=mesh['z'=8,'x'=4,'c'=2,'mp'=4] {'x','c','mp'}, dimensions={0} | all-to-all | bytes 32768 | tf_op jit(solution)/shard_map/norm/all_to_all | solution.py:398
  183.7 3.3 %all-to-all-start.6 = ((f32[8,1,128]{2,1,0:T(1,128)}), f32[8,1,128]{2,1,0:T(1,128)S(1)}, u32[]{:S(2)}, u32[]{:S(2)}) async-start(f32[8,1,128]{2,1,0:T(1,128)} %broadcast_in_dim.37), calls=%async_computation.6 | async-start | bytes 8192 | tf_op jit(solution)/shard_map/norm/all_to_all | solution.py:400
  187.7 5.7 %all-to-all-done.6 = f32[8,1,128]{2,1,0:T(1,128)S(1)} async-done(((f32[8,1,128]{2,1,0:T(1,128)}), f32[8,1,128]{2,1,0:T(1,128)S(1)}, u32[]{:S(2)}, u32[]{:S(2)}) %all-to-all-start.6) | async-done | bytes 4128 | tf_op jit(solution)/shard_map/norm/all_to_all | solution.py:400
  (166 shorter events, 25.1 us)
Async XLA Ops:
  0.6 47.5 %copy-start = (f32[64,64]{1,0:T(8,128)S(1)}, f32[64,64]{1,0:T(8,128)}, u32[]{:S(2)}) copy-start(f32[64,64]{1,0:T(8,128)} %param.26) | copy-start | bytes 49156
  1.4 14.4 %copy-start.10 = (s32[1024,8]{0,1:T(8,128)S(1)}, s32[1024,8]{0,1:T(8,128)}, u32[]{:S(2)}) copy-start(s32[1024,8]{0,1:T(8,128)} %param.15) | copy-start | bytes 98308
  2.5 13.5 %copy-start.1 = (bf16[4096,256]{1,0:T(8,128)(2,1)S(1)}, bf16[4096,256]{1,0:T(8,128)(2,1)}, u32[]{:S(2)}) copy-start(bf16[4096,256]{1,0:T(8,128)(2,1)} %table_ref.1) | copy-start | bytes 6291460
  2.5 41.2 %all-to-all-start = ((bf16[64,32,256]{2,1,0:T(8,128)(2,1)}), bf16[64,32,256]{2,1,0:T(8,128)(2,1)}, u32[]{:S(2)}, u32[]{:S(2)}) async-start(bf16[64,32,256]{2,1,0:T(8,128)(2,1)} %broadcast_in_dim.28), calls=%async_computation | async-start | bytes 2097152 | tf_op jit(solution)/shard_map/weights_dp/all_to_all | solution.py:112
  16.0 13.6 %copy-start.9 = (s32[1024]{0:T(1024)S(1)}, s32[1024]{0:T(1024)}, u32[]{:S(2)}) copy-start(s32[1024]{0:T(1024)} %param.19) | copy-start | bytes 12292
  16.0 13.6 %copy-start.17 = (f32[256]{0:T(256)S(1)}, f32[256]{0:T(256)}, u32[]{:S(2)}) copy-start(f32[256]{0:T(256)} %param.25) | copy-start | bytes 3076
  16.0 13.6 %copy-start.18 = (f32[256]{0:T(256)S(1)}, f32[256]{0:T(256)}, u32[]{:S(2)}) copy-start(f32[256]{0:T(256)} %param.24) | copy-start | bytes 3076
  24.5 26.0 %collective-permute-start.2 = (bf16[1024,256]{1,0:T(8,128)(2,1)S(1)}, bf16[1024,256]{1,0:T(8,128)(2,1)S(1)}, u32[]{:S(2)}, u32[]{:S(2)}) collective-permute-start(bf16[1024,256]{1,0:T(8,128)(2,1)S(1)} %embed.1), channel_id=1, source_target_pairs={{0,1},{1,2},{2,3},{3,0},{4,5},{5,6},{6,7},{7,4},{8,9},{9,10},{10,1... | collective-permute-start | bytes 1572872 | tf_op jit(solution)/shard_map/base_mp/ppermute | solution.py:116
  25.9 25.8 %collective-permute-start.1 = (bf16[1024,256]{1,0:T(8,128)(2,1)S(1)}, bf16[1024,256]{1,0:T(8,128)(2,1)}, u32[]{:S(2)}, u32[]{:S(2)}) collective-permute-start(bf16[1024,256]{1,0:T(8,128)(2,1)S(1)} %embed.1), channel_id=1, source_target_pairs={{0,2},{1,3},{2,0},{3,1},{4,6},{5,7},{6,4},{7,5},{8,10},{9,11},{10,... | collective-permute-start | bytes 1572872 | tf_op jit(solution)/shard_map/base_mp/ppermute | solution.py:116
  28.5 24.8 %collective-permute-start = (bf16[1024,256]{1,0:T(8,128)(2,1)S(1)}, bf16[1024,256]{1,0:T(8,128)(2,1)S(1)}, u32[]{:S(2)}, u32[]{:S(2)}) collective-permute-start(bf16[1024,256]{1,0:T(8,128)(2,1)S(1)} %embed.1), channel_id=1, source_target_pairs={{0,3},{1,0},{2,1},{3,2},{4,7},{5,4},{6,5},{7,6},{8,11},{9,8},{10,9... | collective-permute-start | bytes 1572872 | tf_op jit(solution)/shard_map/base_mp/ppermute | solution.py:116
  29.6 18.5 %copy-start.16 = (s32[1024]{0:T(1024)S(1)}, s32[1024]{0:T(1024)}, u32[]{:S(2)}) copy-start(s32[1024]{0:T(1024)} %param.16) | copy-start | bytes 12292
  29.6 18.6 %copy-start.14 = (s32[1024]{0:T(1024)S(1)}, s32[1024]{0:T(1024)}, u32[]{:S(2)}) copy-start(s32[1024]{0:T(1024)} %param.17) | copy-start | bytes 12292
  29.6 19.1 %copy-start.11 = (f32[64,64]{1,0:T(8,128)S(1)}, f32[64,64]{1,0:T(8,128)}, u32[]{:S(2)}) copy-start(f32[64,64]{1,0:T(8,128)} %param.27) | copy-start | bytes 49156
  29.7 19.1 %copy-start.15 = (s32[1024]{0:T(1024)S(1)}, s32[1024]{0:T(1024)}, u32[]{:S(2)}) copy-start(s32[1024]{0:T(1024)} %param.18) | copy-start | bytes 12292
  29.7 19.7 %copy-start.12 = (f32[128,64]{0,1:T(8,128)S(1)}, f32[128,64]{0,1:T(8,128)}, u32[]{:S(2)}) copy-start(f32[128,64]{0,1:T(8,128)} %param.29) | copy-start | bytes 98308
  45.0 5.0 %copy-start.13 = (f32[128,64]{0,1:T(8,128)S(1)}, f32[128,64]{0,1:T(8,128)}, u32[]{:S(2)}) copy-start(f32[128,64]{0,1:T(8,128)} %param.28) | copy-start | bytes 98308
  45.0 13.6 %collective-permute-start.3 = (bf16[512,256]{1,0:T(8,128)(2,1)S(1)}, bf16[512,256]{1,0:T(8,128)(2,1)}, u32[]{:S(2)}, u32[]{:S(2)}) collective-permute-start(bf16[512,256]{1,0:T(8,128)(2,1)S(1)} %constant_dynamic-slice_fusion.6), channel_id=1, source_target_pairs={{0,3},{1,0},{2,1},{3,2},{4,7},{5,4},{6,5},{7,6},{8,11},{9,8},{10,9... | collective-permute-start | bytes 786440 | tf_op jit(solution)/shard_map/deep_weight_mp/ppermute | solution.py:116
  47.8 10.8 %collective-permute-start.4 = (bf16[512,256]{1,0:T(8,128)(2,1)S(1)}, bf16[512,256]{1,0:T(8,128)(2,1)}, u32[]{:S(2)}, u32[]{:S(2)}) collective-permute-start(bf16[512,256]{1,0:T(8,128)(2,1)S(1)} %constant_dynamic-slice_fusion.6), channel_id=1, source_target_pairs={{0,2},{1,3},{2,0},{3,1},{4,6},{5,7},{6,4},{7,5},{8,10},{9,11},{10,... | collective-permute-start | bytes 786440 | tf_op jit(solution)/shard_map/deep_weight_mp/ppermute | solution.py:116
  50.6 2.4 %copy-start.7 = (bf16[1024,256]{1,0:T(8,128)(2,1)}, bf16[1024,256]{1,0:T(8,128)(2,1)S(1)}, u32[]{:S(2)}) copy-start(bf16[1024,256]{1,0:T(8,128)(2,1)S(1)} %collective-permute-done.2) | copy-start | bytes 1572868
  50.6 12.4 %collective-permute-start.5 = (bf16[512,256]{1,0:T(8,128)(2,1)S(1)}, bf16[512,256]{1,0:T(8,128)(2,1)}, u32[]{:S(2)}, u32[]{:S(2)}) collective-permute-start(bf16[512,256]{1,0:T(8,128)(2,1)S(1)} %constant_dynamic-slice_fusion.6), channel_id=1, source_target_pairs={{0,1},{1,2},{2,3},{3,0},{4,5},{5,6},{6,7},{7,4},{8,9},{9,10},{10,1... | collective-permute-start | bytes 786440 | tf_op jit(solution)/shard_map/deep_weight_mp/ppermute | solution.py:116
  51.4 1.7 copy-start.19
  53.4 0.9 copy-start.5
  55.1 12.7 %all-to-all-start.1 = ((bf16[4,272,256]{2,1,0:T(8,128)(2,1)}), bf16[4,272,256]{2,1,0:T(8,128)(2,1)S(1)}, u32[]{:S(2)}, u32[]{:S(2)}) async-start(bf16[4,272,256]{2,1,0:T(8,128)(2,1)} %pad_maximum_fusion.1), calls=%async_computation.1 | async-start | bytes 1114112 | tf_op jit(solution)/shard_map/crossed_mp/all_to_all | solution.py:249
  66.0 4.3 %collective-permute-start.6 = (bf16[512,1024]{1,0:T(8,128)(2,1)S(1)}, bf16[512,1024]{1,0:T(8,128)(2,1)}, u32[]{:S(2)}, u32[]{:S(2)}) collective-permute-start(bf16[512,1024]{1,0:T(8,128)(2,1)S(1)} %constant_dynamic-update-slice_fusion), channel_id=1, source_target_pairs={{0,4},{4,0},{1,5},{5,1},{2,6},{6,2},{3,7},{7,3},{8,12},{12,8},{9,1... | collective-permute-start | bytes 3145736 | tf_op jit(solution)/shard_map/deep_weight_core/ppermute | solution.py:107
  75.8 14.2 %collective-permute-start.7 = (f32[256]{0:T(256)S(1)}, f32[256]{0:T(256)S(1)}, u32[]{:S(2)}, u32[]{:S(2)}) collective-permute-start(f32[256]{0:T(256)S(1)} %get-tuple-element.29), channel_id=1, source_target_pairs={{0,3},{1,0},{2,1},{3,2},{4,7},{5,4},{6,5},{7,6},{8,11},{9,8},{10,9... | collective-permute-start | bytes 3080 | tf_op jit(solution)/shard_map/stats/ppermute | solution.py:116
  78.3 11.7 %collective-permute-start.8 = (f32[256]{0:T(256)S(1)}, f32[256]{0:T(256)S(1)}, u32[]{:S(2)}, u32[]{:S(2)}) collective-permute-start(f32[256]{0:T(256)S(1)} %get-tuple-element.29), channel_id=1, source_target_pairs={{0,2},{1,3},{2,0},{3,1},{4,6},{5,7},{6,4},{7,5},{8,10},{9,11},{10,... | collective-permute-start | bytes 3080 | tf_op jit(solution)/shard_map/stats/ppermute | solution.py:116
  79.9 10.1 %collective-permute-start.9 = (f32[256]{0:T(256)S(1)}, f32[256]{0:T(256)S(1)}, u32[]{:S(2)}, u32[]{:S(2)}) collective-permute-start(f32[256]{0:T(256)S(1)} %get-tuple-element.29), channel_id=1, source_target_pairs={{0,1},{1,2},{2,3},{3,0},{4,5},{5,6},{6,7},{7,4},{8,9},{9,10},{10,1... | collective-permute-start | bytes 3080 | tf_op jit(solution)/shard_map/stats/ppermute | solution.py:116
  79.9 17.1 %all-to-all-start.2 = ((bf16[4,264,256]{2,1,0:T(8,128)(2,1)}), bf16[4,264,256]{2,1,0:T(8,128)(2,1)}, u32[]{:S(2)}, u32[]{:S(2)}) async-start(bf16[4,264,256]{2,1,0:T(8,128)(2,1)} %pad_maximum_fusion.2), calls=%async_computation.2 | async-start | bytes 1081344 | tf_op jit(solution)/shard_map/crossed_grad/all_to_all | solution.py:299
  87.1 1.6 copy-start.2
  88.7 11.4 %collective-permute-start.11 = (bf16[4,32,16,256]{3,2,1,0:T(8,128)(2,1)}, bf16[4,32,16,256]{3,2,1,0:T(8,128)(2,1)}, u32[]{:S(2)}, u32[]{:S(2)}) collective-permute-start(bf16[4,32,16,256]{3,2,1,0:T(8,128)(2,1)} %fusion.18), channel_id=1, source_target_pairs={{0,4},{4,0},{1,5},{5,1},{2,6},{6,2},{3,7},{7,3},{8,12},{12,8},{9,1... | collective-permute-start | bytes 3145736 | tf_op jit(solution)/shard_map/deep_grad/ppermute | solution.py:107
  96.8 10.5 %collective-permute-start.10 = (bf16[32,80,256]{2,1,0:T(8,128)(2,1)S(1)}, bf16[32,80,256]{2,1,0:T(8,128)(2,1)}, u32[]{:S(2)}, u32[]{:S(2)}) collective-permute-start(bf16[32,80,256]{2,1,0:T(8,128)(2,1)S(1)} %get-tuple-element.31), channel_id=1, source_target_pairs={{0,4},{4,0},{1,5},{5,1},{2,6},{6,2},{3,7},{7,3},{8,12},{12,8},{9,1... | collective-permute-start | bytes 3932168 | tf_op jit(solution)/shard_map/stats_sum/ppermute | solution.py:107
  97.0 3.1 %copy-start.3 = (bf16[4,32,2,16,256]{4,3,2,1,0:T(8,128)(2,1)S(1)}, bf16[4,32,2,16,256]{4,3,2,1,0:T(8,128)(2,1)}, u32[]{:S(2)}) copy-start(bf16[4,32,2,16,256]{4,3,2,1,0:T(8,128)(2,1)} %copy-done.2) | copy-start | bytes 6291460
  102.8 20.1 %all-to-all-start.3 = ((bf16[4,32,16,256]{3,2,1,0:T(8,128)(2,1)}), bf16[4,32,16,256]{3,2,1,0:T(8,128)(2,1)}, u32[]{:S(2)}, u32[]{:S(2)}) async-start(bf16[4,32,16,256]{3,2,1,0:T(8,128)(2,1)} %fusion), calls=%async_computation.3 | async-start | bytes 2097152 | tf_op jit(solution)/shard_map/deep_grad/all_to_all | solution.py:340
  107.3 1.7 copy-start.4
  109.0 1.0 copy-start.6
  110.0 1.7 copy-start.8
  112.3 3.8 %collective-permute-start.12 = (bf16[32,16,256]{2,1,0:T(8,128)(2,1)S(1)}, bf16[32,16,256]{2,1,0:T(8,128)(2,1)S(1)}, u32[]{:S(2)}, u32[]{:S(2)}) collective-permute-start(bf16[32,16,256]{2,1,0:T(8,128)(2,1)S(1)} %fusion.40), channel_id=1, source_target_pairs={{0,4},{4,0},{1,5},{5,1},{2,6},{6,2},{3,7},{7,3},{8,12},{12,8},{9,1... | collective-permute-start | bytes 786440 | tf_op jit(solution)/shard_map/cross_grad/ppermute | solution.py:107
  113.1 3.0 %collective-permute-start.15 = (f32[3,256]{1,0:T(4,128)S(1)}, f32[3,256]{1,0:T(4,128)S(1)}, u32[]{:S(2)}, u32[]{:S(2)}) collective-permute-start(f32[3,256]{1,0:T(4,128)S(1)} %pad_maximum_fusion.7), channel_id=1, source_target_pairs={{0,4},{4,0},{1,5},{5,1},{2,6},{6,2},{3,7},{7,3},{8,12},{12,8},{9,1... | collective-permute-start | bytes 9224 | tf_op jit(solution)/shard_map/cross_grad/ppermute | solution.py:107
  113.3 9.6 %collective-permute-start.13 = (bf16[8,72,256]{2,1,0:T(8,128)(2,1)S(1)}, bf16[8,72,256]{2,1,0:T(8,128)(2,1)S(1)}, u32[]{:S(2)}, u32[]{:S(2)}) collective-permute-start(bf16[8,72,256]{2,1,0:T(8,128)(2,1)S(1)} %get-tuple-element.104), channel_id=1, source_target_pairs={{0,8},{8,16},{16,24},{24,0},{1,9},{9,17},{17,25},{25,1},{2,10},{10... | collective-permute-start | bytes 884744 | tf_op jit(solution)/shard_map/stats_sum/ppermute | solution.py:116
  114.6 8.3 %collective-permute-start.14 = (bf16[8,72,256]{2,1,0:T(8,128)(2,1)S(1)}, bf16[8,72,256]{2,1,0:T(8,128)(2,1)}, u32[]{:S(2)}, u32[]{:S(2)}) collective-permute-start(bf16[8,72,256]{2,1,0:T(8,128)(2,1)S(1)} %get-tuple-element.103), channel_id=1, source_target_pairs={{0,24},{8,0},{16,8},{24,16},{1,25},{9,1},{17,9},{25,17},{2,26},{10... | collective-permute-start | bytes 884744 | tf_op jit(solution)/shard_map/stats_sum/ppermute | solution.py:116
  125.3 5.6 %collective-permute-start.16 = (bf16[8,40,256]{2,1,0:T(8,128)(2,1)}, bf16[8,40,256]{2,1,0:T(8,128)(2,1)S(1)}, u32[]{:S(2)}, u32[]{:S(2)}) collective-permute-start(bf16[8,40,256]{2,1,0:T(8,128)(2,1)} %get-tuple-element.107), channel_id=1, source_target_pairs={{0,8},{8,16},{16,24},{24,0},{1,9},{9,17},{17,25},{25,1},{2,10},{10... | collective-permute-start | bytes 491528 | tf_op jit(solution)/shard_map/grads_x/ppermute | solution.py:116
  126.2 8.8 %collective-permute-start.17 = (bf16[8,40,256]{2,1,0:T(8,128)(2,1)S(1)}, bf16[8,40,256]{2,1,0:T(8,128)(2,1)S(1)}, u32[]{:S(2)}, u32[]{:S(2)}) collective-permute-start(bf16[8,40,256]{2,1,0:T(8,128)(2,1)S(1)} %get-tuple-element.109), channel_id=1, source_target_pairs={{0,16},{8,24},{16,0},{24,8},{1,17},{9,25},{17,1},{25,9},{2,18},{10... | collective-permute-start | bytes 491528 | tf_op jit(solution)/shard_map/grads_x/ppermute | solution.py:116
  128.9 6.1 %collective-permute-start.18 = (bf16[8,40,256]{2,1,0:T(8,128)(2,1)S(1)}, bf16[8,40,256]{2,1,0:T(8,128)(2,1)}, u32[]{:S(2)}, u32[]{:S(2)}) collective-permute-start(bf16[8,40,256]{2,1,0:T(8,128)(2,1)S(1)} %get-tuple-element.108), channel_id=1, source_target_pairs={{0,24},{8,0},{16,8},{24,16},{1,25},{9,1},{17,9},{25,17},{2,26},{10... | collective-permute-start | bytes 491528 | tf_op jit(solution)/shard_map/grads_x/ppermute | solution.py:116
  129.5 12.1 %collective-permute-start.19 = (bf16[8,72,256]{2,1,0:T(8,128)(2,1)S(1)}, bf16[8,72,256]{2,1,0:T(8,128)(2,1)S(1)}, u32[]{:S(2)}, u32[]{:S(2)}) collective-permute-start(bf16[8,72,256]{2,1,0:T(8,128)(2,1)S(1)} %get-tuple-element.35), channel_id=1, source_target_pairs={{0,16},{8,24},{16,0},{24,8},{1,17},{9,25},{17,1},{25,9},{2,18},{10... | collective-permute-start | bytes 884744 | tf_op jit(solution)/shard_map/stats_sum/ppermute | solution.py:116
  143.5 19.4 %all-to-all-start.4 = ((bf16[8,112,256]{2,1,0:T(8,128)(2,1)}), bf16[8,112,256]{2,1,0:T(8,128)(2,1)S(1)}, u32[]{:S(2)}, u32[]{:S(2)}) async-start(bf16[8,112,256]{2,1,0:T(8,128)(2,1)} %pad_maximum_fusion.4), calls=%async_computation.4 | async-start | bytes 917504 | tf_op jit(solution)/shard_map/sums_z/all_to_all | solution.py:387
  183.7 9.7 %all-to-all-start.6 = ((f32[8,1,128]{2,1,0:T(1,128)}), f32[8,1,128]{2,1,0:T(1,128)S(1)}, u32[]{:S(2)}, u32[]{:S(2)}) async-start(f32[8,1,128]{2,1,0:T(1,128)} %broadcast_in_dim.37), calls=%async_computation.6 | async-start | bytes 8192 | tf_op jit(solution)/shard_map/norm/all_to_all | solution.py:400
